TPU v7x, 32 devices: a whole 2x2x4 slice. The times are simulated.
32 devices in a mesh: grp: 4 (over y, x), tile: 8 (over z, core).
Axes of the slice: x: 2, y: 2, z: 4, core: 2. Of those that a mesh axis runs over, the one named last changes fastest.
Arguments:
- jac_point: float32 [6, 32768], P(None, ('grp', 'tile')), may hold values from -6 to 6
- jac_cam: float32 [18, 32768], P(None, ('grp', 'tile')), may hold values from -3 to 3
- resid: float32 [2, 32768], P(None, ('grp', 'tile')), may hold values from -6 to 6
- point_index: int32 [32768], P(('grp', 'tile')), may hold values from 0 to 4095, as said below
- cam_index: int32 [32768], P(('grp', 'tile')), may hold values from 0 to 3071, as said below
Outputs:
- point_step: float32 [3, 131072], P(None, ('grp', 'tile'))
- camera_step: float32 [9, 12288], P(None, ('grp', 'tile'))
- point_resid: float32 [3, 131072], P(None, ('grp', 'tile'))
- camera_resid: float32 [9, 12288], P(None, ('grp', 'tile'))
Inputs may be any that keep to these rules, and one draw needn't show every extreme that they name: `point_index`: index among the points of the observation's own device; every device names point 0 and point 4096 - 1. `cam_index`: block h of a device's observations (slots h * 256 to (h + 1) * 256 - 1) names cameras of group h by their index within the group; every block names camera 0 and camera 3072 - 1.
All inputs are finite; a program needn't handle non-finite values.
Results may differ from a plain program's by a relative error of at most 0.0002.
Values sent between devices are 32-bit elements; how exact they have to be, the bound alone decides.
No kernel may reach another device: no remote copies, remote signals or barrier semaphores. Data moves between devices by JAX's collectives and lax.ppermute only.
A program may use at most 64 MiB of HBM per device.

v0:
```python
import jax
import jax.numpy as jnp
from jax import lax
from jax.sharding import PartitionSpec as P

P_DEV = 4096
CAM_DEV = 384
ITERS = 2


damping = 1.0


def segment_rows(data, ids, count):
    return jax.vmap(lambda row: jax.ops.segment_sum(row, ids, num_segments=count))(data)


def shards(jac_point, jac_cam, resid, point_index, cam_index):
    obs_dev = jac_point.shape[1]
    cam_grp = CAM_DEV * lax.axis_size("tile")
    jp = jac_point.reshape(2, 3, obs_dev)
    jc = jac_cam.reshape(2, 9, obs_dev)
    owned_index = lax.all_to_all(cam_index, "grp", split_axis=0, concat_axis=0, tiled=True)
    point_rhs = segment_rows(-jnp.sum(jp * resid[:, None], axis=0), point_index, P_DEV)
    point_diag = segment_rows(jnp.sum(jp * jp, axis=0), point_index, P_DEV)
    grad_terms, square_terms = (
        lax.all_to_all(
            -jnp.sum(jc * resid[:, None], axis=0), "grp", split_axis=1, concat_axis=1, tiled=True
        ),
        lax.all_to_all(jnp.sum(jc * jc, axis=0), "grp", split_axis=1, concat_axis=1, tiled=True),
    )
    group_terms = segment_rows(
        jnp.concatenate([grad_terms, square_terms], axis=0), owned_index, cam_grp
    )
    camera_both = lax.psum_scatter(group_terms, "tile", scatter_dimension=1, tiled=True)
    camera_rhs, camera_diag = (camera_both[:9], camera_both[9:])

    def apply(vp, vc):
        group_cams = lax.all_gather(vc, "tile", axis=1, tiled=True)
        fetched = group_cams[:, owned_index]
        point_term = jnp.sum(jp * vp[:, point_index][None], axis=1)
        at_obs = lax.all_to_all(fetched, "grp", split_axis=1, concat_axis=1, tiled=True)
        error = point_term + jnp.sum(jc * at_obs[None], axis=1)
        column = lax.all_to_all(
            jnp.sum(jc * error[:, None], axis=0), "grp", split_axis=1, concat_axis=1, tiled=True
        )
        camera_out = lax.psum_scatter(
            segment_rows(column, owned_index, cam_grp), "tile", scatter_dimension=1, tiled=True
        )
        point_out = segment_rows(jnp.sum(jp * error[:, None], axis=0), point_index, P_DEV)
        return (point_out + damping * vp, camera_out + damping * vc)

    def inner(ap, ac, bp, bc):
        return jnp.sum(ap * bp) + jnp.sum(ac * bc)

    def paired_sums(rp, rc, zp, zc, sp, sc):
        return lax.psum((inner(rp, rc, zp, zc), inner(zp, zc, sp, sc)), ("grp", "tile"))

    point_pre = point_diag + damping
    camera_pre = camera_diag + damping
    point_x = jnp.zeros_like(point_rhs)
    camera_x = jnp.zeros_like(camera_rhs)
    point_r, camera_r = (point_rhs, camera_rhs)
    point_z, camera_z = (point_r / point_pre, camera_r / camera_pre)
    point_s, camera_s = apply(point_z, camera_z)
    gamma, delta = paired_sums(point_r, camera_r, point_z, camera_z, point_s, camera_s)
    alpha = gamma / delta
    point_dir, camera_dir, point_q, camera_q = (point_z, camera_z, point_s, camera_s)
    for step_number in range(ITERS):
        point_x = point_x + alpha * point_dir
        camera_x = camera_x + alpha * camera_dir
        point_r = point_r - alpha * point_q
        camera_r = camera_r - alpha * camera_q
        if step_number + 1 < ITERS:
            point_z, camera_z = (point_r / point_pre, camera_r / camera_pre)
            point_s, camera_s = apply(point_z, camera_z)
            gamma_next, delta = paired_sums(point_r, camera_r, point_z, camera_z, point_s, camera_s)
            ratio = gamma_next / gamma
            alpha = gamma_next / (delta - ratio * gamma_next / alpha)
            point_dir = point_z + ratio * point_dir
            camera_dir = camera_z + ratio * camera_dir
            point_q = point_s + ratio * point_q
            camera_q = camera_s + ratio * camera_q
            gamma = gamma_next
    return (point_x, camera_x, point_r, camera_r)


def solution(mesh):
    placed = (
        P(None, ("grp", "tile")),
        P(None, ("grp", "tile")),
        P(None, ("grp", "tile")),
        P(("grp", "tile")),
        P(("grp", "tile")),
    )
    return jax.shard_map(
        shards,
        mesh=mesh,
        in_specs=placed,
        out_specs=(
            P(None, ("grp", "tile")),
            P(None, ("grp", "tile")),
            P(None, ("grp", "tile")),
            P(None, ("grp", "tile")),
        ),
        check_vma=False,
    )
```

profile of v0, /device:TPU:0, one launch (start us, length us, event | category | flops | bytes accessed | tf_op | source)
XLA Modules:
  0.0 375.7 jit_solution(13372487517066194993)
XLA Ops:
  9.5 5.2 %all-to-all-start.1 = ((f32[9,4,256]{2,0,1:T(8,128)}), f32[9,4,256]{2,0,1:T(8,128)S(1)}, u32[]{:S(2)}, u32[]{:S(2)}) async-start(f32[9,4,256]{2,0,1:T(8,128)} %copy.72), calls=%async_computation.1 | async-start | bytes 131072 | tf_op jit(solution)/shard_map/all_to_all | solution.py:27
  24.0 6.5 %scatter_custom_fusion = f32[3,4096]{0,1:T(8,128)S(1)} fusion(s32[1024]{0:T(1024)S(1)} %copy-done.3, f32[1024,3]{1,0:T(8,128)S(1)} %copy.69, f32[]{:T(128)} %constant.5.clone.1), kind=kCustom, calls=%fused_computation.20 | custom fusion | flops 3072 | bytes 49156 | tf_op jit(solution)/shard_map/vmap()/scatter-add | solution.py:15
  30.5 7.4 %scatter_custom_fusion.1 = f32[3,4096]{0,1:T(8,128)} fusion(s32[1024]{0:T(1024)S(1)} %copy-done.3, f32[1024,3]{1,0:T(8,128)S(1)} %copy.70, f32[]{:T(128)} %constant.6.clone.1), kind=kCustom, calls=%fused_computation.18 | custom fusion | flops 3072 | bytes 49156 | tf_op jit(solution)/shard_map/vmap()/scatter-add | solution.py:15
  41.1 4.4 %gather_fusion = f32[1024,3]{1,0:T(8,128)S(1)} fusion(f32[3,4096]{0,1:T(8,128)} %div.24, s32[1024]{0:T(1024)S(1)} %fusion.13), kind=kCustom, calls=%fused_computation | custom fusion | bytes 28672 | tf_op jit(solution)/shard_map/gather | solution.py:41
  45.8 4.2 %all-to-all-start = ((s32[4,256,1]{1,2,0:T(1,128)}), s32[4,256,1]{1,2,0:T(1,128)S(1)}, u32[]{:S(2)}, u32[]{:S(2)}) async-start(s32[4,256,1]{1,2,0:T(1,128)} %bitcast.2), calls=%async_computation | async-start | bytes 8192 | tf_op jit(solution)/shard_map/all_to_all | solution.py:23
  50.3 4.4 %all-to-all-done = s32[4,256,1]{1,2,0:T(1,128)S(1)} async-done(((s32[4,256,1]{1,2,0:T(1,128)}), s32[4,256,1]{1,2,0:T(1,128)S(1)}, u32[]{:S(2)}, u32[]{:S(2)}) %all-to-all-start) | async-done | bytes 4128 | tf_op jit(solution)/shard_map/all_to_all | solution.py:23
  54.7 7.2 %scatter_custom_fusion.2 = f32[18,3072]{0,1:T(8,128)} fusion(s32[1024]{0:T(1024)S(1)} %bitcast.60, f32[1024,18]{1,0:T(8,128)S(1)} %copy.76, f32[]{:T(128)} %constant.5.clone.1), kind=kCustom, calls=%fused_computation.26 | custom fusion | flops 18432 | bytes 221188 | tf_op jit(solution)/shard_map/vmap()/scatter-add | solution.py:15
  64.6 30.0 %reduce-scatter.4.cloned.1.call-done = f32[18,384]{1,0:T(8,128)} async-done(((f32[18,3072]{1,0:T(8,128)}), f32[18,384]{1,0:T(8,128)}) %reduce-scatter.4.cloned.1.call-update) | async-done | bytes 27664 | tf_op jit(solution)/shard_map/reduce_scatter | solution.py:35
  95.4 14.1 %all_gather.6 = f32[9,3072]{1,0:T(8,128)S(1)} all-gather(f32[9,384]{1,0:T(8,128)S(1)} %fusion.12), channel_id=1, replica_groups=mesh['grp'=4,'tile'=8] {'tile'}, dimensions={1}, use_global_device_ids=true | all-gather | bytes 124416 | tf_op jit(solution)/shard_map/all_gather | solution.py:39
  111.2 4.2 %gather_fusion.1 = f32[1024,9]{1,0:T(8,128)S(1)} fusion(f32[9,3072]{0,1:T(8,128)} %copy.79, s32[1024]{0:T(1024)S(1)} %broadcast_clamp_fusion), kind=kCustom, calls=%fused_computation.1 | custom fusion | bytes 77824 | tf_op jit(solution)/shard_map/gather | solution.py:40
  129.3 8.3 %scatter_fusion = f32[3,4096]{0,1:T(8,128)} fusion(f32[3,4096]{0,1:T(8,128)} %copy.104, s32[1024]{0:T(1024)S(1)} %copy-done.3, f32[1024,3]{1,0:T(8,128)S(1)} %copy.82), kind=kCustom, calls=%fused_computation.7 | custom fusion | flops 3072 | bytes 40960 | tf_op jit(solution)/shard_map/vmap()/scatter-add | solution.py:15
  137.9 7.2 %scatter_custom_fusion.4 = f32[9,3072]{0,1:T(8,128)} fusion(s32[1024]{0:T(1024)S(1)} %bitcast.62, f32[1024,9]{1,0:T(8,128)S(1)} %copy.85, f32[]{:T(128)} %constant.5.clone.1), kind=kCustom, calls=%fused_computation.24 | custom fusion | flops 9216 | bytes 110596 | tf_op jit(solution)/shard_map/vmap()/scatter-add | solution.py:15
  151.1 25.5 %reduce-scatter.6.cloned.1.call-done = f32[9,384]{1,0:T(8,128)} async-done(((f32[9,3072]{1,0:T(8,128)}), f32[9,384]{1,0:T(8,128)}) %reduce-scatter.6.cloned.1.call-update) | async-done | bytes 13840 | tf_op jit(solution)/shard_map/reduce_scatter | solution.py:47
  180.6 37.8 %all-reduce.1 = (f32[]{:T(128)}, f32[]{:T(128)}) all-reduce(f32[]{:T(128)S(6)} %add.109, f32[]{:T(128)S(6)} %add.114), channel_id=1, replica_groups=mesh['grp'=4,'tile'=8] {'grp','tile'}, use_global_device_ids=true, to_apply=%region_10.0 | all-reduce | flops 2 | bytes 16 | tf_op jit(solution)/shard_map/psum | solution.py:57
  219.7 3.8 %fusion.10 = f32[3,4096]{0,1:T(8,128)} fusion(f32[3,4096]{0,1:T(8,128)} %scatter_custom_fusion.1, f32[3,4096]{0,1:T(8,128)S(1)} %scatter_custom_fusion, f32[3,4096]{0,1:T(8,128)} %scatter_fusion, f32[]{:T(128)S(6)} %div.26), kind=kLoop, calls=%fused_computation.28 | loop fusion | flops 36864 | bytes 196612 | tf_op jit(solution)/shard_map/div | solution.py:75
  223.5 14.7 %all_gather.7 = f32[9,3072]{1,0:T(8,128)S(1)} all-gather(f32[9,384]{1,0:T(8,128)S(1)} %fusion.11), channel_id=1, replica_groups=mesh['grp'=4,'tile'=8] {'tile'}, dimensions={1}, use_global_device_ids=true | all-gather | bytes 124416 | tf_op jit(solution)/shard_map/all_gather | solution.py:39
  238.2 4.4 %gather_fusion.2 = f32[1024,3]{1,0:T(8,128)S(1)} fusion(f32[3,4096]{0,1:T(8,128)} %fusion.10, s32[1024]{0:T(1024)S(1)} %fusion.13), kind=kCustom, calls=%fused_computation.2 | custom fusion | bytes 28672 | tf_op jit(solution)/shard_map/gather | solution.py:41
  244.5 4.2 %gather_fusion.3 = f32[1024,9]{1,0:T(8,128)S(1)} fusion(f32[9,3072]{0,1:T(8,128)} %copy.88, s32[1024]{0:T(1024)S(1)} %broadcast_clamp_fusion), kind=kCustom, calls=%fused_computation.3 | custom fusion | bytes 77824 | tf_op jit(solution)/shard_map/gather | solution.py:40
  262.5 8.4 %scatter_fusion.1 = f32[3,4096]{0,1:T(8,128)} fusion(f32[3,4096]{0,1:T(8,128)} %copy.105, s32[1024]{0:T(1024)S(1)} %copy-done.3, f32[1024,3]{1,0:T(8,128)S(1)} %copy.91), kind=kCustom, calls=%fused_computation.9 | custom fusion | flops 3072 | bytes 40960 | tf_op jit(solution)/shard_map/vmap()/scatter-add | solution.py:15
  271.2 7.3 %scatter_custom_fusion.6 = f32[9,3072]{0,1:T(8,128)} fusion(s32[1024]{0:T(1024)S(1)} %bitcast.63, f32[1024,9]{1,0:T(8,128)S(1)} %copy.94, f32[]{:T(128)} %constant.5.clone.1), kind=kCustom, calls=%fused_computation.22 | custom fusion | flops 9216 | bytes 110596 | tf_op jit(solution)/shard_map/vmap()/scatter-add | solution.py:15
  281.0 4.0 %multiply_reduce_fusion = (f32[]{:T(128)}, f32[]{:T(128)}) fusion(f32[3,4096]{0,1:T(8,128)} %fusion.10, f32[3,4096]{0,1:T(8,128)} %scatter_fusion.1, f32[3,4096]{0,1:T(8,128)S(1)} %scatter_custom_fusion, f32[3,4096]{0,1:T(8,128)} %scatter_fusion, f32[]{:T(128)S(6)} %div.26), kind=kLoop, calls=%fused_computation.13 | loop fusion | flops 73726 | bytes 196620 | tf_op jit(solution)/shard_map/reduce_sum | solution.py:54
  285.1 26.7 %reduce-scatter.8.cloned.1.call-done = f32[9,384]{1,0:T(8,128)} async-done(((f32[9,3072]{1,0:T(8,128)}), f32[9,384]{1,0:T(8,128)}) %reduce-scatter.8.cloned.1.call-update) | async-done | bytes 13840 | tf_op jit(solution)/shard_map/reduce_scatter | solution.py:47
  315.6 37.8 %all-reduce = (f32[]{:T(128)}, f32[]{:T(128)}) all-reduce(f32[]{:T(128)S(6)} %add.115, f32[]{:T(128)S(6)} %add.118), channel_id=1, replica_groups=mesh['grp'=4,'tile'=8] {'grp','tile'}, use_global_device_ids=true, to_apply=%region_23.0 | all-reduce | flops 2 | bytes 16 | tf_op jit(solution)/shard_map/psum | solution.py:57
  358.1 6.2 %multiply_subtract_fusion = (f32[3,4096]{0,1:T(8,128)}, f32[3,4096]{0,1:T(8,128)}) fusion(f32[3,4096]{0,1:T(8,128)} %scatter_fusion.1, f32[3,4096]{0,1:T(8,128)} %scatter_fusion, f32[]{:T(128)S(6)} %div.29, f32[]{:T(128)S(6)} %div.31, f32[3,4096]{0,1:T(8,128)S(1)} %scatter_custom_fusion, f32[]{:T(128)S(6)} %div.26, f32[3,4096]{0,1:T(8,128)} %fusion.10, ...), kind=kLoop, calls=%fused_computation.11 | loop fusion | flops 135168 | bytes 344076 | tf_op jit(solution)/shard_map/sub | solution.py:72
  (98 shorter events, 66.5 us)
Async XLA Ops:
  7.2 16.8 %copy-start.3 = (s32[1024]{0:T(1024)S(1)}, s32[1024]{0:T(1024)}, u32[]{:S(2)}) copy-start(s32[1024]{0:T(1024)} %param.8) | copy-start | bytes 12292
  9.5 10.0 %all-to-all-start.1 = ((f32[9,4,256]{2,0,1:T(8,128)}), f32[9,4,256]{2,0,1:T(8,128)S(1)}, u32[]{:S(2)}, u32[]{:S(2)}) async-start(f32[9,4,256]{2,0,1:T(8,128)} %copy.72), calls=%async_computation.1 | async-start | bytes 131072 | tf_op jit(solution)/shard_map/all_to_all | solution.py:27
  19.5 26.3 %all-to-all-start.2 = ((f32[9,4,256]{2,0,1:T(8,128)}), f32[9,4,256]{2,0,1:T(8,128)S(1)}, u32[]{:S(2)}, u32[]{:S(2)}) async-start(f32[9,4,256]{2,0,1:T(8,128)} %copy.74), calls=%async_computation.2 | async-start | bytes 131072 | tf_op jit(solution)/shard_map/all_to_all | solution.py:30
  45.8 8.8 %all-to-all-start = ((s32[4,256,1]{1,2,0:T(1,128)}), s32[4,256,1]{1,2,0:T(1,128)S(1)}, u32[]{:S(2)}, u32[]{:S(2)}) async-start(s32[4,256,1]{1,2,0:T(1,128)} %bitcast.2), calls=%async_computation | async-start | bytes 8192 | tf_op jit(solution)/shard_map/all_to_all | solution.py:23
  50.0 44.6 %reduce-scatter.4.cloned.1.call-start = ((), (), s32[]{:S(2)}) async-start(), calls=%async_computation.10 | async-start | bytes 331776 | tf_op jit(solution)/shard_map/reduce_scatter | solution.py:35
  116.3 8.4 %all-to-all-start.3 = ((f32[9,4,256]{2,0,1:T(8,128)}), f32[9,4,256]{2,0,1:T(8,128)S(1)}, u32[]{:S(2)}, u32[]{:S(2)}) async-start(f32[9,4,256]{2,0,1:T(8,128)} %copy.80), calls=%async_computation.4 | async-start | bytes 131072 | tf_op jit(solution)/shard_map/all_to_all | solution.py:42
  125.5 12.1 %all-to-all-start.4 = ((f32[9,4,256]{2,0,1:T(8,128)}), f32[9,4,256]{2,0,1:T(8,128)S(1)}, u32[]{:S(2)}, u32[]{:S(2)}) async-start(f32[9,4,256]{2,0,1:T(8,128)} %copy.83), calls=%async_computation.5 | async-start | bytes 131072 | tf_op jit(solution)/shard_map/all_to_all | solution.py:44
  128.8 47.8 %reduce-scatter.6.cloned.1.call-start = ((), (), s32[]{:S(2)}) async-start(), calls=%async_computation.11 | async-start | bytes 221184 | tf_op jit(solution)/shard_map/reduce_scatter | solution.py:47
  147.7 28.9 %copy-start.1 = (f32[18,384]{1,0:T(8,128)S(1)}, f32[18,384]{1,0:T(8,128)}, u32[]{:S(2)}) copy-start(f32[18,384]{1,0:T(8,128)} %reduce-scatter.4.cloned.1.call-done) | copy-start | bytes 82948
  249.5 8.6 %all-to-all-start.5 = ((f32[9,4,256]{2,0,1:T(8,128)}), f32[9,4,256]{2,0,1:T(8,128)S(1)}, u32[]{:S(2)}, u32[]{:S(2)}) async-start(f32[9,4,256]{2,0,1:T(8,128)} %copy.89), calls=%async_computation.7 | async-start | bytes 131072 | tf_op jit(solution)/shard_map/all_to_all | solution.py:42
  258.9 12.0 %all-to-all-start.6 = ((f32[9,4,256]{2,0,1:T(8,128)}), f32[9,4,256]{2,0,1:T(8,128)S(1)}, u32[]{:S(2)}, u32[]{:S(2)}) async-start(f32[9,4,256]{2,0,1:T(8,128)} %copy.92), calls=%async_computation.8 | async-start | bytes 131072 | tf_op jit(solution)/shard_map/all_to_all | solution.py:44
  262.2 49.6 %reduce-scatter.8.cloned.1.call-start = ((), (), s32[]{:S(2)}) async-start(), calls=%async_computation.12 | async-start | bytes 221184 | tf_op jit(solution)/shard_map/reduce_scatter | solution.py:47
  364.3 3.0 copy-start
  364.3 4.2 %copy-start.2 = (f32[9,384]{1,0:T(8,128)S(1)}, f32[9,384]{1,0:T(8,128)}, u32[]{:S(2)}) copy-start(f32[9,384]{1,0:T(8,128)} %reduce-scatter.8.cloned.1.call-done) | copy-start | bytes 41476
Sparse Core Ops, SparseCore 0:
  64.7 29.8 reduce-scatter.3
  147.8 28.7 reduce-scatter.5
  281.2 30.5 reduce-scatter.7
where the time goes:
time: 378 us; the launch traced here: 376 us
  blocking collectives  104 us (28%)
  waiting for transfers between devices  92.8 us (25%)
  other arithmetic  79.6 us (21%)
  local copies, waits for them, and re-layouts  46.8 us (12%)
  starting transfers between devices  26.7 us (7%)
  between operations  25.2 us (7%)
    psum x2, blocking collectives, paired_sums(): lax.psum((inner(rp, rc, zp, zc), inner(zp, zc, sp, sc)), ('grp', 'tile'))  75.6 us
    scatter-add x7, other arithmetic, segment_rows(): jax.ops.segment_sum(row, ids, num_segments=count)  52.4 us
    reduce_scatter x2, waiting for transfers between devices, apply(): lax.psum_scatter(segment_rows(column, owned_index, cam_grp), 'tile', scat...  52.2 us
    reduce_scatter x1, waiting for transfers between devices, shards(): lax.psum_scatter(group_terms, 'tile', scatter_dimension=1, tiled=True)  30 us
    all_gather x2, blocking collectives, apply(): group_cams = lax.all_gather(vc, 'tile', axis=1, tiled=True)  28.8 us
    unnamed x24, local copies, waits for them, and re-layouts  10.5 us
    reduce_sum x4, other arithmetic, inner(): return jnp.sum(ap * bp) + jnp.sum(ac * bc)  10.1 us
    gather x4, local copies, waits for them, and re-layouts, apply(): point_term = jnp.sum(jp * vp[:, point_index][None], axis=1)  9.16 us
  transfers between devices with their start and end apart: 10, of which 7 were waited for; matrix products, arithmetic and copies ran while one was open for 15% of the time, Pallas kernels for 0%

commit v1 on v0

v1 whole, which is shorter than its diff:
```python
import functools

import jax
import jax.numpy as jnp
from jax import lax
from jax.experimental import pallas as pl
from jax.experimental.pallas import tpu as pltpu
from jax.sharding import PartitionSpec as P

P_DEV = 4096
CAM_DEV = 384
LO_BITS = 8
LO = 1 << LO_BITS
PH = P_DEV // LO
DAMPING = 1.0
F32 = jnp.float32
BF16 = jnp.bfloat16
PARAMS = pltpu.CompilerParams(vmem_limit_bytes=48 * 1024 * 1024)


def halves(v):
    high = v.astype(BF16).astype(F32)
    return high, v - high


def one_hot_rows(index, rows):
    numbers = lax.broadcasted_iota(jnp.int32, (rows, index.shape[1]), 0)
    return jnp.where(numbers == index, 1.0, 0.0).astype(BF16)


def dot_nt(a, b):
    return lax.dot_general(a, b, (((1,), (1,)), ((), ())), preferred_element_type=F32)


def dot_nn(a, b):
    return lax.dot_general(a, b, (((1,), (0,)), ((), ())), preferred_element_type=F32)


def is_row(hi, rows):
    return lax.broadcasted_iota(jnp.int32, (rows, hi.shape[1]), 0) == hi


def spread_row(mask, row):
    return jnp.where(mask, jnp.broadcast_to(row, mask.shape), 0.0)


def scatter_mixed(hi, hot, mains, tails, count, tail_rows):
    total = None
    tail_mask = is_row(hi, tail_rows)
    hi8 = jnp.broadcast_to(hi, (8, hi.shape[1]))
    main_parts = [halves(v) for v in mains]
    tail_parts = [halves(v) for v in tails]
    for part in range(2):
        pieces = []
        for k in range(count):
            here = hi8 == k
            pieces += [jnp.where(here, v[part], 0.0) for v in main_parts]
        pieces += [spread_row(tail_mask, v[part]) for v in tail_parts]
        lhs = jnp.concatenate(pieces, axis=0).astype(BF16)
        product = dot_nt(lhs, hot)
        total = product if total is None else total + product
    return total


def gather_mixed(hi, hot, table_high, table_low, count, tail_rows):
    found = dot_nn(table_high, hot) + dot_nn(table_low, hot)
    hi8 = jnp.broadcast_to(hi, (8, hi.shape[1]))
    main = jnp.zeros(hi8.shape, F32)
    for k in range(count):
        main = main + jnp.where(hi8 == k, found[k * 8 : k * 8 + 8], 0.0)
    tail = jnp.sum(
        jnp.where(is_row(hi, tail_rows), found[count * 8 :], 0.0), axis=0, keepdims=True
    )
    return main, tail


def scatter_points(mask, hot, rows):
    parts = [halves(v) for v in rows]
    total = None
    for part in range(2):
        lhs = jnp.concatenate([spread_row(mask, v[part]) for v in parts], axis=0)
        product = dot_nt(lhs.astype(BF16), hot)
        total = product if total is None else total + product
    return total


def gather_points(mask, hot, table):
    high, low = halves(table)
    found = dot_nn(high.astype(BF16), hot) + dot_nn(low.astype(BF16), hot)
    return [
        jnp.sum(jnp.where(mask, found[i * PH : (i + 1) * PH], 0.0), axis=0, keepdims=True)
        for i in range(found.shape[0] // PH)
    ]


def total_of(v):
    return jnp.sum(jnp.sum(v, axis=0, keepdims=True), axis=1, keepdims=True)


def lanes(v, width):
    return jnp.broadcast_to(v, (v.shape[0], width))


def pack_kernel(n_grp, n_z, jp_ref, jc_ref, res_ref, pidx_ref, cidx_ref, out_ref, pb_ref, pd_ref):
    slot = out_ref.shape[2]
    index = pidx_ref[...]
    mask = is_row(index >> LO_BITS, PH)
    hot = one_hot_rows(index & (LO - 1), LO)
    jp = [jp_ref[k : k + 1, :] for k in range(6)]
    res = [res_ref[a : a + 1, :] for a in range(2)]
    grad = [-(jp[i] * res[0] + jp[3 + i] * res[1]) for i in range(3)]
    square = [jp[i] * jp[i] + jp[3 + i] * jp[3 + i] for i in range(3)]
    table = scatter_points(mask, hot, grad + square)
    rhs = table[: 3 * PH]
    diag = table[3 * PH :] + DAMPING
    pb_ref[...] = rhs
    pd_ref[...] = diag
    z = rhs / diag
    at = gather_points(mask, hot, z)
    u = [sum(jp[3 * a + i] * at[i] for i in range(3)) for a in range(2)]
    gamma = total_of(rhs * z)
    norm = total_of(z * z)
    scalars = jnp.concatenate([lanes(gamma, slot // 2), lanes(norm, slot // 2)], axis=1)
    cams = cidx_ref[...].astype(F32)
    for h in range(n_grp):
        cols = slice(h * slot, (h + 1) * slot)
        block = jnp.concatenate(
            [
                jc_ref[0:8, cols],
                jc_ref[9:17, cols],
                jc_ref[8:9, cols],
                jc_ref[17:18, cols],
                res[0][:, cols],
                res[1][:, cols],
                u[0][:, cols],
                u[1][:, cols],
                cams[:, cols],
                scalars,
            ],
            axis=0,
        )

        @pl.loop(0, n_z)
        def _(z_to, block=block, h=h):
            out_ref[h * n_z + z_to] = block


def read_chunk(ref, chunk, count):
    x = jnp.concatenate([ref[chunk * count + k] for k in range(count)], axis=1)
    index = x[22:23].astype(jnp.int32)
    return x, index


def camera_kernel(n_grp, n_z, a_ref, b_ref, back_ref, cb_ref, cd_ref, cs_ref, acc_ref, w_ref, zh_ref, zl_ref, tb_ref, td_ref, ts_ref):
    blocks, _, slot = a_ref.shape
    per = min(4, blocks)
    chunks = blocks // per
    count = CAM_DEV * 2 * n_z // LO
    tail_rows = tb_ref.shape[0] - 8 * count
    acc_ref[...] = jnp.zeros(acc_ref.shape, F32)

    def first(ref):
        def body(chunk, scalars):
            x, index = read_chunk(ref, chunk, per)
            hi, hot = index >> LO_BITS, one_hot_rows(index & (LO - 1), LO)
            j0, j1 = x[0:8], x[8:16]
            j08, j18, r0, r1 = x[16:17], x[17:18], x[18:19], x[19:20]
            acc_ref[...] += scatter_mixed(
                hi,
                hot,
                [-(j0 * r0 + j1 * r1), j0 * j0 + j1 * j1],
                [-(j08 * r0 + j18 * r1), j08 * j08 + j18 * j18],
                count,
                tail_rows,
            )
            for k in range(per):
                scalars = scalars + x[23:24, k * slot : (k + 1) * slot]
            return scalars

        return body

    scalars = lax.fori_loop(0, chunks, first(a_ref), jnp.zeros((1, slot), F32))
    scalars = lax.fori_loop(0, chunks, first(b_ref), scalars)
    main = 8 * count
    for k in range(count):
        tb_ref[8 * k : 8 * k + 8, :] = acc_ref[16 * k : 16 * k + 8, :]
        td_ref[8 * k : 8 * k + 8, :] = acc_ref[16 * k + 8 : 16 * k + 16, :] + DAMPING
    tb_ref[main:, :] = acc_ref[2 * main : 2 * main + tail_rows, :]
    td_ref[main:, :] = acc_ref[2 * main + tail_rows :, :] + DAMPING
    z = tb_ref[...] / td_ref[...]
    gamma = total_of(tb_ref[...] * z)
    norm = total_of(z * z)
    high, low = halves(z)
    zh_ref[...] = high.astype(BF16)
    zl_ref[...] = low.astype(BF16)
    ts_ref[...] = z

    def second(ref, offset):
        def body(chunk, energy):
            x, index = read_chunk(ref, chunk, per)
            hi, hot = index >> LO_BITS, one_hot_rows(index & (LO - 1), LO)
            j0, j1 = x[0:8], x[8:16]
            j08, j18, u0, u1 = x[16:17], x[17:18], x[20:21], x[21:22]
            at, at8 = gather_mixed(hi, hot, zh_ref[...], zl_ref[...], count, tail_rows)
            w0 = jnp.sum(j0 * at, axis=0, keepdims=True) + j08 * at8
            w1 = jnp.sum(j1 * at, axis=0, keepdims=True) + j18 * at8
            if offset == 0:
                for k in range(per):
                    cols = slice(k * slot, (k + 1) * slot)
                    w_ref[chunk * per + k, 0:1, :] = w0[:, cols]
                    w_ref[chunk * per + k, 1:2, :] = w1[:, cols]
            e0, e1 = u0 + w0, u1 + w1
            ts_ref[...] += scatter_mixed(
                hi, hot, [j0 * e0 + j1 * e1], [j08 * e0 + j18 * e1], count, tail_rows
            )
            return energy + e0 * e0 + e1 * e1

        return body

    energy = jnp.zeros((1, per * slot), F32)
    energy = lax.fori_loop(0, chunks, second(a_ref, 0), energy)
    energy = lax.fori_loop(0, chunks, second(b_ref, 1), energy)
    y = ts_ref[...] / td_ref[...]
    high, low = halves(y)
    zh_ref[...] = high.astype(BF16)
    zl_ref[...] = low.astype(BF16)
    share = 1.0 / n_grp
    gamma = gamma + share * scalars[:, 0:1]
    delta = norm + total_of(energy) + share * scalars[:, slot // 2 : slot // 2 + 1]
    tile = lax.axis_index("tile")
    mine, core = tile // 2, tile % 2
    for g in range(n_grp):
        block = g * n_z + mine
        x = a_ref[block]
        index = x[22:23].astype(jnp.int32)
        hi, hot = index >> LO_BITS, one_hot_rows(index & (LO - 1), LO)
        at, at8 = gather_mixed(hi, hot, zh_ref[...], zl_ref[...], count, tail_rows)
        v0 = jnp.sum(x[0:8] * at, axis=0, keepdims=True) + x[16:17] * at8
        v1 = jnp.sum(x[8:16] * at, axis=0, keepdims=True) + x[17:18] * at8
        back_ref[g, 0:2, 0:slot] = w_ref[block, 0:2, :]
        back_ref[g, 2:3, 0:slot] = v0
        back_ref[g, 3:4, 0:slot] = v1
        back_ref[g, :, slot:] = lanes(jnp.concatenate([gamma, delta, gamma, delta], axis=0), 128)
    for source, target in ((tb_ref, cb_ref), (td_ref, cd_ref), (ts_ref, cs_ref)):
        own, own8 = [], []
        for k in range(3):
            rows = source[pl.ds(pl.multiple_of(8 * (3 * mine + k), 8), 8), :]
            tail = source[pl.ds(main + 3 * mine + k, 1), :]
            own += [rows[:, :128], rows[:, 128:]]
            own8 += [tail[:, :128], tail[:, 128:]]
        for m in range(3):
            cols = slice(m * 128, (m + 1) * 128)
            target[0:8, cols] = jnp.where(core == 0, own[m], own[m + 3])
            target[8:9, cols] = jnp.where(core == 0, own8[m], own8[m + 3])


def point_kernel(
    n_grp, back_ref, jp_ref, pidx_ref, pb_ref, pd_ref, cb_ref, cd_ref, cs_ref, out_ref, ps_ref, pt_ref, sc_ref
):
    slot = back_ref.shape[2] - 128
    index = pidx_ref[...]
    mask = is_row(index >> LO_BITS, PH)
    hot = one_hot_rows(index & (LO - 1), LO)
    jp = [jp_ref[k : k + 1, :] for k in range(6)]
    scalars = back_ref[0, :, slot:]
    for h in range(1, n_grp):
        scalars = scalars + back_ref[h, :, slot:]
    gamma, delta = scalars[0:1, 0:1], scalars[1:2, 0:1]
    alpha = gamma / delta
    w = [
        jnp.concatenate([back_ref[h, r : r + 1, 0:slot] for h in range(n_grp)], axis=1) for r in range(4)
    ]
    rhs, diag = pb_ref[...], pd_ref[...]
    z = rhs / diag
    at = gather_points(mask, hot, z)
    error = [sum(jp[3 * a + i] * at[i] for i in range(3)) + w[a] for a in range(2)]
    s = z + scatter_points(mask, hot, [jp[i] * error[0] + jp[3 + i] * error[1] for i in range(3)])
    r1 = rhs - alpha * s
    z1 = r1 / diag
    at = gather_points(mask, hot, z1)
    error = [
        sum(jp[3 * a + i] * at[i] for i in range(3)) + (w[a] - alpha * w[2 + a]) for a in range(2)
    ]
    t = z1 + scatter_points(mask, hot, [jp[i] * error[0] + jp[3 + i] * error[1] for i in range(3)])
    ps_ref[...] = s
    pt_ref[...] = t
    cr1 = cb_ref[...] - alpha * cs_ref[...]
    cz1 = cr1 / cd_ref[...]
    gamma1 = total_of(r1 * z1) + total_of(cr1 * cz1)
    delta1 = (
        total_of(error[0] * error[0] + error[1] * error[1]) + total_of(z1 * z1) + total_of(cz1 * cz1)
    )
    sc_ref[...] = lanes(jnp.concatenate([gamma, alpha], axis=0), 128)
    tail = lanes(jnp.concatenate([gamma1, delta1], axis=0), 128)
    per = out_ref.shape[0] // n_grp
    for h in range(n_grp):
        cols = slice(h * slot, (h + 1) * slot)
        block = jnp.concatenate([jnp.concatenate([e[:, cols] for e in error], axis=0), tail], axis=1)

        @pl.loop(0, per)
        def _(tile, block=block, h=h):
            out_ref[h * per + tile] = block


def final_kernel(
    err_ref, a_ref, b_ref, pb_ref, pd_ref, ps_ref, pt_ref, cb_ref, cd_ref, cs_ref, sc_ref,
    px_ref, cx_ref, pr_ref, cr_ref, acc_ref,
):
    blocks, _, slot = a_ref.shape
    per = min(4, blocks)
    chunks = blocks // per
    tile = lax.axis_index("tile")
    core = tile % 2
    acc_ref[...] = jnp.zeros(acc_ref.shape, F32)

    def body(ref, parity):
        def step(chunk, scalars):
            x, index = read_chunk(ref, chunk, per)
            errs = [err_ref[2 * (chunk * per + k) + parity] for k in range(per)]
            e = jnp.concatenate([v[:, 0:slot] for v in errs], axis=1)
            for v in errs:
                scalars = scalars + v[:, slot:]
            index = index - tile * CAM_DEV
            hi = index >> 7
            hot = one_hot_rows(index & 127, 128)
            j0, j1 = x[0:8], x[8:16]
            e0, e1 = e[0:1], e[1:2]
            acc_ref[...] += scatter_mixed(
                hi, hot, [j0 * e0 + j1 * e1], [x[16:17] * e0 + x[17:18] * e1], 3, 8
            )
            return scalars

        return step

    scalars = lax.fori_loop(0, chunks, body(a_ref, core), jnp.zeros((2, 128), F32))
    scalars = lax.fori_loop(0, chunks, body(b_ref, 1 - core), scalars)
    gamma1, delta1 = scalars[0:1, 0:1], scalars[1:2, 0:1]
    gamma, alpha = sc_ref[0:1, 0:1], sc_ref[1:2, 0:1]
    ratio = gamma1 / gamma
    alpha1 = gamma1 / (delta1 - ratio * gamma1 / alpha)

    rhs, diag, s = pb_ref[...], pd_ref[...], ps_ref[...]
    z = rhs / diag
    r1 = rhs - alpha * s
    z1 = r1 / diag
    x = alpha * z + alpha1 * (z1 + ratio * z)
    r2 = r1 - alpha1 * (pt_ref[...] + ratio * s)
    for i in range(3):
        for hi in range(PH):
            row = i * PH + hi
            px_ref[i : i + 1, hi * LO : (hi + 1) * LO] = x[row : row + 1]
            pr_ref[i : i + 1, hi * LO : (hi + 1) * LO] = r2[row : row + 1]

    rhs, s = cb_ref[...], cs_ref[...]
    z = rhs / cd_ref[...]
    r1 = rhs - alpha * s
    z1 = r1 / cd_ref[...]
    cx_ref[...] = alpha * z + alpha1 * (z1 + ratio * z)
    base = r1 - alpha1 * (z1 + ratio * s)
    for k in range(3):
        cols = slice(k * 128, (k + 1) * 128)
        cr_ref[0:8, cols] = base[0:8, cols] - alpha1 * acc_ref[8 * k : 8 * k + 8, :]
        cr_ref[8:9, cols] = base[8:9, cols] - alpha1 * acc_ref[24 + k : 25 + k, :]


def shape(*dims):
    return jax.ShapeDtypeStruct(dims, F32)


def shards(jac_point, jac_cam, resid, point_index, cam_index):
    n_grp, n_tile = lax.axis_size("grp"), lax.axis_size("tile")
    n_z = n_tile // 2
    obs = jac_point.shape[1]
    slot = obs // n_grp
    blocks = n_grp * n_z
    count = CAM_DEV * n_tile // LO
    tail_rows = -(-count // 16) * 16
    rows = 8 * count + tail_rows
    groups = [[d * 2 + core for d in range(blocks)] for core in range(2)]
    swap = [(t, t ^ 1) for t in range(n_tile)]
    pidx, cidx = point_index.reshape(1, obs), cam_index.reshape(1, obs)

    packed, pb, pd = pl.pallas_call(
        functools.partial(pack_kernel, n_grp, n_z),
        out_shape=(shape(blocks, 24, slot), shape(3 * PH, LO), shape(3 * PH, LO)),
        compiler_params=PARAMS,
        name="pack",
    )(jac_point, jac_cam, resid, pidx, cidx)
    own = lax.all_to_all(packed, ("grp", "tile"), 0, 0, axis_index_groups=groups, tiled=True)
    other = lax.ppermute(own, "tile", swap)
    back, cb, cd, cs = pl.pallas_call(
        functools.partial(camera_kernel, n_grp, n_z),
        out_shape=(shape(n_grp, 4, slot + 128),) + (shape(9, CAM_DEV),) * 3,
        scratch_shapes=[
            pltpu.VMEM((2 * rows, LO), F32),
            pltpu.VMEM((blocks, 2, slot), F32),
            pltpu.VMEM((rows, LO), BF16),
            pltpu.VMEM((rows, LO), BF16),
            pltpu.VMEM((rows, LO), F32),
            pltpu.VMEM((rows, LO), F32),
            pltpu.VMEM((rows, LO), F32),
        ],
        compiler_params=PARAMS,
        name="cameras",
    )(own, other)
    back = lax.all_to_all(back, "grp", 0, 0, tiled=True)
    errors, ps, pt, sc = pl.pallas_call(
        functools.partial(point_kernel, n_grp),
        out_shape=(
            shape(n_grp * n_tile, 2, slot + 128),
            shape(3 * PH, LO),
            shape(3 * PH, LO),
            shape(2, 128),
        ),
        compiler_params=PARAMS,
        name="points",
    )(back, jac_point, pidx, pb, pd, cb, cd, cs)
    errors = lax.all_to_all(errors, ("grp", "tile"), 0, 0, tiled=True)
    return pl.pallas_call(
        final_kernel,
        out_shape=(shape(3, P_DEV), shape(9, CAM_DEV), shape(3, P_DEV), shape(9, CAM_DEV)),
        scratch_shapes=[pltpu.VMEM((32, 128), F32)],
        compiler_params=PARAMS,
        name="finish",
    )(errors, own, other, pb, pd, ps, pt, cb, cd, cs, sc)


def solution(mesh):
    placed = (
        P(None, ("grp", "tile")),
        P(None, ("grp", "tile")),
        P(None, ("grp", "tile")),
        P(("grp", "tile")),
        P(("grp", "tile")),
    )
    return jax.shard_map(
        shards,
        mesh=mesh,
        in_specs=placed,
        out_specs=(P(None, ("grp", "tile")),) * 4,
        check_vma=False,
    )
```

time: 378 us -> 62.3 us (0.16)
  waiting for transfers between devices: 92.8 us -> 1.72 us
  other arithmetic: 79.6 us -> 0 us
  blocking collectives: 104 us -> 38.1 us
  local copies, waits for them, and re-layouts: 46.8 us -> 4.4 us
  starting transfers between devices: 26.7 us -> 0.01 us
  between operations: 25.2 us -> 0.67 us
  Pallas kernels: 0 us -> 17 us
    reduce_scatter x3 -> x0, waiting for transfers between devices: 82.3 us -> none  [the longest x2 52.2 us: apply(): lax.psum_scatter(segment_rows(column, owned_index, cam_grp), 'tile', scat...]
    psum x2 -> x0, blocking collectives: 75.6 us -> none  [paired_sums(): lax.psum((inner(rp, rc, zp, zc), inner(zp, zc, sp, sc)), ('grp', 'tile'))]
    scatter-add x7 -> x0, other arithmetic: 52.4 us -> none  [segment_rows(): jax.ops.segment_sum(row, ids, num_segments=count)]
    all_to_all x0 -> x3, blocking collectives: none -> 38.1 us  [the longest x1 21.5 us: shards(): lax.all_to_all(packed, ('grp', 'tile'), 0, 0, axis_index_groups=groups, t...]
    all_gather x2 -> x0, blocking collectives: 28.8 us -> none  [apply(): group_cams = lax.all_gather(vc, 'tile', axis=1, tiled=True)]
    all_to_all x7 -> x0, starting transfers between devices: 26.5 us -> none  [the longest x2 7.3 us: apply(): lax.all_to_all(fetched, 'grp', split_axis=1, concat_axis=1, tiled=True)]
    gather x6 -> x0, local copies, waits for them, and re-layouts: 17.6 us -> none  [the longest x4 9.16 us: apply(): point_term = jnp.sum(jp * vp[:, point_index][None], axis=1)]
    pallas_call x0 -> x4, Pallas kernels: none -> 17 us  [the longest x1 10.5 us: shards(): pl.pallas_call(functools.partial(camera_kernel, n_grp, n_z), out_shape=(s...]
  transfers between devices with their start and end apart: 10 -> 1, of which waited for: 7 -> 1; matrix products, arithmetic and copies ran while one was open for 15% -> 0% of each run, Pallas kernels for 0% -> 0%
where the time goes in v1:
time: 62.3 us; the launch traced here: 61.9 us
  blocking collectives  38.1 us (61%)
  Pallas kernels  17 us (27%)
  local copies, waits for them, and re-layouts  4.4 us (7%)
  waiting for transfers between devices  1.72 us (3%)
  between operations  0.67 us (1%)
    all_to_all x1, blocking collectives, shards(): lax.all_to_all(packed, ('grp', 'tile'), 0, 0, axis_index_groups=groups, t...  21.5 us
    pallas_call x1, Pallas kernels, shards(): pl.pallas_call(functools.partial(camera_kernel, n_grp, n_z), out_shape=(s...  10.5 us
    all_to_all x1, blocking collectives, shards(): errors = lax.all_to_all(errors, ('grp', 'tile'), 0, 0, tiled=True)  9.47 us
    all_to_all x1, blocking collectives, shards(): back = lax.all_to_all(back, 'grp', 0, 0, tiled=True)  7.09 us
    unnamed x12, local copies, waits for them, and re-layouts  4.4 us
    pallas_call x1, Pallas kernels, shards(): pl.pallas_call(final_kernel, out_shape=(shape(3, P_DEV), shape(9, CAM_DEV...  3.37 us
    pallas_call x1, Pallas kernels, shards(): pl.pallas_call(functools.partial(point_kernel, n_grp), out_shape=(shape(n...  2.08 us
    ppermute x1, waiting for transfers between devices, shards(): other = lax.ppermute(own, 'tile', swap)  1.72 us
  transfers between devices with their start and end apart: 1, of which 1 were waited for; matrix products, arithmetic and copies ran while one was open for 0% of the time, Pallas kernels for 0%

profile of v1, /device:TPU:0, one launch (start us, length us, event | category | flops | bytes accessed | tf_op | source)
XLA Modules:
  0.0 61.9 jit_solution(7809264279872082678)
XLA Ops:
  0.6 0.0 copy-start
  0.6 0.7 %copy-done = f32[6,1024]{1,0:T(8,128)S(1)} copy-done((f32[6,1024]{1,0:T(8,128)S(1)}, f32[6,1024]{1,0:T(8,128)}, u32[]{:S(2)}) %copy-start) | copy-done | bytes 24600
  1.4 0.0 copy-start.1
  1.4 0.9 %copy-done.1 = f32[18,1024]{1,0:T(8,128)S(1)} copy-done((f32[18,1024]{1,0:T(8,128)S(1)}, f32[18,1024]{1,0:T(8,128)}, u32[]{:S(2)}) %copy-start.1) | copy-done | bytes 73752
  2.3 0.0 copy-start.2
  2.3 0.7 %copy-done.2 = s32[1024]{0:T(1024)S(1)} copy-done((s32[1024]{0:T(1024)S(1)}, s32[1024]{0:T(1024)}, u32[]{:S(2)}) %copy-start.2) | copy-done | bytes 4120
  3.0 0.0 copy-start.4
  3.0 0.7 %copy-done.4 = f32[2,1024]{1,0:T(2,128)S(1)} copy-done((f32[2,1024]{1,0:T(2,128)S(1)}, f32[2,1024]{1,0:T(2,128)}, u32[]{:S(2)}) %copy-start.4) | copy-done | bytes 8216
  3.7 0.0 copy-start.5
  3.7 0.7 %copy-done.5 = s32[1024]{0:T(1024)S(1)} copy-done((s32[1024]{0:T(1024)S(1)}, s32[1024]{0:T(1024)}, u32[]{:S(2)}) %copy-start.5) | copy-done | bytes 4120
  4.4 1.0 %pack.1 = (f32[16,24,256]{2,1,0:T(8,128)S(1)}, f32[48,256]{1,0:T(8,128)S(1)}, f32[48,256]{1,0:T(8,128)S(1)}) custom-call(f32[6,1024]{1,0:T(8,128)S(1)} %copy-done, f32[18,1024]{1,0:T(8,128)S(1)} %copy-done.1, f32[2,1024]{1,0:T(2,128)S(1)} %copy-done.4, s32[1,1024]{1,0:T(1,128)S(1)} %bitcast.2, s32[1,1024]{1,0:T(1,128)S(1)} %bitcast.4), custom_call_target="tpu_custom_call" | custom-call | tf_op jit(solution)/shard_map/pack/pallas_call | solution.py:383
  5.4 21.5 %all_to_all.15.a_ref = f32[16,24,256]{2,1,0:T(8,128)S(1)} all-to-all(f32[16,24,256]{2,1,0:T(8,128)S(1)} %get-tuple-element.15), channel_id=1, replica_groups={{0,2,4,6,8,10,12,14,16,18,20,22,24,26,28,30},{1,3,5,7,9,11,13,15,17,19,..., dimensions={0} | all-to-all | bytes 786432 | tf_op jit(solution)/shard_map/all_to_all | solution.py:389
  26.9 0.0 collective-permute-start
  26.9 1.7 %collective-permute-done.b_ref = f32[16,24,256]{2,1,0:T(8,128)S(1)} collective-permute-done((f32[16,24,256]{2,1,0:T(8,128)S(1)}, f32[16,24,256]{2,1,0:T(8,128)S(1)}, u32[]{:S(2)}, u32[]{:S(2)}) %collective-permute-start) | collective-permute-done | bytes 393248 | tf_op jit(solution)/shard_map/ppermute | solution.py:390
  28.6 10.5 %cameras.1 = (f32[4,4,384]{2,1,0:T(4,128)S(1)}, f32[9,384]{1,0:T(8,128)S(1)}, f32[9,384]{1,0:T(8,128)S(1)}, f32[9,384]{1,0:T(8,128)S(1)}) custom-call(f32[16,24,256]{2,1,0:T(8,128)S(1)} %all_to_all.15.a_ref, f32[16,24,256]{2,1,0:T(8,128)S(1)} %collective-permute-done.b_ref), custom_call_target="tpu_custom_call" | custom-call | tf_op jit(solution)/shard_map/cameras/pallas_call | solution.py:391
  39.2 7.1 %all_to_all.16.back_ref = f32[4,4,384]{2,1,0:T(4,128)S(1)} all-to-all(f32[4,4,384]{2,1,0:T(4,128)S(1)} %get-tuple-element.16), channel_id=1, replica_groups=mesh['grp'=4,'tile'=8] {'grp'}, dimensions={0} | all-to-all | bytes 49152 | tf_op jit(solution)/shard_map/all_to_all | solution.py:406
  46.2 0.0 copy-start.3
  46.2 0.7 %copy-done.3 = s32[1024]{0:T(1024)S(1)} copy-done((s32[1024]{0:T(1024)S(1)}, s32[1024]{0:T(1024)}, u32[]{:S(2)}) %copy-start.3) | copy-done | bytes 4120
  46.9 2.1 %points.1 = (f32[32,2,384]{2,1,0:T(2,128)S(1)}, f32[48,256]{1,0:T(8,128)S(1)}, f32[48,256]{1,0:T(8,128)S(1)}, f32[2,128]{1,0:T(2,128)S(1)}) custom-call(f32[4,4,384]{2,1,0:T(4,128)S(1)} %all_to_all.16.back_ref, f32[6,1024]{1,0:T(8,128)S(1)} %copy-done, s32[1,1024]{1,0:T(1,128)S(1)} %bitcast.3, f32[48,256]{1,0:T(8,128)S(1)} %get-tuple-element.17.pb_ref, ...), custom_call_target="tpu_custom_call" | custom-call | tf_op jit(solution)/shard_map/points/pallas_call | solution.py:407
  49.0 9.5 %all_to_all.17.err_ref = f32[32,2,384]{2,1,0:T(2,128)S(1)} all-to-all(f32[32,2,384]{2,1,0:T(2,128)S(1)} %get-tuple-element.22), channel_id=1, replica_groups=mesh['grp'=4,'tile'=8] {'grp','tile'}, dimensions={0} | all-to-all | bytes 196608 | tf_op jit(solution)/shard_map/all_to_all | solution.py:418
  58.5 3.4 %finish.1 = (f32[3,4096]{1,0:T(4,128)}, f32[9,384]{1,0:T(8,128)}, f32[3,4096]{1,0:T(4,128)}, f32[9,384]{1,0:T(8,128)}) custom-call(f32[32,2,384]{2,1,0:T(2,128)S(1)} %all_to_all.17.err_ref, f32[16,24,256]{2,1,0:T(8,128)S(1)} %all_to_all.15.a_ref, f32[16,24,256]{2,1,0:T(8,128)S(1)} %collective-permute-done.b_ref, f32[48,256]{1,0:T(8,128)S(1)} %get-tuple-element.17.pb_ref, ...), custom_call_target="tpu_custom_call" | custom-call | tf_op jit(solution)/shard_map/finish/pallas_call | solution.py:419
Async XLA Ops:
  0.6 0.8 %copy-start = (f32[6,1024]{1,0:T(8,128)S(1)}, f32[6,1024]{1,0:T(8,128)}, u32[]{:S(2)}) copy-start(f32[6,1024]{1,0:T(8,128)} %jp_ref.3) | copy-start | bytes 73732
  1.4 0.9 %copy-start.1 = (f32[18,1024]{1,0:T(8,128)S(1)}, f32[18,1024]{1,0:T(8,128)}, u32[]{:S(2)}) copy-start(f32[18,1024]{1,0:T(8,128)} %jc_ref.1) | copy-start | bytes 221188
  2.3 0.7 %copy-start.2 = (s32[1024]{0:T(1024)S(1)}, s32[1024]{0:T(1024)}, u32[]{:S(2)}) copy-start(s32[1024]{0:T(1024)} %param.8) | copy-start | bytes 12292
  3.0 0.7 %copy-start.4 = (f32[2,1024]{1,0:T(2,128)S(1)}, f32[2,1024]{1,0:T(2,128)}, u32[]{:S(2)}) copy-start(f32[2,1024]{1,0:T(2,128)} %res_ref.1) | copy-start | bytes 24580
  3.7 0.7 %copy-start.5 = (s32[1024]{0:T(1024)S(1)}, s32[1024]{0:T(1024)}, u32[]{:S(2)}) copy-start(s32[1024]{0:T(1024)} %param.9) | copy-start | bytes 12292
  26.9 1.7 %collective-permute-start = (f32[16,24,256]{2,1,0:T(8,128)S(1)}, f32[16,24,256]{2,1,0:T(8,128)S(1)}, u32[]{:S(2)}, u32[]{:S(2)}) collective-permute-start(f32[16,24,256]{2,1,0:T(8,128)S(1)} %all_to_all.15.a_ref), channel_id=1, source_target_pairs={{0,1},{1,0},{2,3},{3,2},{4,5},{5,4},{6,7},{7,6},{8,9},{9,8},{10,11... | collective-permute-start | bytes 1179656 | tf_op jit(solution)/shard_map/ppermute | solution.py:390
  46.2 0.7 %copy-start.3 = (s32[1024]{0:T(1024)S(1)}, s32[1024]{0:T(1024)}, u32[]{:S(2)}) copy-start(s32[1024]{0:T(1024)} %param.8) | copy-start | bytes 12292

commit v2 on v1

v2 whole, which is shorter than its diff:
```python
import functools

import jax
import jax.numpy as jnp
from jax import lax
from jax.experimental import pallas as pl
from jax.experimental.pallas import tpu as pltpu
from jax.sharding import PartitionSpec as P

P_DEV = 4096
CAM_DEV = 384
LO_BITS = 8
LO = 1 << LO_BITS
PH = P_DEV // LO
DAMPING = 1.0
F32 = jnp.float32
BF16 = jnp.bfloat16
PARAMS = pltpu.CompilerParams(vmem_limit_bytes=48 * 1024 * 1024)


def halves(v):
    high = v.astype(BF16).astype(F32)
    return high, v - high


def rows16(width, step=1):
    numbers = lax.broadcasted_iota(jnp.int32, (16, width), 0)
    return (numbers // step if step > 1 else numbers).astype(F32).astype(BF16)


def sixteen(row):
    return jnp.broadcast_to(row.astype(F32), (16, row.shape[1])).astype(BF16)


def one_hot_rows(index, rows):
    wide, numbers = sixteen(index), rows16(index.shape[1])
    one, none = jnp.ones(wide.shape, BF16), jnp.zeros(wide.shape, BF16)
    return jnp.concatenate(
        [jnp.where(wide == numbers + BF16(16 * k), one, none) for k in range(rows // 16)], axis=0
    )


def dot_nt(a, b):
    return lax.dot_general(a, b, (((1,), (1,)), ((), ())), preferred_element_type=F32)


def dot_nn(a, b):
    return lax.dot_general(a, b, (((1,), (0,)), ((), ())), preferred_element_type=F32)


def is_row(hi, rows):
    return lax.broadcasted_iota(jnp.int32, (rows, hi.shape[1]), 0) == hi


def spread_row(mask, row):
    return jnp.where(mask, jnp.broadcast_to(row, mask.shape), 0.0)


def two_parts(v):
    high = v.astype(BF16)
    return high, (v - high.astype(F32)).astype(BF16)


def scatter_mixed(hi, hot, mains, tails, count, tail_rows):
    wide = sixteen(hi)
    none = jnp.zeros(wide.shape, BF16)
    single = len(mains) == 1
    numbers = rows16(hi.shape[1], 8) if single else none
    main_parts = two_parts(jnp.concatenate(mains * 2 if single else mains, axis=0))
    tail_parts = [two_parts(jnp.broadcast_to(v, wide.shape)) for v in tails]
    here = [wide == numbers + BF16(k) for k in range(0, count, 2 if single else 1)]
    tail_here = [wide == rows16(hi.shape[1]) + BF16(k) for k in range(0, tail_rows, 16)]
    pieces = []
    for part in range(2):
        pieces += [jnp.where(mask, main_parts[part], none) for mask in here]
        pieces += [jnp.where(mask, v[part], none) for v in tail_parts for mask in tail_here]
    return dot_nt(jnp.concatenate(pieces, axis=0), hot)


def both(v):
    half = v.shape[0] // 2
    return v[:half] + v[half:]


def gather_mixed(hi, hot, table, count, tail_rows):
    found = dot_nn(table, hot)
    hi8 = jnp.broadcast_to(hi, (8, hi.shape[1]))
    main = jnp.zeros(hi8.shape, F32)
    half = found.shape[0] // 2
    for k in range(count):
        rows = slice(k * 8, k * 8 + 8)
        low = slice(half + k * 8, half + k * 8 + 8)
        main = main + jnp.where(hi8 == k, found[rows] + found[low], 0.0)
    tail = found[count * 8 : half] + found[half + count * 8 :]
    tail = jnp.sum(jnp.where(is_row(hi, tail_rows), tail, 0.0), axis=0, keepdims=True)
    return main, tail


def stacked(table):
    high, low = halves(table)
    return jnp.concatenate([high, low], axis=0).astype(BF16)


def scatter_points(mask, hot, rows):
    parts = [halves(v) for v in rows]
    lhs = jnp.concatenate([spread_row(mask, v[k]) for k in range(2) for v in parts], axis=0)
    return both(dot_nt(lhs.astype(BF16), hot))


def gather_points(mask, hot, table):
    found = both(dot_nn(stacked(table), hot))
    return [
        jnp.sum(jnp.where(mask, found[i * PH : (i + 1) * PH], 0.0), axis=0, keepdims=True)
        for i in range(found.shape[0] // PH)
    ]


def total_of(v):
    return jnp.sum(jnp.sum(v, axis=0, keepdims=True), axis=1, keepdims=True)


def lanes(v, width):
    return jnp.broadcast_to(v, (v.shape[0], width))


def pack_kernel(
    n_grp, n_z, jp_hbm, jc_hbm, res_hbm, pidx_hbm, cidx_hbm,
    out_ref, pb_ref, pd_ref, pu_ref, jp_ref, pidx_ref,
    jc_ref, res_ref, cidx_ref, sems,
):
    copies = [
        pltpu.make_async_copy(source, target, sems.at[k])
        for k, (source, target) in enumerate(
            (
                (pidx_hbm, pidx_ref),
                (jp_hbm, jp_ref),
                (res_hbm, res_ref),
                (jc_hbm, jc_ref),
                (cidx_hbm, cidx_ref),
            )
        )
    ]
    for copy in copies:
        copy.start()
    for copy in copies:
        copy.wait()
    slot = out_ref.shape[2]
    index = pidx_ref[...]
    mask = is_row(index >> LO_BITS, PH)
    hot = one_hot_rows(index & (LO - 1), LO)
    jp = [jp_ref[k : k + 1, :] for k in range(6)]
    res = [res_ref[a : a + 1, :] for a in range(2)]
    grad = [-(jp[i] * res[0] + jp[3 + i] * res[1]) for i in range(3)]
    square = [jp[i] * jp[i] + jp[3 + i] * jp[3 + i] for i in range(3)]
    table = scatter_points(mask, hot, grad + square)
    rhs = table[: 3 * PH]
    diag = table[3 * PH :] + DAMPING
    pb_ref[...] = rhs
    pd_ref[...] = diag
    z = rhs / diag
    at = gather_points(mask, hot, z)
    u = [sum(jp[3 * a + i] * at[i] for i in range(3)) for a in range(2)]
    pu_ref[0:1, :] = u[0]
    pu_ref[1:2, :] = u[1]
    gamma = total_of(rhs * z)
    norm = total_of(z * z)
    scalars = jnp.concatenate([lanes(gamma, slot // 2), lanes(norm, slot // 2)], axis=1)
    cams = cidx_ref[...].astype(F32)
    for h in range(n_grp):
        cols = slice(h * slot, (h + 1) * slot)
        block = jnp.concatenate(
            [
                jc_ref[0:8, cols],
                jc_ref[9:17, cols],
                jc_ref[8:9, cols],
                jc_ref[17:18, cols],
                res[0][:, cols],
                res[1][:, cols],
                u[0][:, cols],
                u[1][:, cols],
                cams[:, cols],
                scalars,
            ],
            axis=0,
        )

        @pl.loop(0, n_z)
        def _(z_to, block=block, h=h):
            out_ref[h * n_z + z_to] = block


def read_blocks(ref, numbers):
    x = jnp.concatenate([ref[k] for k in numbers], axis=1)
    return x, x[22:23].astype(jnp.int32)


def chunk_of(chunk, per):
    return [chunk * per + k for k in range(per)]


def first_sums(ref, acc_ref, per, count, tail_rows):
    def body(chunk, carry):
        x, index = read_blocks(ref, chunk_of(chunk, per))
        hi, hot = index >> LO_BITS, one_hot_rows(index & (LO - 1), LO)
        j0, j1 = x[0:8], x[8:16]
        j08, j18, r0, r1 = x[16:17], x[17:18], x[18:19], x[19:20]
        acc_ref[...] += scatter_mixed(
            hi,
            hot,
            [-(j0 * r0 + j1 * r1), j0 * j0 + j1 * j1],
            [-(j08 * r0 + j18 * r1), j08 * j08 + j18 * j18],
            count,
            tail_rows,
        )
        return carry

    lax.fori_loop(0, ref.shape[0] // per, body, 0)


def own_sums_kernel(count, tail_rows, a_ref, acc_ref):
    acc_ref[...] = jnp.zeros(acc_ref.shape, F32)
    first_sums(a_ref, acc_ref, min(16, a_ref.shape[0]), count, tail_rows)


def camera_kernel(
    n_grp, n_z, count, tail_rows, a_ref, b_ref, start_ref,
    back_ref, tb_ref, td_ref, ts_ref,
    acc_ref, w_ref, zz_ref,
):
    blocks, _, slot = a_ref.shape
    per = min(8, blocks)
    chunks = blocks // per
    acc_ref[...] = start_ref[...]
    first_sums(b_ref, acc_ref, min(16, blocks), count, tail_rows)
    scalars = jnp.zeros((1, slot), F32)
    for ref in (a_ref, b_ref):
        scalars = scalars + jnp.sum(ref[:, 23, :], axis=0, keepdims=True)
    main = 8 * count
    half = acc_ref.shape[0] // 2
    for k in range(count):
        row = 16 * k
        tb_ref[8 * k : 8 * k + 8, :] = acc_ref[row : row + 8, :] + acc_ref[half + row : half + row + 8, :]
        row = 16 * k + 8
        td_ref[8 * k : 8 * k + 8, :] = (
            acc_ref[row : row + 8, :] + acc_ref[half + row : half + row + 8, :] + DAMPING
        )
    tb_ref[main:, :] = (
        acc_ref[2 * main : 2 * main + tail_rows, :]
        + acc_ref[half + 2 * main : half + 2 * main + tail_rows, :]
    )
    td_ref[main:, :] = (
        acc_ref[2 * main + tail_rows : half, :] + acc_ref[half + 2 * main + tail_rows :, :] + DAMPING
    )
    z = tb_ref[...] / td_ref[...]
    gamma = total_of(tb_ref[...] * z)
    norm = total_of(z * z)
    zz_ref[...] = stacked(z)
    ts_ref[...] = z
    acc_ref[0:half, :] = jnp.zeros((half, LO), F32)

    def second(ref, keep):
        def body(chunk, energy):
            numbers = chunk_of(chunk, per)
            x, index = read_blocks(ref, numbers)
            hi, hot = index >> LO_BITS, one_hot_rows(index & (LO - 1), LO)
            j0, j1 = x[0:8], x[8:16]
            j08, j18, u0, u1 = x[16:17], x[17:18], x[20:21], x[21:22]
            at, at8 = gather_mixed(hi, hot, zz_ref[...], count, tail_rows)
            w0 = jnp.sum(j0 * at, axis=0, keepdims=True) + j08 * at8
            w1 = jnp.sum(j1 * at, axis=0, keepdims=True) + j18 * at8
            if keep:
                for k, number in enumerate(numbers):
                    cols = slice(k * slot, (k + 1) * slot)
                    w_ref[number, 0:1, :] = w0[:, cols]
                    w_ref[number, 1:2, :] = w1[:, cols]
            e0, e1 = u0 + w0, u1 + w1
            acc_ref[0:half, :] += scatter_mixed(
                hi, hot, [j0 * e0 + j1 * e1], [j08 * e0 + j18 * e1], count, tail_rows
            )
            return energy + e0 * e0 + e1 * e1

        return body

    energy = jnp.zeros((1, per * slot), F32)
    energy = lax.fori_loop(0, chunks, second(a_ref, True), energy)
    energy = lax.fori_loop(0, chunks, second(b_ref, False), energy)
    ts_ref[...] += both(acc_ref[0:half, :])
    zz_ref[...] = stacked(ts_ref[...] / td_ref[...])
    share = 1.0 / n_grp
    gamma = gamma + share * scalars[:, 0:1]
    delta = norm + total_of(energy) + share * scalars[:, slot // 2 : slot // 2 + 1]
    mine = lax.axis_index("tile") // 2
    numbers = [g * n_z + mine for g in range(n_grp)]
    per = min(4, n_grp)
    for first in range(0, n_grp, per):
        some = numbers[first : first + per]
        x, index = read_blocks(a_ref, some)
        hi, hot = index >> LO_BITS, one_hot_rows(index & (LO - 1), LO)
        at, at8 = gather_mixed(hi, hot, zz_ref[...], count, tail_rows)
        v0 = jnp.sum(x[0:8] * at, axis=0, keepdims=True) + x[16:17] * at8
        v1 = jnp.sum(x[8:16] * at, axis=0, keepdims=True) + x[17:18] * at8
        for k in range(per):
            cols = slice(k * slot, (k + 1) * slot)
            g = first + k
            back_ref[g, 0:2, 0:slot] = w_ref[some[k], 0:2, :]
            back_ref[g, 2:3, 0:slot] = v0[:, cols]
            back_ref[g, 3:4, 0:slot] = v1[:, cols]
            back_ref[g, :, slot:] = lanes(jnp.concatenate([gamma, delta, gamma, delta], axis=0), 128)


def mine_kernel(main, tb_ref, td_ref, ts_ref, cb_ref, cd_ref, cs_ref):
    tile = lax.axis_index("tile")
    mine, core = tile // 2, tile % 2
    for source, target in ((tb_ref, cb_ref), (td_ref, cd_ref), (ts_ref, cs_ref)):
        own, own8 = [], []
        for k in range(3):
            rows = source[pl.ds(pl.multiple_of(8 * (3 * mine + k), 8), 8), :]
            tail = source[pl.ds(main + 3 * mine + k, 1), :]
            own += [rows[:, :128], rows[:, 128:]]
            own8 += [tail[:, :128], tail[:, 128:]]
        for m in range(3):
            cols = slice(m * 128, (m + 1) * 128)
            target[0:8, cols] = jnp.where(core == 0, own[m], own[m + 3])
            target[8:9, cols] = jnp.where(core == 0, own8[m], own8[m + 3])


def point_kernel(
    n_grp, back_ref, jp_ref, pidx_ref, pb_ref, pd_ref, pu_ref, cb_ref, cd_ref, cs_ref,
    out_ref, ps_ref, pe_ref, sc_ref,
):
    slot = back_ref.shape[2] - 128
    index = pidx_ref[...]
    mask = is_row(index >> LO_BITS, PH)
    hot = one_hot_rows(index & (LO - 1), LO)
    jp = [jp_ref[k : k + 1, :] for k in range(6)]
    scalars = back_ref[0, :, slot:]
    for h in range(1, n_grp):
        scalars = scalars + back_ref[h, :, slot:]
    gamma, delta = scalars[0:1, 0:1], scalars[1:2, 0:1]
    alpha = gamma / delta
    w = [
        jnp.concatenate([back_ref[h, r : r + 1, 0:slot] for h in range(n_grp)], axis=1) for r in range(4)
    ]
    rhs, diag = pb_ref[...], pd_ref[...]
    z = rhs / diag
    error = [pu_ref[a : a + 1, :] + w[a] for a in range(2)]
    s = z + scatter_points(mask, hot, [jp[i] * error[0] + jp[3 + i] * error[1] for i in range(3)])
    r1 = rhs - alpha * s
    z1 = r1 / diag
    at = gather_points(mask, hot, z1)
    error = [
        sum(jp[3 * a + i] * at[i] for i in range(3)) + (w[a] - alpha * w[2 + a]) for a in range(2)
    ]
    ps_ref[...] = s
    pe_ref[0:1, :] = error[0]
    pe_ref[1:2, :] = error[1]
    cr1 = cb_ref[...] - alpha * cs_ref[...]
    cz1 = cr1 / cd_ref[...]
    gamma1 = total_of(r1 * z1) + total_of(cr1 * cz1)
    delta1 = (
        total_of(error[0] * error[0] + error[1] * error[1]) + total_of(z1 * z1) + total_of(cz1 * cz1)
    )
    sc_ref[...] = lanes(jnp.concatenate([gamma, alpha], axis=0), 128)
    tail = lanes(jnp.concatenate([gamma1, delta1], axis=0), 128)
    per = out_ref.shape[0] // n_grp
    for h in range(n_grp):
        cols = slice(h * slot, (h + 1) * slot)
        block = jnp.concatenate([jnp.concatenate([e[:, cols] for e in error], axis=0), tail], axis=1)

        @pl.loop(0, per)
        def _(tile, block=block, h=h):
            out_ref[h * per + tile] = block


def last_point_sums_kernel(jp_ref, pidx_ref, pe_ref, pt_ref):
    index = pidx_ref[...]
    mask = is_row(index >> LO_BITS, PH)
    hot = one_hot_rows(index & (LO - 1), LO)
    jp = [jp_ref[k : k + 1, :] for k in range(6)]
    error = [pe_ref[a : a + 1, :] for a in range(2)]
    pt_ref[...] = scatter_points(
        mask, hot, [jp[i] * error[0] + jp[3 + i] * error[1] for i in range(3)]
    )


def final_kernel(
    err_ref, a_ref, b_ref, pb_ref, pd_ref, ps_ref, pt_ref, cb_ref, cd_ref, cs_ref, sc_ref,
    px_ref, cx_ref, pr_ref, cr_ref, acc_ref,
):
    blocks, _, slot = a_ref.shape
    per = min(8, blocks)
    chunks = blocks // per
    tile = lax.axis_index("tile")
    core = tile % 2
    acc_ref[...] = jnp.zeros(acc_ref.shape, F32)

    def body(ref, parity):
        def step(chunk, scalars):
            numbers = chunk_of(chunk, per)
            x, index = read_blocks(ref, numbers)
            errs = [err_ref[2 * k + parity] for k in numbers]
            e = jnp.concatenate([v[:, 0:slot] for v in errs], axis=1)
            for v in errs:
                scalars = scalars + v[:, slot:]
            index = index - tile * CAM_DEV
            hi = index >> 7
            hot = one_hot_rows(index & 127, 128)
            j0, j1 = x[0:8], x[8:16]
            e0, e1 = e[0:1], e[1:2]
            acc_ref[...] += scatter_mixed(
                hi, hot, [j0 * e0 + j1 * e1], [x[16:17] * e0 + x[17:18] * e1], 4, 16
            )
            return scalars

        return step

    scalars = lax.fori_loop(0, chunks, body(a_ref, core), jnp.zeros((2, 128), F32))
    scalars = lax.fori_loop(0, chunks, body(b_ref, 1 - core), scalars)
    gamma1, delta1 = scalars[0:1, 0:1], scalars[1:2, 0:1]
    gamma, alpha = sc_ref[0:1, 0:1], sc_ref[1:2, 0:1]
    ratio = gamma1 / gamma
    alpha1 = gamma1 / (delta1 - ratio * gamma1 / alpha)

    rhs, diag, s = pb_ref[...], pd_ref[...], ps_ref[...]
    z = rhs / diag
    r1 = rhs - alpha * s
    z1 = r1 / diag
    x = alpha * z + alpha1 * (z1 + ratio * z)
    r2 = r1 - alpha1 * (z1 + pt_ref[...] + ratio * s)
    for i in range(3):
        for hi in range(PH):
            row = i * PH + hi
            px_ref[i : i + 1, hi * LO : (hi + 1) * LO] = x[row : row + 1]
            pr_ref[i : i + 1, hi * LO : (hi + 1) * LO] = r2[row : row + 1]

    rhs, s = cb_ref[...], cs_ref[...]
    z = rhs / cd_ref[...]
    r1 = rhs - alpha * s
    z1 = r1 / cd_ref[...]
    cx_ref[...] = alpha * z + alpha1 * (z1 + ratio * z)
    sums = both(acc_ref[...])
    base = r1 - alpha1 * (z1 + ratio * s)
    for k in range(3):
        cols = slice(k * 128, (k + 1) * 128)
        cr_ref[0:8, cols] = base[0:8, cols] - alpha1 * sums[8 * k : 8 * k + 8, :]
        cr_ref[8:9, cols] = base[8:9, cols] - alpha1 * sums[32 + k : 33 + k, :]


def shape(*dims):
    return jax.ShapeDtypeStruct(dims, F32)


def shards(jac_point, jac_cam, resid, point_index, cam_index):
    n_grp, n_tile = lax.axis_size("grp"), lax.axis_size("tile")
    n_z = n_tile // 2
    obs = jac_point.shape[1]
    slot = obs // n_grp
    blocks = n_grp * n_z
    count = CAM_DEV * n_tile // LO
    tail_rows = -(-count // 16) * 16
    rows = 8 * count + tail_rows
    groups = [[d * 2 + core for d in range(blocks)] for core in range(2)]
    swap = [(t, t ^ 1) for t in range(n_tile)]
    pidx, cidx = point_index.reshape(1, obs), cam_index.reshape(1, obs)

    hbm = pl.BlockSpec(memory_space=pltpu.HBM)
    packed, pb, pd, pu, jp, pidx = pl.pallas_call(
        functools.partial(pack_kernel, n_grp, n_z),
        in_specs=[hbm] * 5,
        out_shape=(
            shape(blocks, 24, slot),
            shape(3 * PH, LO),
            shape(3 * PH, LO),
            shape(2, obs),
            shape(6, obs),
            jax.ShapeDtypeStruct((1, obs), jnp.int32),
        ),
        scratch_shapes=[
            pltpu.VMEM((18, obs), F32),
            pltpu.VMEM((2, obs), F32),
            pltpu.VMEM((1, obs), jnp.int32),
            pltpu.SemaphoreType.DMA((5,)),
        ],
        compiler_params=PARAMS,
        name="pack",
    )(*(pltpu.with_memory_space_constraint(x, pltpu.HBM) for x in (jac_point, jac_cam, resid, pidx, cidx)))
    own = lax.all_to_all(packed, ("grp", "tile"), 0, 0, axis_index_groups=groups, tiled=True)
    other = lax.ppermute(own, "tile", swap)
    sums = pl.pallas_call(
        functools.partial(own_sums_kernel, count, tail_rows),
        out_shape=shape(4 * rows, LO),
        compiler_params=PARAMS,
        name="own_sums",
        cost_estimate=pl.CostEstimate(flops=2 * 10**9, bytes_accessed=10**6, transcendentals=0),
    )(own)
    table = shape(rows, LO)
    back, tb, td, ts = pl.pallas_call(
        functools.partial(camera_kernel, n_grp, n_z, count, tail_rows),
        out_shape=(shape(n_grp, 4, slot + 128), table, table, table),
        scratch_shapes=[
            pltpu.VMEM((4 * rows, LO), F32),
            pltpu.VMEM((blocks, 2, slot), F32),
            pltpu.VMEM((2 * rows, LO), BF16),
        ],
        compiler_params=PARAMS,
        name="cameras",
    )(own, other, sums)
    back = lax.all_to_all(back, "grp", 0, 0, tiled=True)
    cb, cd, cs = pl.pallas_call(
        functools.partial(mine_kernel, 8 * count),
        out_shape=(shape(9, CAM_DEV),) * 3,
        compiler_params=PARAMS,
        name="mine",
    )(tb, td, ts)
    errors, ps, pe, sc = pl.pallas_call(
        functools.partial(point_kernel, n_grp),
        out_shape=(
            shape(n_grp * n_tile, 2, slot + 128),
            shape(3 * PH, LO),
            shape(2, obs),
            shape(2, 128),
        ),
        compiler_params=PARAMS,
        name="points",
    )(back, jp, pidx, pb, pd, pu, cb, cd, cs)
    errors = lax.all_to_all(errors, ("grp", "tile"), 0, 0, tiled=True)
    pt = pl.pallas_call(
        last_point_sums_kernel,
        out_shape=shape(3 * PH, LO),
        compiler_params=PARAMS,
        name="last_point_sums",
    )(jp, pidx, pe)
    return pl.pallas_call(
        final_kernel,
        out_shape=(shape(3, P_DEV), shape(9, CAM_DEV), shape(3, P_DEV), shape(9, CAM_DEV)),
        scratch_shapes=[pltpu.VMEM((96, 128), F32)],
        compiler_params=PARAMS,
        name="finish",
    )(errors, own, other, pb, pd, ps, pt, cb, cd, cs, sc)


def solution(mesh):
    placed = (
        P(None, ("grp", "tile")),
        P(None, ("grp", "tile")),
        P(None, ("grp", "tile")),
        P(("grp", "tile")),
        P(("grp", "tile")),
    )
    return jax.shard_map(
        shards,
        mesh=mesh,
        in_specs=placed,
        out_specs=(P(None, ("grp", "tile")),) * 4,
        check_vma=False,
    )
```

time: 62.3 us -> 53.1 us (0.85)
  blocking collectives: 38.1 us -> 21.5 us
  waiting for transfers between devices: 1.72 us -> 12.7 us
  starting transfers between devices: 0.01 us -> 5.83 us
  Pallas kernels: 17 us -> 12.1 us
  local copies, waits for them, and re-layouts: 4.4 us -> 0 us
    all_to_all x2 -> x0, blocking collectives: 16.6 us -> none  [the longest x1 9.47 us: shards(): errors = lax.all_to_all(errors, ('grp', 'tile'), 0, 0, tiled=True)]
    all_to_all x0 -> x2, waiting for transfers between devices: none -> 12.1 us  [the longest x1 7.48 us: shards(): errors = lax.all_to_all(errors, ('grp', 'tile'), 0, 0, tiled=True)]
    all_to_all x0 -> x2, starting transfers between devices: none -> 5.83 us  [the longest x1 3.26 us: shards(): back = lax.all_to_all(back, 'grp', 0, 0, tiled=True)]
    unnamed x12 -> x0, local copies, waits for them, and re-layouts: 4.4 us -> none
    pallas_call x2 -> x5, Pallas kernels: 11.6 us -> 8.46 us  [the longest x1 5.25 us: shards(): pl.pallas_call(functools.partial(camera_kernel, n_grp, n_z, count, tail_r...]
    pallas_call x1, Pallas kernels: 3.37 us -> 2.03 us  [shards(): pl.pallas_call(final_kernel, out_shape=(shape(3, P_DEV), shape(9, CAM_DEV...]
    ppermute x1, waiting for transfers between devices: 1.72 us -> 0.56 us  [shards(): other = lax.ppermute(own, 'tile', swap)]
  transfers between devices with their start and end apart: 1 -> 3, of which waited for: 1 -> 3; matrix products, arithmetic and copies ran while one was open for 0% -> 0% of each run, Pallas kernels for 0% -> 3%
where the time goes in v2:
time: 53.1 us; the launch traced here: 52.8 us
  blocking collectives  21.5 us (40%)
  waiting for transfers between devices  12.7 us (24%)
  Pallas kernels  12.1 us (23%)
  starting transfers between devices  5.83 us (11%)
  between operations  0.68 us (1%)
    all_to_all x1, blocking collectives, shards(): lax.all_to_all(packed, ('grp', 'tile'), 0, 0, axis_index_groups=groups, t...  21.5 us
    all_to_all x1, waiting for transfers between devices, shards(): errors = lax.all_to_all(errors, ('grp', 'tile'), 0, 0, tiled=True)  7.48 us
    pallas_call x1, Pallas kernels, shards(): pl.pallas_call(functools.partial(camera_kernel, n_grp, n_z, count, tail_r...  5.25 us
    all_to_all x1, waiting for transfers between devices, shards(): back = lax.all_to_all(back, 'grp', 0, 0, tiled=True)  4.66 us
    all_to_all x1, starting transfers between devices, shards(): back = lax.all_to_all(back, 'grp', 0, 0, tiled=True)  3.26 us
    all_to_all x1, starting transfers between devices, shards(): errors = lax.all_to_all(errors, ('grp', 'tile'), 0, 0, tiled=True)  2.57 us
    pallas_call x1, Pallas kernels, shards(): pl.pallas_call(final_kernel, out_shape=(shape(3, P_DEV), shape(9, CAM_DEV...  2.03 us
    pallas_call x1, Pallas kernels, shards(): pl.pallas_call(functools.partial(pack_kernel, n_grp, n_z), in_specs=[hbm]...  1.73 us
  transfers between devices with their start and end apart: 3, of which 3 were waited for; matrix products, arithmetic and copies ran while one was open for 0% of the time, Pallas kernels for 3%

profile of v2, /device:TPU:0, one launch (start us, length us, event | category | flops | bytes accessed | tf_op | source)
XLA Modules:
  0.0 52.8 jit_solution(13499589197423752305)
XLA Ops:
  0.6 1.7 %pack.1 = (f32[16,24,256]{2,1,0:T(8,128)S(1)}, f32[48,256]{1,0:T(8,128)S(1)}, f32[48,256]{1,0:T(8,128)S(1)}, f32[2,1024]{1,0:T(2,128)S(1)}, f32[6,1024]{1,0:T(8,128)S(1)}, /*index=5*/s32[1,1024]{1,0:T(1,128)S(1)}) custom-call(f32[6,1024]{1,0:T(8,128)} %jp_hbm.1, f32[18,1024]{1,0:T(8,128)} %jc_hbm.1, f32[2,1024]{1,0:T(2,128)} %res_hbm.1, s32[1,1024]{1,0:T(1,128)} %bitcast.2, ...), custom_call_target="tpu_custom_call" | custom-call | tf_op jit(solution)/shard_map/pack/pallas_call | solution.py:467
  2.4 21.5 %all_to_all.15.a_ref = f32[16,24,256]{2,1,0:T(8,128)S(1)} all-to-all(f32[16,24,256]{2,1,0:T(8,128)S(1)} %get-tuple-element.21), channel_id=1, replica_groups={{0,2,4,6,8,10,12,14,16,18,20,22,24,26,28,30},{1,3,5,7,9,11,13,15,17,19,..., dimensions={0} | all-to-all | bytes 786432 | tf_op jit(solution)/shard_map/all_to_all | solution.py:487
  23.9 0.0 collective-permute-start
  23.9 1.2 %own_sums.1.start_ref = f32[448,256]{1,0:T(8,128)S(1)} custom-call(f32[16,24,256]{2,1,0:T(8,128)S(1)} %all_to_all.15.a_ref), custom_call_target="tpu_custom_call" | custom-call | flops 2000000000 | bytes 1000000 | tf_op jit(solution)/shard_map/own_sums/pallas_call | solution.py:489
  25.0 0.6 %collective-permute-done.b_ref = f32[16,24,256]{2,1,0:T(8,128)S(1)} collective-permute-done((f32[16,24,256]{2,1,0:T(8,128)S(1)}, f32[16,24,256]{2,1,0:T(8,128)S(1)}, u32[]{:S(2)}, u32[]{:S(2)}) %collective-permute-start) | collective-permute-done | bytes 393248 | tf_op jit(solution)/shard_map/ppermute | solution.py:488
  25.6 5.2 %cameras.1 = (f32[4,4,384]{2,1,0:T(4,128)}, f32[112,256]{1,0:T(8,128)S(1)}, f32[112,256]{1,0:T(8,128)S(1)}, f32[112,256]{1,0:T(8,128)S(1)}) custom-call(f32[16,24,256]{2,1,0:T(8,128)S(1)} %all_to_all.15.a_ref, f32[16,24,256]{2,1,0:T(8,128)S(1)} %collective-permute-done.b_ref, f32[448,256]{1,0:T(8,128)S(1)} %own_sums.1.start_ref), custom_call_target="tpu_custom_call" | custom-call | tf_op jit(solution)/shard_map/cameras/pallas_call | solution.py:497
  30.8 3.3 %all-to-all-start.1 = ((f32[4,4,384]{2,1,0:T(4,128)}), f32[4,4,384]{2,1,0:T(4,128)S(1)}, u32[]{:S(2)}, u32[]{:S(2)}) async-start(f32[4,4,384]{2,1,0:T(4,128)} %get-tuple-element.22), calls=%async_computation.1 | async-start | bytes 49152 | tf_op jit(solution)/shard_map/all_to_all | solution.py:508
  34.1 4.7 %all-to-all-done.1.back_ref = f32[4,4,384]{2,1,0:T(4,128)S(1)} async-done(((f32[4,4,384]{2,1,0:T(4,128)}), f32[4,4,384]{2,1,0:T(4,128)S(1)}, u32[]{:S(2)}, u32[]{:S(2)}) %all-to-all-start.1) | async-done | bytes 24608 | tf_op jit(solution)/shard_map/all_to_all | solution.py:508
  38.8 1.6 %points.1 = (f32[32,2,384]{2,1,0:T(2,128)}, f32[48,256]{1,0:T(8,128)S(1)}, f32[2,1024]{1,0:T(2,128)S(1)}, f32[2,128]{1,0:T(2,128)S(1)}) custom-call(f32[4,4,384]{2,1,0:T(4,128)S(1)} %all-to-all-done.1.back_ref, f32[6,1024]{1,0:T(8,128)S(1)} %get-tuple-element.23.jp_ref, s32[1,1024]{1,0:T(1,128)S(1)} %get-tuple-element.24.pidx_ref, ...), custom_call_target="tpu_custom_call" | custom-call | tf_op jit(solution)/shard_map/points/pallas_call | solution.py:515
  40.4 2.6 %all-to-all-start.2 = ((f32[32,2,384]{2,1,0:T(2,128)}), f32[32,2,384]{2,1,0:T(2,128)S(1)}, u32[]{:S(2)}, u32[]{:S(2)}) async-start(f32[32,2,384]{2,1,0:T(2,128)} %get-tuple-element.34), calls=%async_computation.2 | async-start | bytes 196608 | tf_op jit(solution)/shard_map/all_to_all | solution.py:526
  43.0 0.3 last_point_sums.1.pt_ref
  43.3 7.5 %all-to-all-done.2.err_ref = f32[32,2,384]{2,1,0:T(2,128)S(1)} async-done(((f32[32,2,384]{2,1,0:T(2,128)}), f32[32,2,384]{2,1,0:T(2,128)S(1)}, u32[]{:S(2)}, u32[]{:S(2)}) %all-to-all-start.2) | async-done | bytes 98336 | tf_op jit(solution)/shard_map/all_to_all | solution.py:526
  50.7 2.0 %finish.1 = (f32[3,4096]{1,0:T(4,128)}, f32[9,384]{1,0:T(8,128)}, f32[3,4096]{1,0:T(4,128)}, f32[9,384]{1,0:T(8,128)}) custom-call(f32[32,2,384]{2,1,0:T(2,128)S(1)} %all-to-all-done.2.err_ref, f32[16,24,256]{2,1,0:T(8,128)S(1)} %all_to_all.15.a_ref, f32[16,24,256]{2,1,0:T(8,128)S(1)} %collective-permute-done.b_ref, f32[48,256]{1,0:T(8,128)S(1)} %get-tuple-element.25.pb_ref, ...), custom_call_target="tpu_custom_call" | custom-call | tf_op jit(solution)/shard_map/finish/pallas_call | solution.py:533
  (1 shorter events, 0.0 us)
Async XLA Ops:
  23.9 1.7 %collective-permute-start = (f32[16,24,256]{2,1,0:T(8,128)S(1)}, f32[16,24,256]{2,1,0:T(8,128)S(1)}, u32[]{:S(2)}, u32[]{:S(2)}) collective-permute-start(f32[16,24,256]{2,1,0:T(8,128)S(1)} %all_to_all.15.a_ref), channel_id=1, source_target_pairs={{0,1},{1,0},{2,3},{3,2},{4,5},{5,4},{6,7},{7,6},{8,9},{9,8},{10,11... | collective-permute-start | bytes 1179656 | tf_op jit(solution)/shard_map/ppermute | solution.py:488
  30.8 8.0 %all-to-all-start.1 = ((f32[4,4,384]{2,1,0:T(4,128)}), f32[4,4,384]{2,1,0:T(4,128)S(1)}, u32[]{:S(2)}, u32[]{:S(2)}) async-start(f32[4,4,384]{2,1,0:T(4,128)} %get-tuple-element.22), calls=%async_computation.1 | async-start | bytes 49152 | tf_op jit(solution)/shard_map/all_to_all | solution.py:508
  40.4 10.4 %all-to-all-start.2 = ((f32[32,2,384]{2,1,0:T(2,128)}), f32[32,2,384]{2,1,0:T(2,128)S(1)}, u32[]{:S(2)}, u32[]{:S(2)}) async-start(f32[32,2,384]{2,1,0:T(2,128)} %get-tuple-element.34), calls=%async_computation.2 | async-start | bytes 196608 | tf_op jit(solution)/shard_map/all_to_all | solution.py:526

commit v3 on v2

--- a/solution.py
+++ b/solution.py
@@ -15,6 +15,8 @@
 DAMPING = 1.0
 F32 = jnp.float32
 BF16 = jnp.bfloat16
+SLOTS = 64
+HALF = 128
 PARAMS = pltpu.CompilerParams(vmem_limit_bytes=48 * 1024 * 1024)
 
 
@@ -33,11 +35,16 @@
 
 
 def one_hot_rows(index, rows):
-    wide, numbers = sixteen(index), rows16(index.shape[1])
-    one, none = jnp.ones(wide.shape, BF16), jnp.zeros(wide.shape, BF16)
-    return jnp.concatenate(
-        [jnp.where(wide == numbers + BF16(16 * k), one, none) for k in range(rows // 16)], axis=0
-    )
+    numbers = rows16(index.shape[1])
+    pieces = []
+    for base in range(0, rows, 256):
+        wide = sixteen(index - base)
+        one, none = jnp.ones(wide.shape, BF16), jnp.zeros(wide.shape, BF16)
+        pieces += [
+            jnp.where(wide == numbers + BF16(16 * k), one, none)
+            for k in range(min(256, rows - base) // 16)
+        ]
+    return jnp.concatenate(pieces, axis=0)
 
 
 def dot_nt(a, b):
@@ -450,7 +457,7 @@
     return jax.ShapeDtypeStruct(dims, F32)
 
 
-def shards(jac_point, jac_cam, resid, point_index, cam_index):
+def replicated(jac_point, jac_cam, resid, point_index, cam_index):
     n_grp, n_tile = lax.axis_size("grp"), lax.axis_size("tile")
     n_z = n_tile // 2
     obs = jac_point.shape[1]
@@ -539,6 +546,368 @@
     )(errors, own, other, pb, pd, ps, pt, cb, cd, cs, sc)
 
 
+def three_parts(v):
+    high = v.astype(BF16).astype(F32)
+    rest = v - high
+    middle = rest.astype(BF16).astype(F32)
+    return jnp.concatenate([high, middle, rest - middle], axis=0).astype(BF16)
+
+
+def thirds(v):
+    rows = v.shape[0] // 3
+    return v[:rows] + v[rows : 2 * rows] + v[2 * rows :]
+
+
+def low_lanes(rows):
+    return lax.broadcasted_iota(jnp.int32, (rows, HALF), 1) < SLOTS
+
+
+def swap_lanes(v):
+    return pltpu.roll(v, SLOTS, 1)
+
+
+def point_start(pidx_ref, jp_ref, res_ref, pb_ref, pd_ref):
+    index = pidx_ref[...]
+    mask = is_row(index >> LO_BITS, PH)
+    hot = one_hot_rows(index & (LO - 1), LO)
+    jp = [jp_ref[k : k + 1, :] for k in range(6)]
+    res = [res_ref[a : a + 1, :] for a in range(2)]
+    grad = [-(jp[i] * res[0] + jp[3 + i] * res[1]) for i in range(3)]
+    square = [jp[i] * jp[i] + jp[3 + i] * jp[3 + i] for i in range(3)]
+    table = scatter_points(mask, hot, grad + square)
+    rhs = table[: 3 * PH]
+    diag = table[3 * PH :] + DAMPING
+    pb_ref[...] = rhs
+    pd_ref[...] = diag
+    z = rhs / diag
+    at = gather_points(mask, hot, z)
+    u = [sum(jp[3 * a + i] * at[i] for i in range(3)) for a in range(2)]
+    return u, total_of(rhs * z), total_of(z * z)
+
+
+def start_copies(pairs, sems):
+    copies = [pltpu.make_async_copy(a, b, sems.at[k]) for k, (a, b) in enumerate(pairs)]
+    for copy in copies:
+        copy.start()
+    for copy in copies:
+        copy.wait()
+
+
+def route_kernel(
+    n_grp, n_tile, jp_hbm, jc_hbm, res_hbm, pidx_hbm, cidx_hbm,
+    out_ref, pb_ref, pd_ref, pu_ref, jp_ref, pidx_ref, place_ref, sc_ref,
+    jc_ref, res_ref, cidx_ref, sems,
+):
+    start_copies(
+        (
+            (pidx_hbm, pidx_ref),
+            (jp_hbm, jp_ref),
+            (res_hbm, res_ref),
+            (jc_hbm, jc_ref),
+            (cidx_hbm, cidx_ref),
+        ),
+        sems,
+    )
+    slot = cidx_ref.shape[1] // n_grp
+    cams = cidx_ref[...]
+    owner = ((cams >> 7) * 171) >> 9
+    local = (cams - owner * CAM_DEV).astype(F32)
+    mine = is_row(owner, n_tile)
+    ones = jnp.where(mine, 1.0, 0.0)
+    stack = jnp.concatenate([ones[:, h * slot : (h + 1) * slot] for h in range(n_grp)], axis=0)
+    before = lax.broadcasted_iota(jnp.int32, (slot, slot), 0)
+    before = before < lax.broadcasted_iota(jnp.int32, (slot, slot), 1)
+    counts = dot_nn(stack.astype(BF16), jnp.where(before, 1.0, 0.0).astype(BF16))
+    counts = jnp.concatenate([counts[h * n_tile : (h + 1) * n_tile] for h in range(n_grp)], axis=1)
+    rank = jnp.sum(jnp.where(mine, counts, 0.0), axis=0, keepdims=True)
+    place = owner * SLOTS + rank.astype(jnp.int32)
+    place_ref[...] = place
+    over = jnp.max(jnp.where(rank >= SLOTS, 1.0, 0.0), axis=1, keepdims=True)
+    u, gamma, norm = point_start(pidx_ref, jp_ref, res_ref, pb_ref, pd_ref)
+    pu_ref[0:1, :] = u[0]
+    pu_ref[1:2, :] = u[1]
+    sc_ref[...] = lanes(jnp.concatenate([gamma, norm, over], axis=0), HALF)
+    low = low_lanes(16)
+    for h in range(n_grp):
+        cols = slice(h * slot, (h + 1) * slot)
+        rows = []
+        for a in range(2):
+            rows += [
+                jc_ref[9 * a : 9 * a + 8, cols],
+                jc_ref[9 * a + 8 : 9 * a + 9, cols],
+                res_ref[a : a + 1, cols],
+                u[a][:, cols],
+                local[:, cols],
+                jnp.zeros((4, slot), F32),
+            ]
+        hot = one_hot_rows(place[:, cols], n_tile * SLOTS)
+        moved = thirds(dot_nt(three_parts(jnp.concatenate(rows, axis=0)), hot))
+        for k in range(n_tile // 2):
+            first = moved[0:16, k * HALF : (k + 1) * HALF]
+            second = moved[16:32, k * HALF : (k + 1) * HALF]
+            for t, block in (
+                (2 * k, jnp.where(low, first, swap_lanes(second))),
+                (2 * k + 1, jnp.where(low, swap_lanes(first), second)),
+            ):
+                for part in range(3):
+                    out_ref[3 * (h * n_tile + t) + part] = block[4 * part : 4 * part + 4]
+
+
+def read_routed(ref, sources):
+    main = jnp.concatenate([jnp.concatenate([ref[3 * s], ref[3 * s + 1]], axis=0) for s in sources], axis=1)
+    rest = jnp.concatenate([ref[3 * s + 2] for s in sources], axis=1)
+    index = rest[3:4].astype(jnp.int32)
+    return main, rest[0:1], rest[1:2], rest[2:3], index >> 7, one_hot_rows(index & 127, 128)
+
+
+OWN_COUNT = 4
+OWN_TAIL = 16
+OWN_ROWS = 8 * OWN_COUNT + OWN_TAIL
+
+
+def owner_kernel(in_ref, sc_ref, back_ref, tb_ref, td_ref, ts_ref, acc_ref, zz_ref):
+    devices = back_ref.shape[0]
+    per = min(32, devices)
+    steps = devices // per
+    acc_ref[...] = jnp.zeros(acc_ref.shape, F32)
+
+    def loop(body, start):
+        if steps == 1:
+            return body(0, start)
+        return lax.fori_loop(0, steps, body, start)
+
+    def rhs_and_diag(step, carry):
+        j, j8, r, _, hi, hot = read_routed(in_ref, chunk_of(step, per))
+        acc_ref[...] += scatter_mixed(hi, hot, [-(j * r), j * j], [-(j8 * r), j8 * j8], OWN_COUNT, OWN_TAIL)
+        return carry
+
+    loop(rhs_and_diag, 0)
+    sums = both(acc_ref[...])
+    main = 8 * OWN_COUNT
+    for k in range(OWN_COUNT):
+        tb_ref[8 * k : 8 * k + 8, :] = sums[16 * k : 16 * k + 8]
+        td_ref[8 * k : 8 * k + 8, :] = sums[16 * k + 8 : 16 * k + 16] + DAMPING
+    tb_ref[main:, :] = sums[2 * main : 2 * main + OWN_TAIL]
+    td_ref[main:, :] = sums[2 * main + OWN_TAIL :] + DAMPING
+    z = tb_ref[...] / td_ref[...]
+    zz_ref[...] = stacked(z)
+    acc_ref[0 : 2 * OWN_ROWS, :] = jnp.zeros((2 * OWN_ROWS, 128), F32)
+
+    def apply(step, energy):
+        sources = chunk_of(step, per)
+        j, j8, _, u, hi, hot = read_routed(in_ref, sources)
+        at, at8 = gather_mixed(hi, hot, zz_ref[...], OWN_COUNT, OWN_TAIL)
+        w = jnp.sum(j * at, axis=0, keepdims=True) + j8 * at8
+        for k, s in enumerate(sources):
+            back_ref[s, 0:1, :] = w[:, k * HALF : (k + 1) * HALF]
+        e = u + w
+        acc_ref[0 : 2 * OWN_ROWS, :] += scatter_mixed(hi, hot, [j * e], [j8 * e], OWN_COUNT, OWN_TAIL)
+        return energy + e * e
+
+    energy = loop(apply, jnp.zeros((1, per * HALF), F32))
+    ts_ref[...] = z + both(acc_ref[0 : 2 * OWN_ROWS, :])
+    zz_ref[...] = stacked(ts_ref[...] / td_ref[...])
+
+    def gather_again(step, carry):
+        sources = chunk_of(step, per)
+        j, j8, _, _, hi, hot = read_routed(in_ref, sources)
+        at, at8 = gather_mixed(hi, hot, zz_ref[...], OWN_COUNT, OWN_TAIL)
+        v = jnp.sum(j * at, axis=0, keepdims=True) + j8 * at8
+        for k, s in enumerate(sources):
+            back_ref[s, 1:2, :] = v[:, k * HALF : (k + 1) * HALF]
+        return carry
+
+    loop(gather_again, 0)
+    gamma = sc_ref[0:1, :] + total_of(tb_ref[...] * z)
+    delta = sc_ref[1:2, :] + total_of(z * z) + total_of(energy)
+    tail = jnp.concatenate([jnp.where(low_lanes(1), gamma, sc_ref[2:3, :]), delta], axis=0)
+    back_ref[:, 2:4, :] = jnp.broadcast_to(tail[None], (devices, 2, HALF))
+
+
+def routed_point_kernel(
+    n_grp, n_tile, back_ref, jp_ref, pidx_ref, place_ref, pb_ref, pd_ref, pu_ref, cb_ref, cd_ref, cs_ref,
+    out_ref, ps_ref, pe_ref, sc_ref, over_ref,
+):
+    slot = place_ref.shape[1] // n_grp
+    index = pidx_ref[...]
+    mask = is_row(index >> LO_BITS, PH)
+    hot = one_hot_rows(index & (LO - 1), LO)
+    jp = [jp_ref[k : k + 1, :] for k in range(6)]
+    scalars = jnp.sum(back_ref[...], axis=0)
+    gamma, delta = scalars[2:3, 0:1], scalars[3:4, 0:1]
+    over_ref[...] = lanes(scalars[2:3, SLOTS : SLOTS + 1], HALF)
+    alpha = gamma / delta
+    low = low_lanes(4)
+    places = [one_hot_rows(place_ref[:, h * slot : (h + 1) * slot], n_tile * SLOTS) for h in range(n_grp)]
+    terms = []
+    for h in range(n_grp):
+        first, second = [], []
+        for k in range(n_tile // 2):
+            even, odd = back_ref[h * n_tile + 2 * k], back_ref[h * n_tile + 2 * k + 1]
+            first.append(jnp.where(low, even, swap_lanes(odd)))
+            second.append(jnp.where(low, swap_lanes(even), odd))
+        both_rows = jnp.concatenate(
+            [jnp.concatenate(first, axis=1), jnp.concatenate(second, axis=1)], axis=0
+        )
+        terms.append(thirds(dot_nn(three_parts(both_rows), places[h])))
+    terms = jnp.concatenate(terms, axis=1)
+    w0 = [terms[4 * a : 4 * a + 1] for a in range(2)]
+    w1 = [terms[4 * a + 1 : 4 * a + 2] for a in range(2)]
+    rhs, diag = pb_ref[...], pd_ref[...]
+    z = rhs / diag
+    error = [pu_ref[a : a + 1, :] + w0[a] for a in range(2)]
+    s = z + scatter_points(mask, hot, [jp[i] * error[0] + jp[3 + i] * error[1] for i in range(3)])
+    r1 = rhs - alpha * s
+    z1 = r1 / diag
+    at = gather_points(mask, hot, z1)
+    error = [sum(jp[3 * a + i] * at[i] for i in range(3)) + (w0[a] - alpha * w1[a]) for a in range(2)]
+    ps_ref[...] = s
+    pe_ref[0:1, :] = error[0]
+    pe_ref[1:2, :] = error[1]
+    cr1 = cb_ref[...] - alpha * cs_ref[...]
+    cz1 = cr1 / cd_ref[...]
+    gamma1 = total_of(r1 * z1) + total_of(cr1 * cz1)
+    delta1 = (
+        total_of(error[0] * error[0] + error[1] * error[1]) + total_of(z1 * z1) + total_of(cz1 * cz1)
+    )
+    sc_ref[...] = lanes(jnp.concatenate([gamma, alpha], axis=0), HALF)
+    tail = jnp.where(low_lanes(1), gamma1, delta1)
+    low = low_lanes(8)
+    for h in range(n_grp):
+        rows = [jnp.broadcast_to(e[:, h * slot : (h + 1) * slot], (8, slot)) for e in error]
+        moved = thirds(dot_nt(three_parts(jnp.concatenate(rows, axis=0)), places[h]))
+        for k in range(n_tile // 2):
+            first = moved[0:8, k * HALF : (k + 1) * HALF]
+            second = moved[8:16, k * HALF : (k + 1) * HALF]
+            out_ref[h * n_tile + 2 * k, 0:1, :] = jnp.where(low, first, swap_lanes(second))[0:1]
+            out_ref[h * n_tile + 2 * k + 1, 0:1, :] = jnp.where(low, swap_lanes(first), second)[0:1]
+    out_ref[:, 1:2, :] = jnp.broadcast_to(tail[None], (n_grp * n_tile, 1, HALF))
+
+
+def point_results(alpha, alpha1, ratio, pb_ref, pd_ref, ps_ref, pt_ref, px_ref, pr_ref):
+    rhs, diag, s = pb_ref[...], pd_ref[...], ps_ref[...]
+    z = rhs / diag
+    r1 = rhs - alpha * s
+    z1 = r1 / diag
+    x = alpha * z + alpha1 * (z1 + ratio * z)
+    r2 = r1 - alpha1 * (z1 + pt_ref[...] + ratio * s)
+    for i in range(3):
+        for hi in range(PH):
+            row = i * PH + hi
+            px_ref[i : i + 1, hi * LO : (hi + 1) * LO] = x[row : row + 1]
+            pr_ref[i : i + 1, hi * LO : (hi + 1) * LO] = r2[row : row + 1]
+
+
+def routed_final_kernel(
+    err_ref, in_ref, pb_ref, pd_ref, ps_ref, pt_ref, cb_ref, cd_ref, cs_ref, sc_ref,
+    px_ref, cx_ref, pr_ref, cr_ref, acc_ref,
+):
+    devices = err_ref.shape[0]
+    per = min(32, devices)
+    steps = devices // per
+    acc_ref[...] = jnp.zeros(acc_ref.shape, F32)
+
+    def body(step, carry):
+        sources = chunk_of(step, per)
+        j, j8, _, _, hi, hot = read_routed(in_ref, sources)
+        e = jnp.concatenate([err_ref[s, 0:1, :] for s in sources], axis=1)
+        acc_ref[...] += scatter_mixed(hi, hot, [j * e], [j8 * e], OWN_COUNT, OWN_TAIL)
+        return carry
+
+    if steps == 1:
+        body(0, 0)
+    else:
+        lax.fori_loop(0, steps, body, 0)
+    scalars = jnp.sum(err_ref[...], axis=0)
+    gamma1, delta1 = scalars[1:2, 0:1], scalars[1:2, SLOTS : SLOTS + 1]
+    gamma, alpha = sc_ref[0:1, 0:1], sc_ref[1:2, 0:1]
+    ratio = gamma1 / gamma
+    alpha1 = gamma1 / (delta1 - ratio * gamma1 / alpha)
+    point_results(alpha, alpha1, ratio, pb_ref, pd_ref, ps_ref, pt_ref, px_ref, pr_ref)
+    rhs, s = cb_ref[...], cs_ref[...]
+    z = rhs / cd_ref[...]
+    r1 = rhs - alpha * s
+    z1 = r1 / cd_ref[...]
+    x = alpha * z + alpha1 * (z1 + ratio * z)
+    r2 = r1 - alpha1 * (z1 + both(acc_ref[...]) + ratio * s)
+    for table, target in ((x, cx_ref), (r2, cr_ref)):
+        for k in range(CAM_DEV // 128):
+            cols = slice(k * 128, (k + 1) * 128)
+            target[0:8, cols] = table[8 * k : 8 * k + 8]
+            row = 8 * OWN_COUNT + k
+            target[8:9, cols] = table[row : row + 1]
+
+
+def shards(jac_point, jac_cam, resid, point_index, cam_index):
+    n_grp, n_tile = lax.axis_size("grp"), lax.axis_size("tile")
+    devices = n_grp * n_tile
+    obs = jac_point.shape[1]
+    pidx, cidx = point_index.reshape(1, obs), cam_index.reshape(1, obs)
+    hbm = pl.BlockSpec(memory_space=pltpu.HBM)
+    ints = jax.ShapeDtypeStruct((1, obs), jnp.int32)
+    points = shape(3 * PH, LO)
+    cameras = shape(OWN_ROWS, 128)
+    routed, pb, pd, pu, jp, pidx_here, place, sc = pl.pallas_call(
+        functools.partial(route_kernel, n_grp, n_tile),
+        in_specs=[hbm] * 5,
+        out_shape=(shape(3 * devices, 4, HALF), points, points, shape(2, obs), shape(6, obs), ints, ints, shape(3, HALF)),
+        scratch_shapes=[
+            pltpu.VMEM((18, obs), F32),
+            pltpu.VMEM((2, obs), F32),
+            pltpu.VMEM((1, obs), jnp.int32),
+            pltpu.SemaphoreType.DMA((5,)),
+        ],
+        compiler_params=PARAMS,
+        name="route",
+    )(*(pltpu.with_memory_space_constraint(x, pltpu.HBM) for x in (jac_point, jac_cam, resid, pidx, cidx)))
+    routed = lax.all_to_all(routed, ("grp", "tile"), 0, 0, tiled=True)
+    back, tb, td, ts = pl.pallas_call(
+        owner_kernel,
+        out_shape=(shape(devices, 4, HALF), cameras, cameras, cameras),
+        scratch_shapes=[
+            pltpu.VMEM((4 * OWN_ROWS, 128), F32),
+            pltpu.VMEM((2 * OWN_ROWS, 128), BF16),
+        ],
+        compiler_params=PARAMS,
+        name="owner",
+    )(routed, sc)
+    back = lax.all_to_all(back, ("grp", "tile"), 0, 0, tiled=True)
+    errors, ps, pe, sc, over = pl.pallas_call(
+        functools.partial(routed_point_kernel, n_grp, n_tile),
+        out_shape=(shape(devices, 2, HALF), points, shape(2, obs), shape(2, HALF), shape(1, HALF)),
+        compiler_params=PARAMS,
+        name="points",
+    )(back, jp, pidx_here, place, pb, pd, pu, tb, td, ts)
+    errors = lax.all_to_all(errors, ("grp", "tile"), 0, 0, tiled=True)
+    pt = pl.pallas_call(
+        last_point_sums_kernel,
+        out_shape=points,
+        compiler_params=PARAMS,
+        name="last_point_sums",
+    )(jp, pidx_here, pe)
+    outputs = (shape(3, P_DEV), shape(9, CAM_DEV), shape(3, P_DEV), shape(9, CAM_DEV))
+
+    def fits(*operands):
+        return pl.pallas_call(
+            routed_final_kernel,
+            out_shape=outputs,
+            scratch_shapes=[pltpu.VMEM((2 * OWN_ROWS, 128), F32)],
+            compiler_params=PARAMS,
+            name="finish",
+        )(*operands[5:])
+
+    def overflows(*operands):
+        return tuple(replicated(*operands[:5]))
+
+    return lax.cond(
+        over[0, 0] > 0,
+        overflows,
+        lambda *operands: tuple(fits(*operands)),
+        jac_point, jac_cam, resid, point_index, cam_index,
+        errors, routed, pb, pd, ps, pt, tb, td, ts, sc,
+    )
+
+
 def solution(mesh):
     placed = (
         P(None, ("grp", "tile")),

time: 53.1 us -> 44.3 us (0.83)
  waiting for transfers between devices: 12.7 us -> 6.9 us
  blocking collectives: 21.5 us -> 25.8 us
  Pallas kernels: 12.1 us -> 8.1 us
  starting transfers between devices: 5.83 us -> 2.57 us
    all_to_all x1 -> x0, waiting for transfers between devices: 4.66 us -> none  [shards(): back = lax.all_to_all(back, 'grp', 0, 0, tiled=True)]
    all_to_all x1 -> x2, blocking collectives: 21.5 us -> 25.8 us  [the longest x1 15.9 us: shards(): routed = lax.all_to_all(routed, ('grp', 'tile'), 0, 0, tiled=True)]
    pallas_call x7 -> x5, Pallas kernels: 12.1 us -> 8.1 us  [the longest x1 2.37 us: shards(): pl.pallas_call(owner_kernel, out_shape=(shape(devices, 4, HALF), cameras,...]
    all_to_all x1 -> x0, starting transfers between devices: 3.26 us -> none  [shards(): back = lax.all_to_all(back, 'grp', 0, 0, tiled=True)]
    all_to_all x1, waiting for transfers between devices: 7.48 us -> 6.9 us  [shards(): errors = lax.all_to_all(errors, ('grp', 'tile'), 0, 0, tiled=True)]
    ppermute x1 -> x0, waiting for transfers between devices: 0.56 us -> none  [shards(): other = lax.ppermute(own, 'tile', swap)]
  transfers between devices with their start and end apart: 3 -> 1, of which waited for: 3 -> 1; matrix products, arithmetic and copies ran while one was open for 0% -> 0% of each run, Pallas kernels for 3% -> 1%
where the time goes in v3:
time: 44.3 us; the launch traced here: 44 us
  blocking collectives  25.8 us (58%)
  Pallas kernels  8.1 us (18%)
  waiting for transfers between devices  6.9 us (16%)
  starting transfers between devices  2.57 us (6%)
  between operations  0.7 us (2%)
    all_to_all x1, blocking collectives, shards(): routed = lax.all_to_all(routed, ('grp', 'tile'), 0, 0, tiled=True)  15.9 us
    all_to_all x1, blocking collectives, shards(): back = lax.all_to_all(back, ('grp', 'tile'), 0, 0, tiled=True)  9.92 us
    all_to_all x1, waiting for transfers between devices, shards(): errors = lax.all_to_all(errors, ('grp', 'tile'), 0, 0, tiled=True)  6.9 us
    all_to_all x1, starting transfers between devices, shards(): errors = lax.all_to_all(errors, ('grp', 'tile'), 0, 0, tiled=True)  2.57 us
    pallas_call x1, Pallas kernels, shards(): pl.pallas_call(owner_kernel, out_shape=(shape(devices, 4, HALF), cameras,...  2.37 us
    pallas_call x1, Pallas kernels, shards(): pl.pallas_call(functools.partial(route_kernel, n_grp, n_tile), in_specs=[...  2.22 us
    pallas_call x1, Pallas kernels, shards(): pl.pallas_call(functools.partial(routed_point_kernel, n_grp, n_tile), out...  2.07 us
    pallas_call x1, Pallas kernels, fits(): pl.pallas_call(routed_final_kernel, out_shape=outputs, scratch_shapes=[pl...  1.14 us
  transfers between devices with their start and end apart: 1, of which 1 were waited for; matrix products, arithmetic and copies ran while one was open for 0% of the time, Pallas kernels for 1%

profile of v3, /device:TPU:0, one launch (start us, length us, event | category | flops | bytes accessed | tf_op | source)
XLA Modules:
  0.0 44.0 jit_solution(11992084485248657881)
XLA Ops:
  0.6 2.2 %route.1 = (f32[96,4,128]{2,1,0:T(4,128)S(1)}, f32[48,256]{1,0:T(8,128)S(1)}, f32[48,256]{1,0:T(8,128)S(1)}, f32[2,1024]{1,0:T(2,128)S(1)}, f32[6,1024]{1,0:T(8,...) custom-call(f32[6,1024]{1,0:T(8,128)} %jp_hbm.1, f32[18,1024]{1,0:T(8,128)} %jc_hbm.1, ...), custom_call_target="tpu_custom_call" | custom-call | tf_op jit(solution)/shard_map/route/pallas_call | solution.py:850
  2.9 15.9 %all_to_all.28.in_ref = f32[96,4,128]{2,1,0:T(4,128)S(1)} all-to-all(f32[96,4,128]{2,1,0:T(4,128)S(1)} %get-tuple-element.83), channel_id=1, replica_groups=mesh['grp'=4,'tile'=8] {'grp','tile'}, dimensions={0} | all-to-all | bytes 393216 | tf_op jit(solution)/shard_map/all_to_all | solution.py:863
  18.7 2.4 %owner.1 = (f32[32,4,128]{2,1,0:T(4,128)S(1)}, f32[48,128]{1,0:T(8,128)S(1)}, f32[48,128]{1,0:T(8,128)S(1)}, f32[48,128]{1,0:T(8,128)S(1)}) custom-call(f32[96,4,128]{2,1,0:T(4,128)S(1)} %all_to_all.28.in_ref, f32[3,128]{1,0:T(4,128)S(1)} %get-tuple-element.84.sc_ref), custom_call_target="tpu_custom_call" | custom-call | tf_op jit(solution)/shard_map/owner/pallas_call | solution.py:864
  21.1 9.9 %all_to_all.29.back_ref = f32[32,4,128]{2,1,0:T(4,128)S(1)} all-to-all(f32[32,4,128]{2,1,0:T(4,128)S(1)} %get-tuple-element.85), channel_id=1, replica_groups=mesh['grp'=4,'tile'=8] {'grp','tile'}, dimensions={0} | all-to-all | bytes 131072 | tf_op jit(solution)/shard_map/all_to_all | solution.py:874
  31.0 2.1 %points.3 = (f32[32,2,128]{2,1,0:T(2,128)}, f32[48,256]{1,0:T(8,128)S(1)}, f32[2,1024]{1,0:T(2,128)S(1)}, f32[2,128]{1,0:T(2,128)S(1)}, f32[1,128]{1,0:T(1,128)S(1)}) custom-call(f32[32,4,128]{2,1,0:T(4,128)S(1)} %all_to_all.29.back_ref, f32[6,1024]{1,0:T(8,128)S(1)} %get-tuple-element.86.jp_ref, s32[1,1024]{1,0:T(1,128)S(1)} %get-tuple-element.87.pidx_ref, ...), custom_call_target="tpu_custom_call" | custom-call | tf_op jit(solution)/shard_map/points/pallas_call | solution.py:875
  33.1 2.6 %all-to-all-start.5 = ((f32[32,2,128]{2,1,0:T(2,128)}), f32[32,2,128]{2,1,0:T(2,128)S(1)}, u32[]{:S(2)}, u32[]{:S(2)}) async-start(f32[32,2,128]{2,1,0:T(2,128)} %get-tuple-element.96), calls=%async_computation.5 | async-start | bytes 65536 | tf_op jit(solution)/shard_map/all_to_all | solution.py:881
  35.7 0.3 last_point_sums.3
  36.0 6.9 %all-to-all-done.5 = f32[32,2,128]{2,1,0:T(2,128)S(1)} async-done(((f32[32,2,128]{2,1,0:T(2,128)}), f32[32,2,128]{2,1,0:T(2,128)S(1)}, u32[]{:S(2)}, u32[]{:S(2)}) %all-to-all-start.5) | async-done | bytes 32800 | tf_op jit(solution)/shard_map/all_to_all | solution.py:881
  42.9 1.1 %conditional.1 = ((f32[3,4096]{1,0:T(4,128)}, f32[9,384]{1,0:T(8,128)}, f32[3,4096]{1,0:T(4,128)}, f32[9,384]{1,0:T(8,128)})) conditional(s32[]{:T(128)} %bitcast.4, (f32[32,2,128]{2,1,0:T(2,128)S(1)}, f32[96,4,128]{2,1,0:T(4,128)S(1)}, f32[48,256]{1,0:T(8,128)S(1)}, f32[48,256]{1,0:T(8,128)S(1)}, f32[48,256]{1,0:T(8,128)S(1)}, ...), branch_computations={%region_0.0_spmd, %region_1.0_spmd} | conditional | flops 2000000000 | bytes 3728048 | solution.py:902
  42.9 1.1 %finish.2 = (f32[3,4096]{1,0:T(4,128)}, f32[9,384]{1,0:T(8,128)}, f32[3,4096]{1,0:T(4,128)}, f32[9,384]{1,0:T(8,128)}) custom-call(f32[32,2,128]{2,1,0:T(2,128)S(1)} %get-tuple-element.30.err_ref, f32[96,4,128]{2,1,0:T(4,128)S(1)} %get-tuple-element.31.in_ref, f32[48,256]{1,0:T(8,128)S(1)} %get-tuple-element.32.pb_ref, ...), custom_call_target="tpu_custom_call" | custom-call | tf_op jit(solution)/shard_map/cond/branch_0_fun/finish/pallas_call | solution.py:891
Async XLA Ops:
  33.1 9.8 %all-to-all-start.5 = ((f32[32,2,128]{2,1,0:T(2,128)}), f32[32,2,128]{2,1,0:T(2,128)S(1)}, u32[]{:S(2)}, u32[]{:S(2)}) async-start(f32[32,2,128]{2,1,0:T(2,128)} %get-tuple-element.96), calls=%async_computation.5 | async-start | bytes 65536 | tf_op jit(solution)/shard_map/all_to_all | solution.py:881

commit v4 on v3

--- a/solution.py
+++ b/solution.py
@@ -653,75 +653,127 @@
                     out_ref[3 * (h * n_tile + t) + part] = block[4 * part : 4 * part + 4]
 
 
+def unfold(even, odd):
+    low = low_lanes(even.shape[0])
+    return jnp.where(low, even, swap_lanes(odd)), jnp.where(low, swap_lanes(even), odd)
+
+
+def side_by_side(even, odd):
+    return jnp.where(low_lanes(even.shape[0]), even, swap_lanes(odd))
+
+
 def read_routed(ref, sources):
-    main = jnp.concatenate([jnp.concatenate([ref[3 * s], ref[3 * s + 1]], axis=0) for s in sources], axis=1)
-    rest = jnp.concatenate([ref[3 * s + 2] for s in sources], axis=1)
-    index = rest[3:4].astype(jnp.int32)
-    return main, rest[0:1], rest[1:2], rest[2:3], index >> 7, one_hot_rows(index & 127, 128)
-
-
-OWN_COUNT = 4
-OWN_TAIL = 16
-OWN_ROWS = 8 * OWN_COUNT + OWN_TAIL
-
-
-def owner_kernel(in_ref, sc_ref, back_ref, tb_ref, td_ref, ts_ref, acc_ref, zz_ref):
+    main, rest = ([], []), ([], [])
+    for s, t in zip(sources[::2], sources[1::2]):
+        pair = unfold(*(jnp.concatenate([ref[3 * k], ref[3 * k + 1]], axis=0) for k in (s, t)))
+        pair_rest = unfold(ref[3 * s + 2], ref[3 * t + 2])
+        for a in range(2):
+            main[a].append(pair[a])
+            rest[a].append(pair_rest[a])
+    main = [jnp.concatenate(v, axis=1) for v in main]
+    rest = [jnp.concatenate(v, axis=1) for v in rest]
+    return main, rest, one_hot_rows(rest[0][3:4].astype(jnp.int32), CAM_DEV)
+
+
+def padded(main, tail):
+    below = lax.broadcasted_iota(jnp.int32, main.shape, 0) == 0
+    return jnp.concatenate([main, jnp.where(below, jnp.broadcast_to(tail, main.shape), 0.0)], axis=0)
+
+
+def scatter_own(hot, values):
+    return both(dot_nt(stacked(values), hot))
+
+
+def gather_own(hot, table, main, rest):
+    at = both(dot_nn(table, hot))
+    return [
+        jnp.sum(main[a] * at[0:8], axis=0, keepdims=True) + rest[a][0:1] * at[8:9] for a in range(2)
+    ]
+
+
+def transposed_j(main, rest, e):
+    return padded(main[0] * e[0] + main[1] * e[1], rest[0][0:1] * e[0] + rest[1][0:1] * e[1])
+
+
+OWN_ROWS = 16
+STEP = 32
+
+
+def owner_kernel(in_ref, sc_ref, back_ref, tb_ref, td_ref, ts_ref, acc_ref, zz_ref, w_ref, *kept):
     devices = back_ref.shape[0]
-    per = min(32, devices)
+    per = min(STEP, devices)
     steps = devices // per
+
+    if steps == 1:
+        main, rest, hot = read_routed(in_ref, range(devices))
+        kept[0][...] = hot
+        for a in range(2):
+            kept[1][8 * a : 8 * a + 8, :] = main[a]
+            kept[1][16 + a : 17 + a, :] = rest[a][0:1]
+
+        def loop(body, start):
+            return body((main, rest, hot), 0, start)
+    else:
+
+        def loop(body, start):
+            def step(number, carry):
+                return body(read_routed(in_ref, chunk_of(number, per)), number, carry)
+
+            return lax.fori_loop(0, steps, step, start)
+
+    def rhs_and_diag(slots, number, carry):
+        main, rest, hot = slots
+        r = [rest[a][1:2] for a in range(2)]
+        rhs = padded(
+            -(main[0] * r[0] + main[1] * r[1]), -(rest[0][0:1] * r[0] + rest[1][0:1] * r[1])
+        )
+        square = padded(
+            main[0] * main[0] + main[1] * main[1],
+            rest[0][0:1] * rest[0][0:1] + rest[1][0:1] * rest[1][0:1],
+        )
+        acc_ref[...] += scatter_own(hot, jnp.concatenate([rhs, square], axis=0))
+        return carry
+
     acc_ref[...] = jnp.zeros(acc_ref.shape, F32)
-
-    def loop(body, start):
-        if steps == 1:
-            return body(0, start)
-        return lax.fori_loop(0, steps, body, start)
-
-    def rhs_and_diag(step, carry):
-        j, j8, r, _, hi, hot = read_routed(in_ref, chunk_of(step, per))
-        acc_ref[...] += scatter_mixed(hi, hot, [-(j * r), j * j], [-(j8 * r), j8 * j8], OWN_COUNT, OWN_TAIL)
+    loop(rhs_and_diag, 0)
+    rhs, diag = acc_ref[0:OWN_ROWS, :], acc_ref[OWN_ROWS:, :] + DAMPING
+    tb_ref[...] = rhs
+    td_ref[...] = diag
+    z = rhs / diag
+    zz_ref[...] = stacked(z)
+    acc_ref[0:OWN_ROWS, :] = z
+
+    def apply(slots, number, energy):
+        main, rest, hot = slots
+        w = gather_own(hot, zz_ref[...], main, rest)
+        e = [rest[a][2:3] + w[a] for a in range(2)]
+        for a in range(2):
+            w_ref[number, a : a + 1, :] = w[a]
+        acc_ref[0:OWN_ROWS, :] += scatter_own(hot, transposed_j(main, rest, e))
+        return energy + e[0] * e[0] + e[1] * e[1]
+
+    energy = loop(apply, jnp.zeros((1, per * SLOTS), F32))
+    s = acc_ref[0:OWN_ROWS, :]
+    ts_ref[...] = s
+    zz_ref[...] = stacked(s / diag)
+    gamma = sc_ref[0:1, :] + total_of(rhs * z)
+    delta = sc_ref[1:2, :] + total_of(z * z) + total_of(energy)
+    tail = jnp.concatenate([gamma, delta, sc_ref[2:3, :], sc_ref[2:3, :]], axis=0)
+
+    def send(slots, number, carry):
+        main, rest, hot = slots
+        v = gather_own(hot, zz_ref[...], main, rest)
+        for a in range(2):
+            w_ref[number, 2 + a : 3 + a, :] = v[a]
+        w = w_ref[number]
+        low = low_lanes(4)
+        for k in range(per // 2):
+            pair = w[:, k * HALF : (k + 1) * HALF]
+            back_ref[number * per + 2 * k] = jnp.where(low, pair, tail)
+            back_ref[number * per + 2 * k + 1] = jnp.where(low, swap_lanes(pair), tail)
         return carry
 
-    loop(rhs_and_diag, 0)
-    sums = both(acc_ref[...])
-    main = 8 * OWN_COUNT
-    for k in range(OWN_COUNT):
-        tb_ref[8 * k : 8 * k + 8, :] = sums[16 * k : 16 * k + 8]
-        td_ref[8 * k : 8 * k + 8, :] = sums[16 * k + 8 : 16 * k + 16] + DAMPING
-    tb_ref[main:, :] = sums[2 * main : 2 * main + OWN_TAIL]
-    td_ref[main:, :] = sums[2 * main + OWN_TAIL :] + DAMPING
-    z = tb_ref[...] / td_ref[...]
-    zz_ref[...] = stacked(z)
-    acc_ref[0 : 2 * OWN_ROWS, :] = jnp.zeros((2 * OWN_ROWS, 128), F32)
-
-    def apply(step, energy):
-        sources = chunk_of(step, per)
-        j, j8, _, u, hi, hot = read_routed(in_ref, sources)
-        at, at8 = gather_mixed(hi, hot, zz_ref[...], OWN_COUNT, OWN_TAIL)
-        w = jnp.sum(j * at, axis=0, keepdims=True) + j8 * at8
-        for k, s in enumerate(sources):
-            back_ref[s, 0:1, :] = w[:, k * HALF : (k + 1) * HALF]
-        e = u + w
-        acc_ref[0 : 2 * OWN_ROWS, :] += scatter_mixed(hi, hot, [j * e], [j8 * e], OWN_COUNT, OWN_TAIL)
-        return energy + e * e
-
-    energy = loop(apply, jnp.zeros((1, per * HALF), F32))
-    ts_ref[...] = z + both(acc_ref[0 : 2 * OWN_ROWS, :])
-    zz_ref[...] = stacked(ts_ref[...] / td_ref[...])
-
-    def gather_again(step, carry):
-        sources = chunk_of(step, per)
-        j, j8, _, _, hi, hot = read_routed(in_ref, sources)
-        at, at8 = gather_mixed(hi, hot, zz_ref[...], OWN_COUNT, OWN_TAIL)
-        v = jnp.sum(j * at, axis=0, keepdims=True) + j8 * at8
-        for k, s in enumerate(sources):
-            back_ref[s, 1:2, :] = v[:, k * HALF : (k + 1) * HALF]
-        return carry
-
-    loop(gather_again, 0)
-    gamma = sc_ref[0:1, :] + total_of(tb_ref[...] * z)
-    delta = sc_ref[1:2, :] + total_of(z * z) + total_of(energy)
-    tail = jnp.concatenate([jnp.where(low_lanes(1), gamma, sc_ref[2:3, :]), delta], axis=0)
-    back_ref[:, 2:4, :] = jnp.broadcast_to(tail[None], (devices, 2, HALF))
+    loop(send, 0)
 
 
 def routed_point_kernel(
@@ -733,26 +785,19 @@
     mask = is_row(index >> LO_BITS, PH)
     hot = one_hot_rows(index & (LO - 1), LO)
     jp = [jp_ref[k : k + 1, :] for k in range(6)]
-    scalars = jnp.sum(back_ref[...], axis=0)
-    gamma, delta = scalars[2:3, 0:1], scalars[3:4, 0:1]
-    over_ref[...] = lanes(scalars[2:3, SLOTS : SLOTS + 1], HALF)
+    scalars = jnp.sum(back_ref[...], axis=0)[:, SLOTS : SLOTS + 1]
+    gamma, delta = scalars[0:1], scalars[1:2]
+    over_ref[...] = lanes(scalars[2:3], HALF)
     alpha = gamma / delta
-    low = low_lanes(4)
     places = [one_hot_rows(place_ref[:, h * slot : (h + 1) * slot], n_tile * SLOTS) for h in range(n_grp)]
     terms = []
     for h in range(n_grp):
-        first, second = [], []
-        for k in range(n_tile // 2):
-            even, odd = back_ref[h * n_tile + 2 * k], back_ref[h * n_tile + 2 * k + 1]
-            first.append(jnp.where(low, even, swap_lanes(odd)))
-            second.append(jnp.where(low, swap_lanes(even), odd))
-        both_rows = jnp.concatenate(
-            [jnp.concatenate(first, axis=1), jnp.concatenate(second, axis=1)], axis=0
-        )
-        terms.append(thirds(dot_nn(three_parts(both_rows), places[h])))
+        pairs = range(h * n_tile, (h + 1) * n_tile, 2)
+        rows = jnp.concatenate([side_by_side(back_ref[k], back_ref[k + 1]) for k in pairs], axis=1)
+        terms.append(thirds(dot_nn(three_parts(rows), places[h])))
     terms = jnp.concatenate(terms, axis=1)
-    w0 = [terms[4 * a : 4 * a + 1] for a in range(2)]
-    w1 = [terms[4 * a + 1 : 4 * a + 2] for a in range(2)]
+    w0 = [terms[a : a + 1] for a in range(2)]
+    w1 = [terms[2 + a : 3 + a] for a in range(2)]
     rhs, diag = pb_ref[...], pd_ref[...]
     z = rhs / diag
     error = [pu_ref[a : a + 1, :] + w0[a] for a in range(2)]
@@ -771,17 +816,15 @@
         total_of(error[0] * error[0] + error[1] * error[1]) + total_of(z1 * z1) + total_of(cz1 * cz1)
     )
     sc_ref[...] = lanes(jnp.concatenate([gamma, alpha], axis=0), HALF)
-    tail = jnp.where(low_lanes(1), gamma1, delta1)
-    low = low_lanes(8)
+    tail = lanes(jnp.concatenate([gamma1, delta1], axis=0), HALF)
+    low = low_lanes(2)
     for h in range(n_grp):
-        rows = [jnp.broadcast_to(e[:, h * slot : (h + 1) * slot], (8, slot)) for e in error]
-        moved = thirds(dot_nt(three_parts(jnp.concatenate(rows, axis=0)), places[h]))
+        rows = jnp.concatenate([e[:, h * slot : (h + 1) * slot] for e in error], axis=0)
+        moved = thirds(dot_nt(three_parts(rows), places[h]))
         for k in range(n_tile // 2):
-            first = moved[0:8, k * HALF : (k + 1) * HALF]
-            second = moved[8:16, k * HALF : (k + 1) * HALF]
-            out_ref[h * n_tile + 2 * k, 0:1, :] = jnp.where(low, first, swap_lanes(second))[0:1]
-            out_ref[h * n_tile + 2 * k + 1, 0:1, :] = jnp.where(low, swap_lanes(first), second)[0:1]
-    out_ref[:, 1:2, :] = jnp.broadcast_to(tail[None], (n_grp * n_tile, 1, HALF))
+            pair = moved[:, k * HALF : (k + 1) * HALF]
+            out_ref[h * n_tile + 2 * k] = jnp.where(low, pair, tail)
+            out_ref[h * n_tile + 2 * k + 1] = jnp.where(low, swap_lanes(pair), tail)
 
 
 def point_results(alpha, alpha1, ratio, pb_ref, pd_ref, ps_ref, pt_ref, px_ref, pr_ref):
@@ -799,27 +842,34 @@
 
 
 def routed_final_kernel(
-    err_ref, in_ref, pb_ref, pd_ref, ps_ref, pt_ref, cb_ref, cd_ref, cs_ref, sc_ref,
-    px_ref, cx_ref, pr_ref, cr_ref, acc_ref,
+    err_ref, in_ref, pb_ref, pd_ref, ps_ref, pt_ref, cb_ref, cd_ref, cs_ref, sc_ref, *rest_refs
 ):
+    kept, (px_ref, cx_ref, pr_ref, cr_ref, acc_ref) = rest_refs[:-5], rest_refs[-5:]
     devices = err_ref.shape[0]
-    per = min(32, devices)
+    per = min(STEP, devices)
     steps = devices // per
-    acc_ref[...] = jnp.zeros(acc_ref.shape, F32)
 
     def body(step, carry):
         sources = chunk_of(step, per)
-        j, j8, _, _, hi, hot = read_routed(in_ref, sources)
-        e = jnp.concatenate([err_ref[s, 0:1, :] for s in sources], axis=1)
-        acc_ref[...] += scatter_mixed(hi, hot, [j * e], [j8 * e], OWN_COUNT, OWN_TAIL)
+        if kept:
+            hot, rows = kept[0][...], kept[1]
+            main = [rows[8 * a : 8 * a + 8, :] for a in range(2)]
+            rest = [rows[16 + a : 17 + a, :] for a in range(2)]
+        else:
+            main, rest, hot = read_routed(in_ref, sources)
+        e = jnp.concatenate(
+            [side_by_side(err_ref[s], err_ref[t]) for s, t in zip(sources[::2], sources[1::2])], axis=1
+        )
+        acc_ref[...] += scatter_own(hot, transposed_j(main, rest, [e[0:1], e[1:2]]))
         return carry
 
+    acc_ref[...] = jnp.zeros(acc_ref.shape, F32)
     if steps == 1:
         body(0, 0)
     else:
         lax.fori_loop(0, steps, body, 0)
     scalars = jnp.sum(err_ref[...], axis=0)
-    gamma1, delta1 = scalars[1:2, 0:1], scalars[1:2, SLOTS : SLOTS + 1]
+    gamma1, delta1 = scalars[0:1, SLOTS : SLOTS + 1], scalars[1:2, SLOTS : SLOTS + 1]
     gamma, alpha = sc_ref[0:1, 0:1], sc_ref[1:2, 0:1]
     ratio = gamma1 / gamma
     alpha1 = gamma1 / (delta1 - ratio * gamma1 / alpha)
@@ -828,14 +878,8 @@
     z = rhs / cd_ref[...]
     r1 = rhs - alpha * s
     z1 = r1 / cd_ref[...]
-    x = alpha * z + alpha1 * (z1 + ratio * z)
-    r2 = r1 - alpha1 * (z1 + both(acc_ref[...]) + ratio * s)
-    for table, target in ((x, cx_ref), (r2, cr_ref)):
-        for k in range(CAM_DEV // 128):
-            cols = slice(k * 128, (k + 1) * 128)
-            target[0:8, cols] = table[8 * k : 8 * k + 8]
-            row = 8 * OWN_COUNT + k
-            target[8:9, cols] = table[row : row + 1]
+    cx_ref[...] = (alpha * z + alpha1 * (z1 + ratio * z))[0:9]
+    cr_ref[...] = (r1 - alpha1 * (z1 + acc_ref[...] + ratio * s))[0:9]
 
 
 def shards(jac_point, jac_cam, resid, point_index, cam_index):
@@ -846,7 +890,7 @@
     hbm = pl.BlockSpec(memory_space=pltpu.HBM)
     ints = jax.ShapeDtypeStruct((1, obs), jnp.int32)
     points = shape(3 * PH, LO)
-    cameras = shape(OWN_ROWS, 128)
+    cameras = shape(OWN_ROWS, CAM_DEV)
     routed, pb, pd, pu, jp, pidx_here, place, sc = pl.pallas_call(
         functools.partial(route_kernel, n_grp, n_tile),
         in_specs=[hbm] * 5,
@@ -861,13 +905,25 @@
         name="route",
     )(*(pltpu.with_memory_space_constraint(x, pltpu.HBM) for x in (jac_point, jac_cam, resid, pidx, cidx)))
     routed = lax.all_to_all(routed, ("grp", "tile"), 0, 0, tiled=True)
-    back, tb, td, ts = pl.pallas_call(
-        owner_kernel,
-        out_shape=(shape(devices, 4, HALF), cameras, cameras, cameras),
-        scratch_shapes=[
-            pltpu.VMEM((4 * OWN_ROWS, 128), F32),
-            pltpu.VMEM((2 * OWN_ROWS, 128), BF16),
-        ],
+    slots = devices * SLOTS
+    per = min(STEP, devices)
+    scratch = [
+        pltpu.VMEM((2 * OWN_ROWS, CAM_DEV), F32),
+        pltpu.VMEM((2 * OWN_ROWS, CAM_DEV), BF16),
+        pltpu.VMEM((devices // per, 4, per * SLOTS), F32),
+    ]
+    kept_shapes = ()
+    if devices == per:
+        kept_shapes = (jax.ShapeDtypeStruct((CAM_DEV, slots), BF16), shape(24, slots))
+
+    def owner(in_ref, sc_ref, back_ref, tb_ref, td_ref, ts_ref, *others):
+        kept, work = others[: len(kept_shapes)], others[len(kept_shapes) :]
+        owner_kernel(in_ref, sc_ref, back_ref, tb_ref, td_ref, ts_ref, *work, *kept)
+
+    back, tb, td, ts, *kept = pl.pallas_call(
+        owner,
+        out_shape=(shape(devices, 4, HALF), cameras, cameras, cameras) + kept_shapes,
+        scratch_shapes=scratch,
         compiler_params=PARAMS,
         name="owner",
     )(routed, sc)
@@ -891,7 +947,7 @@
         return pl.pallas_call(
             routed_final_kernel,
             out_shape=outputs,
-            scratch_shapes=[pltpu.VMEM((2 * OWN_ROWS, 128), F32)],
+            scratch_shapes=[pltpu.VMEM((OWN_ROWS, CAM_DEV), F32)],
             compiler_params=PARAMS,
             name="finish",
         )(*operands[5:])
@@ -904,7 +960,7 @@
         overflows,
         lambda *operands: tuple(fits(*operands)),
         jac_point, jac_cam, resid, point_index, cam_index,
-        errors, routed, pb, pd, ps, pt, tb, td, ts, sc,
+        errors, routed, pb, pd, ps, pt, tb, td, ts, sc, *kept,
     )
 
 

time: 44.3 us -> 44.1 us (level)
  no operation moved by 1% of the time
where the time goes in v4:
time: 44.1 us; the launch traced here: 43.8 us
  blocking collectives  25.8 us (59%)
  Pallas kernels  7.9 us (18%)
  waiting for transfers between devices  6.9 us (16%)
  starting transfers between devices  2.57 us (6%)
  between operations  0.69 us (2%)
    all_to_all x1, blocking collectives, shards(): routed = lax.all_to_all(routed, ('grp', 'tile'), 0, 0, tiled=True)  15.9 us
    all_to_all x1, blocking collectives, shards(): back = lax.all_to_all(back, ('grp', 'tile'), 0, 0, tiled=True)  9.91 us
    all_to_all x1, waiting for transfers between devices, shards(): errors = lax.all_to_all(errors, ('grp', 'tile'), 0, 0, tiled=True)  6.9 us
    all_to_all x1, starting transfers between devices, shards(): errors = lax.all_to_all(errors, ('grp', 'tile'), 0, 0, tiled=True)  2.57 us
    pallas_call x1, Pallas kernels, shards(): pl.pallas_call(functools.partial(route_kernel, n_grp, n_tile), in_specs=[...  2.22 us
    pallas_call x1, Pallas kernels, shards(): pl.pallas_call(owner, out_shape=(shape(devices, 4, HALF), cameras, camera...  2.14 us
    pallas_call x1, Pallas kernels, shards(): pl.pallas_call(functools.partial(routed_point_kernel, n_grp, n_tile), out...  2 us
    pallas_call x1, Pallas kernels, fits(): pl.pallas_call(routed_final_kernel, out_shape=outputs, scratch_shapes=[pl...  1.25 us
  transfers between devices with their start and end apart: 1, of which 1 were waited for; matrix products, arithmetic and copies ran while one was open for 0% of the time, Pallas kernels for 1%

profile of v4, /device:TPU:0, one launch (start us, length us, event | category | flops | bytes accessed | tf_op | source)
XLA Modules:
  0.0 43.8 jit_solution(5839908196514396932)
XLA Ops:
  0.6 2.2 %route.1 = (f32[96,4,128]{2,1,0:T(4,128)S(1)}, f32[48,256]{1,0:T(8,128)S(1)}, f32[48,256]{1,0:T(8,128)S(1)}, f32[2,1024]{1,0:T(2,128)S(1)}, f32[6,1024]{1,0:T(8,...) custom-call(f32[6,1024]{1,0:T(8,128)} %jp_hbm.1, f32[18,1024]{1,0:T(8,128)} %jc_hbm.1, ...), custom_call_target="tpu_custom_call" | custom-call | tf_op jit(solution)/shard_map/route/pallas_call | solution.py:894
  2.9 15.9 %all_to_all.28.in_ref = f32[96,4,128]{2,1,0:T(4,128)S(1)} all-to-all(f32[96,4,128]{2,1,0:T(4,128)S(1)} %get-tuple-element.91), channel_id=1, replica_groups=mesh['grp'=4,'tile'=8] {'grp','tile'}, dimensions={0} | all-to-all | bytes 393216 | tf_op jit(solution)/shard_map/all_to_all | solution.py:907
  18.7 2.1 %owner.1 = (f32[32,4,128]{2,1,0:T(4,128)S(1)}, f32[16,384]{1,0:T(8,128)S(1)}, f32[16,384]{1,0:T(8,128)S(1)}, f32[16,384]{1,0:T(8,128)S(1)}, bf16[384,2048]{1,0:T(8,128)(2,1)S(1)}, /*index=5*/f32[24,2048]{1,0:T(8,128)S(1)}) custom-call(f32[96,4,128]{2,1,0:T(4,128)S(1)} %all_to_all.28.in_ref, f32[3,128]{1,0:T(4,128)S(1)} %get-tuple-element.92.sc_ref), custom_call_target="tpu_custom_call" | custom-call | tf_op jit(solution)/shard_map/owner/pallas_call | solution.py:923
  20.9 9.9 %all_to_all.29.back_ref = f32[32,4,128]{2,1,0:T(4,128)S(1)} all-to-all(f32[32,4,128]{2,1,0:T(4,128)S(1)} %get-tuple-element.93), channel_id=1, replica_groups=mesh['grp'=4,'tile'=8] {'grp','tile'}, dimensions={0} | all-to-all | bytes 131072 | tf_op jit(solution)/shard_map/all_to_all | solution.py:930
  30.8 2.0 %points.3 = (f32[32,2,128]{2,1,0:T(2,128)}, f32[48,256]{1,0:T(8,128)S(1)}, f32[2,1024]{1,0:T(2,128)S(1)}, f32[2,128]{1,0:T(2,128)S(1)}, f32[1,128]{1,0:T(1,128)S(1)}) custom-call(f32[32,4,128]{2,1,0:T(4,128)S(1)} %all_to_all.29.back_ref, f32[6,1024]{1,0:T(8,128)S(1)} %get-tuple-element.94.jp_ref, s32[1,1024]{1,0:T(1,128)S(1)} %get-tuple-element.95.pidx_ref, ...), custom_call_target="tpu_custom_call" | custom-call | tf_op jit(solution)/shard_map/points/pallas_call | solution.py:931
  32.8 2.6 %all-to-all-start.5 = ((f32[32,2,128]{2,1,0:T(2,128)}), f32[32,2,128]{2,1,0:T(2,128)S(1)}, u32[]{:S(2)}, u32[]{:S(2)}) async-start(f32[32,2,128]{2,1,0:T(2,128)} %get-tuple-element.104), calls=%async_computation.5 | async-start | bytes 65536 | tf_op jit(solution)/shard_map/all_to_all | solution.py:937
  35.4 0.3 last_point_sums.3
  35.7 6.9 %all-to-all-done.5 = f32[32,2,128]{2,1,0:T(2,128)S(1)} async-done(((f32[32,2,128]{2,1,0:T(2,128)}), f32[32,2,128]{2,1,0:T(2,128)S(1)}, u32[]{:S(2)}, u32[]{:S(2)}) %all-to-all-start.5) | async-done | bytes 32800 | tf_op jit(solution)/shard_map/all_to_all | solution.py:937
  42.6 1.2 %conditional.1 = ((f32[3,4096]{1,0:T(4,128)}, f32[9,384]{1,0:T(8,128)}, f32[3,4096]{1,0:T(4,128)}, f32[9,384]{1,0:T(8,128)})) conditional(s32[]{:T(128)} %bitcast.4, (f32[32,2,128]{2,1,0:T(2,128)S(1)}, f32[96,4,128]{2,1,0:T(4,128)S(1)}, f32[48,256]{1,0:T(8,128)S(1)}, f32[48,256]{1,0:T(8,128)S(1)}, f32[48,256]{1,0:T(8,128)S(1)}, ...), branch_computations={%region_0.0_spmd, %region_1.0_spmd} | conditional | flops 2000000000 | bytes 3728048 | solution.py:958
  42.6 1.2 %finish.2 = (f32[3,4096]{1,0:T(4,128)}, f32[9,384]{1,0:T(8,128)}, f32[3,4096]{1,0:T(4,128)}, f32[9,384]{1,0:T(8,128)}) custom-call(f32[32,2,128]{2,1,0:T(2,128)S(1)} %get-tuple-element.34.err_ref, f32[96,4,128]{2,1,0:T(4,128)S(1)} %get-tuple-element.35.in_ref, f32[48,256]{1,0:T(8,128)S(1)} %get-tuple-element.36.pb_ref, ...), custom_call_target="tpu_custom_call" | custom-call | tf_op jit(solution)/shard_map/cond/branch_0_fun/finish/pallas_call | solution.py:947
Async XLA Ops:
  32.8 9.8 %all-to-all-start.5 = ((f32[32,2,128]{2,1,0:T(2,128)}), f32[32,2,128]{2,1,0:T(2,128)S(1)}, u32[]{:S(2)}, u32[]{:S(2)}) async-start(f32[32,2,128]{2,1,0:T(2,128)} %get-tuple-element.104), calls=%async_computation.5 | async-start | bytes 65536 | tf_op jit(solution)/shard_map/all_to_all | solution.py:937

commit v5 on v4

--- a/solution.py
+++ b/solution.py
@@ -546,16 +546,21 @@
     )(errors, own, other, pb, pd, ps, pt, cb, cd, cs, sc)
 
 
-def three_parts(v):
-    high = v.astype(BF16).astype(F32)
-    rest = v - high
-    middle = rest.astype(BF16).astype(F32)
-    return jnp.concatenate([high, middle, rest - middle], axis=0).astype(BF16)
-
-
-def thirds(v):
-    rows = v.shape[0] // 3
-    return v[:rows] + v[rows : 2 * rows] + v[2 * rows :]
+def eights(row):
+    return jnp.broadcast_to(row, (8, row.shape[1]))
+
+
+def row_numbers(width):
+    return lax.broadcasted_iota(jnp.int32, (16, width), 0)
+
+
+def as_16_bit(numbers):
+    return numbers.astype(F32).astype(BF16)
+
+
+def masked_rows(parts, masks):
+    none = jnp.zeros(parts[0].shape, BF16)
+    return jnp.concatenate([jnp.where(m, p, none) for p in parts for m in masks], axis=0)
 
 
 def low_lanes(rows):
@@ -566,7 +571,7 @@
     return pltpu.roll(v, SLOTS, 1)
 
 
-def point_start(pidx_ref, jp_ref, res_ref, pb_ref, pd_ref):
+def point_sums(pidx_ref, jp_ref, res_ref):
     index = pidx_ref[...]
     mask = is_row(index >> LO_BITS, PH)
     hot = one_hot_rows(index & (LO - 1), LO)
@@ -574,15 +579,7 @@
     res = [res_ref[a : a + 1, :] for a in range(2)]
     grad = [-(jp[i] * res[0] + jp[3 + i] * res[1]) for i in range(3)]
     square = [jp[i] * jp[i] + jp[3 + i] * jp[3 + i] for i in range(3)]
-    table = scatter_points(mask, hot, grad + square)
-    rhs = table[: 3 * PH]
-    diag = table[3 * PH :] + DAMPING
-    pb_ref[...] = rhs
-    pd_ref[...] = diag
-    z = rhs / diag
-    at = gather_points(mask, hot, z)
-    u = [sum(jp[3 * a + i] * at[i] for i in range(3)) for a in range(2)]
-    return u, total_of(rhs * z), total_of(z * z)
+    return scatter_points(mask, hot, grad + square), mask, hot, jp
 
 
 def start_copies(pairs, sems):
@@ -620,37 +617,54 @@
     counts = dot_nn(stack.astype(BF16), jnp.where(before, 1.0, 0.0).astype(BF16))
     counts = jnp.concatenate([counts[h * n_tile : (h + 1) * n_tile] for h in range(n_grp)], axis=1)
     rank = jnp.sum(jnp.where(mine, counts, 0.0), axis=0, keepdims=True)
-    place = owner * SLOTS + rank.astype(jnp.int32)
-    place_ref[...] = place
+    place_ref[0:1, :] = owner
+    place_ref[1:2, :] = rank.astype(jnp.int32)
     over = jnp.max(jnp.where(rank >= SLOTS, 1.0, 0.0), axis=1, keepdims=True)
-    u, gamma, norm = point_start(pidx_ref, jp_ref, res_ref, pb_ref, pd_ref)
-    pu_ref[0:1, :] = u[0]
-    pu_ref[1:2, :] = u[1]
-    sc_ref[...] = lanes(jnp.concatenate([gamma, norm, over], axis=0), HALF)
-    low = low_lanes(16)
-    for h in range(n_grp):
+    rank = rank.astype(jnp.int32)
+    hots = [one_hot_rows(rank + a * SLOTS, HALF) for a in range(2)]
+    rights = [
+        jnp.concatenate([hot[:, h * slot : (h + 1) * slot] for hot in hots], axis=1) for h in range(n_grp)
+    ]
+    def route_block(h):
         cols = slice(h * slot, (h + 1) * slot)
-        rows = []
+        here = [sixteen(owner[:, cols]) == BF16(t) for t in range(n_tile)]
+        left = []
         for a in range(2):
-            rows += [
+            rows = [
                 jc_ref[9 * a : 9 * a + 8, cols],
                 jc_ref[9 * a + 8 : 9 * a + 9, cols],
                 res_ref[a : a + 1, cols],
-                u[a][:, cols],
                 local[:, cols],
-                jnp.zeros((4, slot), F32),
+                jnp.zeros((5, slot), F32),
             ]
-        hot = one_hot_rows(place[:, cols], n_tile * SLOTS)
-        moved = thirds(dot_nt(three_parts(jnp.concatenate(rows, axis=0)), hot))
-        for k in range(n_tile // 2):
-            first = moved[0:16, k * HALF : (k + 1) * HALF]
-            second = moved[16:32, k * HALF : (k + 1) * HALF]
-            for t, block in (
-                (2 * k, jnp.where(low, first, swap_lanes(second))),
-                (2 * k + 1, jnp.where(low, swap_lanes(first), second)),
-            ):
-                for part in range(3):
-                    out_ref[3 * (h * n_tile + t) + part] = block[4 * part : 4 * part + 4]
+            left.append(masked_rows(two_parts(jnp.concatenate(rows, axis=0)), here))
+        moved = both(dot_nt(jnp.concatenate(left, axis=1), rights[h]))
+        for t in range(n_tile):
+            for part in range(3):
+                row = 16 * t + 4 * part
+                out_ref[3 * (h * n_tile + t) + part] = moved[row : row + 4]
+
+    table, mask, hot, jp = point_sums(pidx_ref, jp_ref, res_ref)
+    for h in range(n_grp // 2):
+        route_block(h)
+    rhs, diag = table[: 3 * PH], table[3 * PH :] + DAMPING
+    z = rhs / diag
+    at = gather_points(mask, hot, z)
+    for h in range(n_grp // 2, n_grp):
+        route_block(h)
+    pb_ref[...] = rhs
+    pd_ref[...] = diag
+    u = [sum(jp[3 * a + i] * at[i] for i in range(3)) for a in range(2)]
+    pu_ref[0:1, :] = u[0]
+    pu_ref[1:2, :] = u[1]
+    sc_ref[...] = lanes(jnp.concatenate([total_of(rhs * z), total_of(z * z), over], axis=0), HALF)
+    masks = [sixteen(owner) == as_16_bit(row_numbers(owner.shape[1]) + t) for t in range(0, n_tile, 16)]
+    left = [masked_rows(two_parts(jnp.broadcast_to(u[a], (16, u[a].shape[1]))), masks) for a in range(2)]
+    for h in range(n_grp):
+        cols = slice(h * slot, (h + 1) * slot)
+        moved = both(dot_nt(jnp.concatenate([v[:, cols] for v in left], axis=1), rights[h]))
+        for t in range(n_tile):
+            out_ref[3 * (h * n_tile + t) + 2, 3:4, :] = moved[t : t + 1]
 
 
 def unfold(even, odd):
@@ -672,31 +686,56 @@
             rest[a].append(pair_rest[a])
     main = [jnp.concatenate(v, axis=1) for v in main]
     rest = [jnp.concatenate(v, axis=1) for v in rest]
-    return main, rest, one_hot_rows(rest[0][3:4].astype(jnp.int32), CAM_DEV)
-
-
-def padded(main, tail):
-    below = lax.broadcasted_iota(jnp.int32, main.shape, 0) == 0
-    return jnp.concatenate([main, jnp.where(below, jnp.broadcast_to(tail, main.shape), 0.0)], axis=0)
-
-
-def scatter_own(hot, values):
-    return both(dot_nt(stacked(values), hot))
-
-
-def gather_own(hot, table, main, rest):
-    at = both(dot_nn(table, hot))
+    index = rest[0][2:3].astype(jnp.int32)
+    return main, rest, (index >> 7).astype(F32), one_hot_rows(index & 127, 128)
+
+
+OWN_ROWS = 32
+STEP = 32
+
+
+def scatter_two(hi, hot, first, second):
+    wide, numbers = sixteen(hi), row_numbers(hi.shape[1])
+    blocks = [wide == BF16(k) for k in range(3)]
+    tail = wide == as_16_bit(numbers & 7)
+    rows = two_parts(jnp.concatenate([first[0], second[0]], axis=0))
+    tails = two_parts(jnp.concatenate([eights(first[1]), eights(second[1])], axis=0))
+    none = jnp.zeros(wide.shape, BF16)
+    pieces = []
+    for part in range(2):
+        pieces += [jnp.where(mask, rows[part], none) for mask in blocks]
+        pieces.append(jnp.where(tail, tails[part], none))
+    return both(dot_nt(jnp.concatenate(pieces, axis=0), hot))
+
+
+def scatter_one(hi, hot, main, tail):
+    wide, numbers = sixteen(hi), row_numbers(hi.shape[1])
+    upper = wide == as_16_bit(numbers >> 3)
+    lower = wide == as_16_bit(jnp.where(numbers < 8, 2, numbers - 8))
+    rows = two_parts(jnp.concatenate([main, main], axis=0))
+    tails = two_parts(jnp.concatenate([main, eights(tail)], axis=0))
+    none = jnp.zeros(wide.shape, BF16)
+    pieces = []
+    for part in range(2):
+        pieces += [jnp.where(upper, rows[part], none), jnp.where(lower, tails[part], none)]
+    return both(dot_nt(jnp.concatenate(pieces, axis=0), hot))
+
+
+def gather_own(hi, hot, table, main, rest):
+    found = both(dot_nn(table, hot))
+    block = eights(hi)
+    at = jnp.where(block == 0, found[0:8], jnp.where(block == 1, found[8:16], found[16:24]))
+    numbers = lax.broadcasted_iota(jnp.int32, block.shape, 0).astype(F32)
+    tail = jnp.where(block == numbers, found[24:32], 0.0)
     return [
-        jnp.sum(main[a] * at[0:8], axis=0, keepdims=True) + rest[a][0:1] * at[8:9] for a in range(2)
+        jnp.sum(main[a] * at + eights(rest[a][0:1]) * tail, axis=0, keepdims=True) for a in range(2)
     ]
 
 
-def transposed_j(main, rest, e):
-    return padded(main[0] * e[0] + main[1] * e[1], rest[0][0:1] * e[0] + rest[1][0:1] * e[1])
-
-
-OWN_ROWS = 16
-STEP = 32
+def scatter_j(hi, hot, main, rest, e):
+    return scatter_one(
+        hi, hot, main[0] * e[0] + main[1] * e[1], rest[0][0:1] * e[0] + rest[1][0:1] * e[1]
+    )
 
 
 def owner_kernel(in_ref, sc_ref, back_ref, tb_ref, td_ref, ts_ref, acc_ref, zz_ref, w_ref, *kept):
@@ -705,14 +744,15 @@
     steps = devices // per
 
     if steps == 1:
-        main, rest, hot = read_routed(in_ref, range(devices))
+        main, rest, hi, hot = read_routed(in_ref, range(devices))
         kept[0][...] = hot
         for a in range(2):
             kept[1][8 * a : 8 * a + 8, :] = main[a]
             kept[1][16 + a : 17 + a, :] = rest[a][0:1]
+        kept[1][18:19, :] = hi
 
         def loop(body, start):
-            return body((main, rest, hot), 0, start)
+            return body((main, rest, hi, hot), 0, start)
     else:
 
         def loop(body, start):
@@ -722,21 +762,20 @@
             return lax.fori_loop(0, steps, step, start)
 
     def rhs_and_diag(slots, number, carry):
-        main, rest, hot = slots
+        main, rest, hi, hot = slots
         r = [rest[a][1:2] for a in range(2)]
-        rhs = padded(
-            -(main[0] * r[0] + main[1] * r[1]), -(rest[0][0:1] * r[0] + rest[1][0:1] * r[1])
-        )
-        square = padded(
+        rhs = (-(main[0] * r[0] + main[1] * r[1]), -(rest[0][0:1] * r[0] + rest[1][0:1] * r[1]))
+        square = (
             main[0] * main[0] + main[1] * main[1],
             rest[0][0:1] * rest[0][0:1] + rest[1][0:1] * rest[1][0:1],
         )
-        acc_ref[...] += scatter_own(hot, jnp.concatenate([rhs, square], axis=0))
+        acc_ref[...] += scatter_two(hi, hot, rhs, square)
         return carry
 
     acc_ref[...] = jnp.zeros(acc_ref.shape, F32)
     loop(rhs_and_diag, 0)
-    rhs, diag = acc_ref[0:OWN_ROWS, :], acc_ref[OWN_ROWS:, :] + DAMPING
+    rhs = jnp.concatenate([acc_ref[16 * k : 16 * k + 8, :] for k in range(4)], axis=0)
+    diag = jnp.concatenate([acc_ref[16 * k + 8 : 16 * k + 16, :] for k in range(4)], axis=0) + DAMPING
     tb_ref[...] = rhs
     td_ref[...] = diag
     z = rhs / diag
@@ -744,12 +783,12 @@
     acc_ref[0:OWN_ROWS, :] = z
 
     def apply(slots, number, energy):
-        main, rest, hot = slots
-        w = gather_own(hot, zz_ref[...], main, rest)
-        e = [rest[a][2:3] + w[a] for a in range(2)]
+        main, rest, hi, hot = slots
+        w = gather_own(hi, hot, zz_ref[...], main, rest)
+        e = [rest[a][3:4] + w[a] for a in range(2)]
         for a in range(2):
             w_ref[number, a : a + 1, :] = w[a]
-        acc_ref[0:OWN_ROWS, :] += scatter_own(hot, transposed_j(main, rest, e))
+        acc_ref[0:OWN_ROWS, :] += scatter_j(hi, hot, main, rest, e)
         return energy + e[0] * e[0] + e[1] * e[1]
 
     energy = loop(apply, jnp.zeros((1, per * SLOTS), F32))
@@ -761,8 +800,8 @@
     tail = jnp.concatenate([gamma, delta, sc_ref[2:3, :], sc_ref[2:3, :]], axis=0)
 
     def send(slots, number, carry):
-        main, rest, hot = slots
-        v = gather_own(hot, zz_ref[...], main, rest)
+        main, rest, hi, hot = slots
+        v = gather_own(hi, hot, zz_ref[...], main, rest)
         for a in range(2):
             w_ref[number, 2 + a : 3 + a, :] = v[a]
         w = w_ref[number]
@@ -789,12 +828,17 @@
     gamma, delta = scalars[0:1], scalars[1:2]
     over_ref[...] = lanes(scalars[2:3], HALF)
     alpha = gamma / delta
-    places = [one_hot_rows(place_ref[:, h * slot : (h + 1) * slot], n_tile * SLOTS) for h in range(n_grp)]
+    owner = place_ref[0:1, :]
+    slots = one_hot_rows(place_ref[1:2, :], HALF)
+    numbers = lax.broadcasted_iota(jnp.int32, (4 * n_tile, slot), 0) >> 2
     terms = []
     for h in range(n_grp):
-        pairs = range(h * n_tile, (h + 1) * n_tile, 2)
-        rows = jnp.concatenate([side_by_side(back_ref[k], back_ref[k + 1]) for k in pairs], axis=1)
-        terms.append(thirds(dot_nn(three_parts(rows), places[h])))
+        cols = slice(h * slot, (h + 1) * slot)
+        rows = jnp.concatenate([back_ref[h * n_tile + t] for t in range(n_tile)], axis=0)
+        found = both(dot_nn(stacked(rows), slots[:, cols]))
+        found = jnp.where(numbers == owner[:, cols], found, 0.0)
+        found = sum(found[8 * k : 8 * k + 8] for k in range(n_tile // 2))
+        terms.append(found[0:4] + found[4:8])
     terms = jnp.concatenate(terms, axis=1)
     w0 = [terms[a : a + 1] for a in range(2)]
     w1 = [terms[2 + a : 3 + a] for a in range(2)]
@@ -818,13 +862,16 @@
     sc_ref[...] = lanes(jnp.concatenate([gamma, alpha], axis=0), HALF)
     tail = lanes(jnp.concatenate([gamma1, delta1], axis=0), HALF)
     low = low_lanes(2)
+    numbers = row_numbers(slot)
     for h in range(n_grp):
-        rows = jnp.concatenate([e[:, h * slot : (h + 1) * slot] for e in error], axis=0)
-        moved = thirds(dot_nt(three_parts(rows), places[h]))
-        for k in range(n_tile // 2):
-            pair = moved[:, k * HALF : (k + 1) * HALF]
-            out_ref[h * n_tile + 2 * k] = jnp.where(low, pair, tail)
-            out_ref[h * n_tile + 2 * k + 1] = jnp.where(low, swap_lanes(pair), tail)
+        cols = slice(h * slot, (h + 1) * slot)
+        first, second = (jnp.broadcast_to(e[:, cols], (16, slot)) for e in error)
+        parts = two_parts(jnp.where((numbers & 1) == 0, first, second))
+        wide = sixteen(owner[:, cols])
+        here = [wide == as_16_bit((numbers >> 1) + t) for t in range(0, n_tile, 8)]
+        moved = both(dot_nt(masked_rows(parts, here), slots[:, cols]))
+        for t in range(n_tile):
+            out_ref[h * n_tile + t] = jnp.where(low, moved[2 * t : 2 * t + 2], tail)
 
 
 def point_results(alpha, alpha1, ratio, pb_ref, pd_ref, ps_ref, pt_ref, px_ref, pr_ref):
@@ -855,12 +902,13 @@
             hot, rows = kept[0][...], kept[1]
             main = [rows[8 * a : 8 * a + 8, :] for a in range(2)]
             rest = [rows[16 + a : 17 + a, :] for a in range(2)]
+            hi = rows[18:19, :]
         else:
-            main, rest, hot = read_routed(in_ref, sources)
+            main, rest, hi, hot = read_routed(in_ref, sources)
         e = jnp.concatenate(
             [side_by_side(err_ref[s], err_ref[t]) for s, t in zip(sources[::2], sources[1::2])], axis=1
         )
-        acc_ref[...] += scatter_own(hot, transposed_j(main, rest, [e[0:1], e[1:2]]))
+        acc_ref[...] += scatter_j(hi, hot, main, rest, [e[0:1], e[1:2]])
         return carry
 
     acc_ref[...] = jnp.zeros(acc_ref.shape, F32)
@@ -878,8 +926,13 @@
     z = rhs / cd_ref[...]
     r1 = rhs - alpha * s
     z1 = r1 / cd_ref[...]
-    cx_ref[...] = (alpha * z + alpha1 * (z1 + ratio * z))[0:9]
-    cr_ref[...] = (r1 - alpha1 * (z1 + acc_ref[...] + ratio * s))[0:9]
+    x = alpha * z + alpha1 * (z1 + ratio * z)
+    r2 = r1 - alpha1 * (z1 + acc_ref[...] + ratio * s)
+    for table, target in ((x, cx_ref), (r2, cr_ref)):
+        for k in range(3):
+            cols = slice(k * 128, (k + 1) * 128)
+            target[0:8, cols] = table[8 * k : 8 * k + 8]
+            target[8:9, cols] = table[24 + k : 25 + k]
 
 
 def shards(jac_point, jac_cam, resid, point_index, cam_index):
@@ -889,12 +942,13 @@
     pidx, cidx = point_index.reshape(1, obs), cam_index.reshape(1, obs)
     hbm = pl.BlockSpec(memory_space=pltpu.HBM)
     ints = jax.ShapeDtypeStruct((1, obs), jnp.int32)
+    places = jax.ShapeDtypeStruct((2, obs), jnp.int32)
     points = shape(3 * PH, LO)
-    cameras = shape(OWN_ROWS, CAM_DEV)
+    cameras = shape(OWN_ROWS, 128)
     routed, pb, pd, pu, jp, pidx_here, place, sc = pl.pallas_call(
         functools.partial(route_kernel, n_grp, n_tile),
         in_specs=[hbm] * 5,
-        out_shape=(shape(3 * devices, 4, HALF), points, points, shape(2, obs), shape(6, obs), ints, ints, shape(3, HALF)),
+        out_shape=(shape(3 * devices, 4, HALF), points, points, shape(2, obs), shape(6, obs), ints, places, shape(3, HALF)),
         scratch_shapes=[
             pltpu.VMEM((18, obs), F32),
             pltpu.VMEM((2, obs), F32),
@@ -908,13 +962,13 @@
     slots = devices * SLOTS
     per = min(STEP, devices)
     scratch = [
-        pltpu.VMEM((2 * OWN_ROWS, CAM_DEV), F32),
-        pltpu.VMEM((2 * OWN_ROWS, CAM_DEV), BF16),
+        pltpu.VMEM((2 * OWN_ROWS, 128), F32),
+        pltpu.VMEM((2 * OWN_ROWS, 128), BF16),
         pltpu.VMEM((devices // per, 4, per * SLOTS), F32),
     ]
     kept_shapes = ()
     if devices == per:
-        kept_shapes = (jax.ShapeDtypeStruct((CAM_DEV, slots), BF16), shape(24, slots))
+        kept_shapes = (jax.ShapeDtypeStruct((128, slots), BF16), shape(24, slots))
 
     def owner(in_ref, sc_ref, back_ref, tb_ref, td_ref, ts_ref, *others):
         kept, work = others[: len(kept_shapes)], others[len(kept_shapes) :]
@@ -947,7 +1001,7 @@
         return pl.pallas_call(
             routed_final_kernel,
             out_shape=outputs,
-            scratch_shapes=[pltpu.VMEM((OWN_ROWS, CAM_DEV), F32)],
+            scratch_shapes=[pltpu.VMEM((OWN_ROWS, 128), F32)],
             compiler_params=PARAMS,
             name="finish",
         )(*operands[5:])

time: 44.1 us -> 42.3 us (0.959)
  Pallas kernels: 7.9 us -> 6.09 us
    pallas_call x1, Pallas kernels: 2.14 us -> 1.2 us  [shards(): pl.pallas_call(owner, out_shape=(shape(devices, 4, HALF), cameras, camera...]
where the time goes in v5:
time: 42.3 us; the launch traced here: 42 us
  blocking collectives  25.8 us (61%)
  waiting for transfers between devices  6.9 us (16%)
  Pallas kernels  6.09 us (14%)
  starting transfers between devices  2.57 us (6%)
  between operations  0.69 us (2%)
    all_to_all x1, blocking collectives, shards(): routed = lax.all_to_all(routed, ('grp', 'tile'), 0, 0, tiled=True)  15.9 us
    all_to_all x1, blocking collectives, shards(): back = lax.all_to_all(back, ('grp', 'tile'), 0, 0, tiled=True)  9.9 us
    all_to_all x1, waiting for transfers between devices, shards(): errors = lax.all_to_all(errors, ('grp', 'tile'), 0, 0, tiled=True)  6.9 us
    all_to_all x1, starting transfers between devices, shards(): errors = lax.all_to_all(errors, ('grp', 'tile'), 0, 0, tiled=True)  2.57 us
    pallas_call x1, Pallas kernels, shards(): pl.pallas_call(functools.partial(route_kernel, n_grp, n_tile), in_specs=[...  1.95 us
    pallas_call x1, Pallas kernels, shards(): pl.pallas_call(functools.partial(routed_point_kernel, n_grp, n_tile), out...  1.65 us
    pallas_call x1, Pallas kernels, shards(): pl.pallas_call(owner, out_shape=(shape(devices, 4, HALF), cameras, camera...  1.2 us
    pallas_call x1, Pallas kernels, fits(): pl.pallas_call(routed_final_kernel, out_shape=outputs, scratch_shapes=[pl...  1 us
  transfers between devices with their start and end apart: 1, of which 1 were waited for; matrix products, arithmetic and copies ran while one was open for 0% of the time, Pallas kernels for 1%

profile of v5, /device:TPU:0, one launch (start us, length us, event | category | flops | bytes accessed | tf_op | source)
XLA Modules:
  0.0 42.0 jit_solution(126697652139723813)
XLA Ops:
  0.6 1.9 %route.1 = (f32[96,4,128]{2,1,0:T(4,128)S(1)}, f32[48,256]{1,0:T(8,128)S(1)}, f32[48,256]{1,0:T(8,128)S(1)}, f32[2,1024]{1,0:T(2,128)S(1)}, f32[6,1024]{1,0:T(8,...) custom-call(f32[6,1024]{1,0:T(8,128)} %jp_hbm.1, f32[18,1024]{1,0:T(8,128)} %jc_hbm.1, ...), custom_call_target="tpu_custom_call" | custom-call | tf_op jit(solution)/shard_map/route/pallas_call | solution.py:948
  2.6 15.9 %all_to_all.28.in_ref = f32[96,4,128]{2,1,0:T(4,128)S(1)} all-to-all(f32[96,4,128]{2,1,0:T(4,128)S(1)} %get-tuple-element.91), channel_id=1, replica_groups=mesh['grp'=4,'tile'=8] {'grp','tile'}, dimensions={0} | all-to-all | bytes 393216 | tf_op jit(solution)/shard_map/all_to_all | solution.py:961
  18.4 1.2 %owner.1 = (f32[32,4,128]{2,1,0:T(4,128)S(1)}, f32[32,128]{1,0:T(8,128)S(1)}, f32[32,128]{1,0:T(8,128)S(1)}, f32[32,128]{1,0:T(8,128)S(1)}, bf16[128,2048]{1,0:T(8,128)(2,1)S(1)}, /*index=5*/f32[24,2048]{1,0:T(8,128)S(1)}) custom-call(f32[96,4,128]{2,1,0:T(4,128)S(1)} %all_to_all.28.in_ref, f32[3,128]{1,0:T(4,128)S(1)} %get-tuple-element.92.sc_ref), custom_call_target="tpu_custom_call" | custom-call | tf_op jit(solution)/shard_map/owner/pallas_call | solution.py:977
  19.6 9.9 %all_to_all.29.back_ref = f32[32,4,128]{2,1,0:T(4,128)S(1)} all-to-all(f32[32,4,128]{2,1,0:T(4,128)S(1)} %get-tuple-element.93), channel_id=1, replica_groups=mesh['grp'=4,'tile'=8] {'grp','tile'}, dimensions={0} | all-to-all | bytes 131072 | tf_op jit(solution)/shard_map/all_to_all | solution.py:984
  29.5 1.6 %points.3 = (f32[32,2,128]{2,1,0:T(2,128)}, f32[48,256]{1,0:T(8,128)S(1)}, f32[2,1024]{1,0:T(2,128)S(1)}, f32[2,128]{1,0:T(2,128)S(1)}, f32[1,128]{1,0:T(1,128)S(1)}) custom-call(f32[32,4,128]{2,1,0:T(4,128)S(1)} %all_to_all.29.back_ref, f32[6,1024]{1,0:T(8,128)S(1)} %get-tuple-element.94.jp_ref, s32[1,1024]{1,0:T(1,128)S(1)} %get-tuple-element.95.pidx_ref, ...), custom_call_target="tpu_custom_call" | custom-call | tf_op jit(solution)/shard_map/points/pallas_call | solution.py:985
  31.2 2.6 %all-to-all-start.5 = ((f32[32,2,128]{2,1,0:T(2,128)}), f32[32,2,128]{2,1,0:T(2,128)S(1)}, u32[]{:S(2)}, u32[]{:S(2)}) async-start(f32[32,2,128]{2,1,0:T(2,128)} %get-tuple-element.104), calls=%async_computation.5 | async-start | bytes 65536 | tf_op jit(solution)/shard_map/all_to_all | solution.py:991
  33.8 0.3 last_point_sums.3
  34.1 6.9 %all-to-all-done.5 = f32[32,2,128]{2,1,0:T(2,128)S(1)} async-done(((f32[32,2,128]{2,1,0:T(2,128)}), f32[32,2,128]{2,1,0:T(2,128)S(1)}, u32[]{:S(2)}, u32[]{:S(2)}) %all-to-all-start.5) | async-done | bytes 32800 | tf_op jit(solution)/shard_map/all_to_all | solution.py:991
  41.0 1.0 %conditional.1 = ((f32[3,4096]{1,0:T(4,128)}, f32[9,384]{1,0:T(8,128)}, f32[3,4096]{1,0:T(4,128)}, f32[9,384]{1,0:T(8,128)})) conditional(s32[]{:T(128)} %bitcast.4, (f32[32,2,128]{2,1,0:T(2,128)S(1)}, f32[96,4,128]{2,1,0:T(4,128)S(1)}, f32[48,256]{1,0:T(8,128)S(1)}, f32[48,256]{1,0:T(8,128)S(1)}, f32[48,256]{1,0:T(8,128)S(1)}, ...), branch_computations={%region_0.0_spmd, %region_1.0_spmd} | conditional | flops 2000000000 | bytes 3728048 | solution.py:1012
  41.0 1.0 %finish.2 = (f32[3,4096]{1,0:T(4,128)}, f32[9,384]{1,0:T(8,128)}, f32[3,4096]{1,0:T(4,128)}, f32[9,384]{1,0:T(8,128)}) custom-call(f32[32,2,128]{2,1,0:T(2,128)S(1)} %get-tuple-element.34.err_ref, f32[96,4,128]{2,1,0:T(4,128)S(1)} %get-tuple-element.35.in_ref, f32[48,256]{1,0:T(8,128)S(1)} %get-tuple-element.36.pb_ref, ...), custom_call_target="tpu_custom_call" | custom-call | tf_op jit(solution)/shard_map/cond/branch_0_fun/finish/pallas_call | solution.py:1001
Async XLA Ops:
  31.2 9.8 %all-to-all-start.5 = ((f32[32,2,128]{2,1,0:T(2,128)}), f32[32,2,128]{2,1,0:T(2,128)S(1)}, u32[]{:S(2)}, u32[]{:S(2)}) async-start(f32[32,2,128]{2,1,0:T(2,128)} %get-tuple-element.104), calls=%async_computation.5 | async-start | bytes 65536 | tf_op jit(solution)/shard_map/all_to_all | solution.py:991

commit v6 on v5

--- a/solution.py
+++ b/solution.py
@@ -889,9 +889,13 @@
 
 
 def routed_final_kernel(
-    err_ref, in_ref, pb_ref, pd_ref, ps_ref, pt_ref, cb_ref, cd_ref, cs_ref, sc_ref, *rest_refs
+    err_ref, in_ref, jp_ref, pidx_ref, pe_ref, pb_ref, pd_ref, ps_ref, cb_ref, cd_ref, cs_ref, sc_ref, *rest_refs
 ):
-    kept, (px_ref, cx_ref, pr_ref, cr_ref, acc_ref) = rest_refs[:-5], rest_refs[-5:]
+    kept, outs, (px_ref, cx_ref, pr_ref, cr_ref, acc_ref, pt_ref, sems) = (
+        rest_refs[:-11],
+        rest_refs[-11:-7],
+        rest_refs[-7:],
+    )
     devices = err_ref.shape[0]
     per = min(STEP, devices)
     steps = devices // per
@@ -916,12 +920,19 @@
         body(0, 0)
     else:
         lax.fori_loop(0, steps, body, 0)
+    last_point_sums_kernel(jp_ref, pidx_ref, pe_ref, pt_ref)
     scalars = jnp.sum(err_ref[...], axis=0)
     gamma1, delta1 = scalars[0:1, SLOTS : SLOTS + 1], scalars[1:2, SLOTS : SLOTS + 1]
     gamma, alpha = sc_ref[0:1, 0:1], sc_ref[1:2, 0:1]
     ratio = gamma1 / gamma
     alpha1 = gamma1 / (delta1 - ratio * gamma1 / alpha)
     point_results(alpha, alpha1, ratio, pb_ref, pd_ref, ps_ref, pt_ref, px_ref, pr_ref)
+    copies = [
+        pltpu.make_async_copy(here, there, sems.at[k])
+        for k, (here, there) in enumerate(zip((px_ref, cx_ref, pr_ref, cr_ref), outs))
+    ]
+    copies[0].start()
+    copies[2].start()
     rhs, s = cb_ref[...], cs_ref[...]
     z = rhs / cd_ref[...]
     r1 = rhs - alpha * s
@@ -933,6 +944,10 @@
             cols = slice(k * 128, (k + 1) * 128)
             target[0:8, cols] = table[8 * k : 8 * k + 8]
             target[8:9, cols] = table[24 + k : 25 + k]
+    copies[1].start()
+    copies[3].start()
+    for copy in copies:
+        copy.wait()
 
 
 def shards(jac_point, jac_cam, resid, point_index, cam_index):
@@ -988,23 +1003,23 @@
         compiler_params=PARAMS,
         name="points",
     )(back, jp, pidx_here, place, pb, pd, pu, tb, td, ts)
-    errors = lax.all_to_all(errors, ("grp", "tile"), 0, 0, tiled=True)
-    pt = pl.pallas_call(
-        last_point_sums_kernel,
-        out_shape=points,
-        compiler_params=PARAMS,
-        name="last_point_sums",
-    )(jp, pidx_here, pe)
     outputs = (shape(3, P_DEV), shape(9, CAM_DEV), shape(3, P_DEV), shape(9, CAM_DEV))
 
     def fits(*operands):
+        errors = lax.all_to_all(operands[5], ("grp", "tile"), 0, 0, tiled=True)
         return pl.pallas_call(
             routed_final_kernel,
             out_shape=outputs,
-            scratch_shapes=[pltpu.VMEM((OWN_ROWS, 128), F32)],
+            out_specs=[hbm] * 4,
+            scratch_shapes=[pltpu.VMEM(v.shape, F32) for v in outputs]
+            + [
+                pltpu.VMEM((OWN_ROWS, 128), F32),
+                pltpu.VMEM((3 * PH, LO), F32),
+                pltpu.SemaphoreType.DMA((4,)),
+            ],
             compiler_params=PARAMS,
             name="finish",
-        )(*operands[5:])
+        )(errors, *operands[6:])
 
     def overflows(*operands):
         return tuple(replicated(*operands[:5]))
@@ -1014,7 +1029,7 @@
         overflows,
         lambda *operands: tuple(fits(*operands)),
         jac_point, jac_cam, resid, point_index, cam_index,
-        errors, routed, pb, pd, ps, pt, tb, td, ts, sc, *kept,
+        errors, routed, jp, pidx_here, pe, pb, pd, ps, tb, td, ts, sc, *kept,
     )
 
 

time: 42.3 us -> 41.9 us (level)
  blocking collectives: 25.8 us -> 24.8 us
  waiting for transfers between devices: 6.9 us -> 7.39 us
    all_to_all x1, blocking collectives: 9.9 us -> 8.93 us  [fits(): errors = lax.all_to_all(operands[5], ('grp', 'tile'), 0, 0, tiled=True)]
    pallas_call x1, Pallas kernels: 1.65 us -> 1.01 us  [shards(): pl.pallas_call(functools.partial(routed_point_kernel, n_grp, n_tile), out...]
    pallas_call x1, Pallas kernels: 1.2 us -> 1.83 us  [shards(): pl.pallas_call(owner, out_shape=(shape(devices, 4, HALF), cameras, camera...]
    all_to_all x1, waiting for transfers between devices: 6.9 us -> 7.39 us  [shards(): back = lax.all_to_all(back, ('grp', 'tile'), 0, 0, tiled=True)]
    pallas_call x2 -> x1, Pallas kernels: 1.3 us -> 1.21 us  [fits(): pl.pallas_call(routed_final_kernel, out_shape=outputs, out_specs=[hbm] *...]
  transfers between devices with their start and end apart: 1 -> 1, of which waited for: 1 -> 1; matrix products, arithmetic and copies ran while one was open for 0% -> 0% of each run, Pallas kernels for 1% -> 0%
where the time goes in v6:
time: 41.9 us; the launch traced here: 41.6 us
  blocking collectives  24.8 us (59%)
  waiting for transfers between devices  7.39 us (18%)
  Pallas kernels  5.99 us (14%)
  starting transfers between devices  2.72 us (6%)
  between operations  0.72 us (2%)
    all_to_all x1, blocking collectives, shards(): routed = lax.all_to_all(routed, ('grp', 'tile'), 0, 0, tiled=True)  15.9 us
    all_to_all x1, blocking collectives, fits(): errors = lax.all_to_all(operands[5], ('grp', 'tile'), 0, 0, tiled=True)  8.93 us
    all_to_all x1, waiting for transfers between devices, shards(): back = lax.all_to_all(back, ('grp', 'tile'), 0, 0, tiled=True)  7.39 us
    all_to_all x1, starting transfers between devices, shards(): back = lax.all_to_all(back, ('grp', 'tile'), 0, 0, tiled=True)  2.72 us
    pallas_call x1, Pallas kernels, shards(): pl.pallas_call(functools.partial(route_kernel, n_grp, n_tile), in_specs=[...  1.95 us
    pallas_call x1, Pallas kernels, shards(): pl.pallas_call(owner, out_shape=(shape(devices, 4, HALF), cameras, camera...  1.83 us
    pallas_call x1, Pallas kernels, fits(): pl.pallas_call(routed_final_kernel, out_shape=outputs, out_specs=[hbm] *...  1.21 us
    pallas_call x1, Pallas kernels, shards(): pl.pallas_call(functools.partial(routed_point_kernel, n_grp, n_tile), out...  1.01 us
  transfers between devices with their start and end apart: 1, of which 1 were waited for; matrix products, arithmetic and copies ran while one was open for 0% of the time, Pallas kernels for 0%

profile of v6, /device:TPU:0, one launch (start us, length us, event | category | flops | bytes accessed | tf_op | source)
XLA Modules:
  0.0 41.6 jit_solution(11979255205129411087)
XLA Ops:
  0.6 1.9 %route.1 = (f32[96,4,128]{2,1,0:T(4,128)S(1)}, f32[48,256]{1,0:T(8,128)S(1)}, f32[48,256]{1,0:T(8,128)S(1)}, f32[2,1024]{1,0:T(2,128)S(1)}, f32[6,1024]{1,0:T(8,...) custom-call(f32[6,1024]{1,0:T(8,128)} %jp_hbm.1, f32[18,1024]{1,0:T(8,128)} %jc_hbm.1, ...), custom_call_target="tpu_custom_call" | custom-call | tf_op jit(solution)/shard_map/route/pallas_call | solution.py:963
  2.6 15.9 %all_to_all.28.in_ref = f32[96,4,128]{2,1,0:T(4,128)S(1)} all-to-all(f32[96,4,128]{2,1,0:T(4,128)S(1)} %get-tuple-element.97), channel_id=1, replica_groups=mesh['grp'=4,'tile'=8] {'grp','tile'}, dimensions={0} | all-to-all | bytes 393216 | tf_op jit(solution)/shard_map/all_to_all | solution.py:976
  18.4 1.8 %owner.1 = (f32[32,4,128]{2,1,0:T(4,128)}, f32[32,128]{1,0:T(8,128)S(1)}, f32[32,128]{1,0:T(8,128)S(1)}, f32[32,128]{1,0:T(8,128)S(1)}, bf16[128,2048]{1,0:T(8,128)(2,1)S(1)}, /*index=5*/f32[24,2048]{1,0:T(8,128)S(1)}) custom-call(f32[96,4,128]{2,1,0:T(4,128)S(1)} %all_to_all.28.in_ref, f32[3,128]{1,0:T(4,128)S(1)} %get-tuple-element.98.sc_ref), custom_call_target="tpu_custom_call" | custom-call | tf_op jit(solution)/shard_map/owner/pallas_call | solution.py:992
  20.3 2.7 %all-to-all-start.5 = ((f32[32,4,128]{2,1,0:T(4,128)}), f32[32,4,128]{2,1,0:T(4,128)S(1)}, u32[]{:S(2)}, u32[]{:S(2)}) async-start(f32[32,4,128]{2,1,0:T(4,128)} %get-tuple-element.99), calls=%async_computation.5 | async-start | bytes 131072 | tf_op jit(solution)/shard_map/all_to_all | solution.py:999
  23.0 7.4 %all-to-all-done.5.back_ref = f32[32,4,128]{2,1,0:T(4,128)S(1)} async-done(((f32[32,4,128]{2,1,0:T(4,128)}), f32[32,4,128]{2,1,0:T(4,128)S(1)}, u32[]{:S(2)}, u32[]{:S(2)}) %all-to-all-start.5) | async-done | bytes 65568 | tf_op jit(solution)/shard_map/all_to_all | solution.py:999
  30.4 1.0 %points.3 = (f32[32,2,128]{2,1,0:T(2,128)S(1)}, f32[48,256]{1,0:T(8,128)S(1)}, f32[2,1024]{1,0:T(2,128)S(1)}, f32[2,128]{1,0:T(2,128)S(1)}, f32[1,128]{1,0:T(1,128)S(1)}) custom-call(f32[32,4,128]{2,1,0:T(4,128)S(1)} %all-to-all-done.5.back_ref, f32[6,1024]{1,0:T(8,128)S(1)} %get-tuple-element.100.jp_ref, s32[1,1024]{1,0:T(1,128)S(1)} %get-tuple-element.101.pidx_ref, ...), custom_call_target="tpu_custom_call" | custom-call | tf_op jit(solution)/shard_map/points/pallas_call | solution.py:1000
  31.5 10.2 %conditional.1 = ((f32[3,4096]{1,0:T(4,128)}, f32[9,384]{1,0:T(8,128)}, f32[3,4096]{1,0:T(4,128)}, f32[9,384]{1,0:T(8,128)})) conditional(s32[]{:T(128)} %bitcast.4, (f32[32,2,128]{2,1,0:T(2,128)S(1)}, f32[96,4,128]{2,1,0:T(4,128)S(1)}, f32[6,1024]{1,0:T(8,128)S(1)}, s32[1,1024]{1,0:T(1,128)S(1)}, f32[2,1024]{1,0:T(2,128)S(1)}, ...), branch_computations={%region_0.0_spmd, %region_1.0_spmd} | conditional | flops 2000000000 | bytes 3728048 | solution.py:1027
  31.5 8.9 %all_to_all.26.err_ref = f32[32,2,128]{2,1,0:T(2,128)S(1)} all-to-all(f32[32,2,128]{2,1,0:T(2,128)S(1)} %get-tuple-element.38), channel_id=1, replica_groups=mesh['grp'=4,'tile'=8] {'grp','tile'}, dimensions={0} | all-to-all | bytes 65536 | tf_op jit(solution)/shard_map/cond/branch_0_fun/all_to_all | solution.py:1009
  40.4 1.2 %finish.2 = (f32[3,4096]{1,0:T(4,128)}, f32[9,384]{1,0:T(8,128)}, f32[3,4096]{1,0:T(4,128)}, f32[9,384]{1,0:T(8,128)}) custom-call(f32[32,2,128]{2,1,0:T(2,128)S(1)} %all_to_all.26.err_ref, f32[96,4,128]{2,1,0:T(4,128)S(1)} %get-tuple-element.39.in_ref, f32[6,1024]{1,0:T(8,128)S(1)} %get-tuple-element.40.jp_ref, s32[1,1024]{1,0:T(1,128)S(1)} %get-tuple-element.41.pidx_ref, ...), custom_call_target="tpu_custom_call" | custom-call | tf_op jit(solution)/shard_map/cond/branch_0_fun/finish/pallas_call | solution.py:1010
Async XLA Ops:
  20.3 10.1 %all-to-all-start.5 = ((f32[32,4,128]{2,1,0:T(4,128)}), f32[32,4,128]{2,1,0:T(4,128)S(1)}, u32[]{:S(2)}, u32[]{:S(2)}) async-start(f32[32,4,128]{2,1,0:T(4,128)} %get-tuple-element.99), calls=%async_computation.5 | async-start | bytes 131072 | tf_op jit(solution)/shard_map/all_to_all | solution.py:999

commit v7 on v6

--- a/solution.py
+++ b/solution.py
@@ -1024,13 +1024,13 @@
     def overflows(*operands):
         return tuple(replicated(*operands[:5]))
 
-    return lax.cond(
-        over[0, 0] > 0,
-        overflows,
-        lambda *operands: tuple(fits(*operands)),
-        jac_point, jac_cam, resid, point_index, cam_index,
-        errors, routed, jp, pidx_here, pe, pb, pd, ps, tb, td, ts, sc, *kept,
+    over, *operands = lax.optimization_barrier(
+        (
+            over, jac_point, jac_cam, resid, point_index, cam_index,
+            errors, routed, jp, pidx_here, pe, pb, pd, ps, tb, td, ts, sc, *kept,
+        )
     )
+    return lax.cond(over[0, 0] > 0, overflows, lambda *operands: tuple(fits(*operands)), *operands)
 
 
 def solution(mesh):

time: 41.9 us -> 41 us (0.979)
  blocking collectives: 24.8 us -> 34.7 us
  waiting for transfers between devices: 7.39 us -> 0 us
  starting transfers between devices: 2.72 us -> 0 us
  Pallas kernels: 5.99 us -> 5.36 us
    all_to_all x0 -> x1, blocking collectives: none -> 9.9 us  [shards(): back = lax.all_to_all(back, ('grp', 'tile'), 0, 0, tiled=True)]
    all_to_all x1 -> x0, waiting for transfers between devices: 7.39 us -> none  [shards(): back = lax.all_to_all(back, ('grp', 'tile'), 0, 0, tiled=True)]
    all_to_all x1 -> x0, starting transfers between devices: 2.72 us -> none  [shards(): back = lax.all_to_all(back, ('grp', 'tile'), 0, 0, tiled=True)]
    pallas_call x1, Pallas kernels: 1.83 us -> 1.2 us  [shards(): pl.pallas_call(owner, out_shape=(shape(devices, 4, HALF), cameras, camera...]
  transfers between devices with their start and end apart: 1 -> 0, of which waited for: 1 -> 0; matrix products, arithmetic and copies ran while one was open for 0% -> 0% of each run, Pallas kernels for 0% -> 0%
where the time goes in v7:
time: 41 us; the launch traced here: 40.8 us
  blocking collectives  34.7 us (85%)
  Pallas kernels  5.36 us (13%)
  between operations  0.71 us (2%)
    all_to_all x1, blocking collectives, shards(): routed = lax.all_to_all(routed, ('grp', 'tile'), 0, 0, tiled=True)  15.9 us
    all_to_all x1, blocking collectives, shards(): back = lax.all_to_all(back, ('grp', 'tile'), 0, 0, tiled=True)  9.9 us
    all_to_all x1, blocking collectives, fits(): errors = lax.all_to_all(operands[5], ('grp', 'tile'), 0, 0, tiled=True)  8.93 us
    pallas_call x1, Pallas kernels, shards(): pl.pallas_call(functools.partial(route_kernel, n_grp, n_tile), in_specs=[...  1.95 us
    pallas_call x1, Pallas kernels, fits(): pl.pallas_call(routed_final_kernel, out_shape=outputs, out_specs=[hbm] *...  1.21 us
    pallas_call x1, Pallas kernels, shards(): pl.pallas_call(owner, out_shape=(shape(devices, 4, HALF), cameras, camera...  1.2 us
    pallas_call x1, Pallas kernels, shards(): pl.pallas_call(functools.partial(routed_point_kernel, n_grp, n_tile), out...  1.01 us

profile of v7, /device:TPU:0, one launch (start us, length us, event | category | flops | bytes accessed | tf_op | source)
XLA Modules:
  0.0 40.8 jit_solution(11346253126786055305)
XLA Ops:
  0.6 1.9 %route.1 = (f32[96,4,128]{2,1,0:T(4,128)S(1)}, f32[48,256]{1,0:T(8,128)S(1)}, f32[48,256]{1,0:T(8,128)S(1)}, f32[2,1024]{1,0:T(2,128)S(1)}, f32[6,1024]{1,0:T(8,...) custom-call(f32[6,1024]{1,0:T(8,128)} %jp_hbm.1, f32[18,1024]{1,0:T(8,128)} %jc_hbm.1, ...), custom_call_target="tpu_custom_call" | custom-call | tf_op jit(solution)/shard_map/route/pallas_call | solution.py:963
  2.6 15.9 %all_to_all.28.in_ref = f32[96,4,128]{2,1,0:T(4,128)S(1)} all-to-all(f32[96,4,128]{2,1,0:T(4,128)S(1)} %get-tuple-element.117), channel_id=1, replica_groups=mesh['grp'=4,'tile'=8] {'grp','tile'}, dimensions={0} | all-to-all | bytes 393216 | tf_op jit(solution)/shard_map/all_to_all | solution.py:976
  18.4 1.2 %owner.1 = (f32[32,4,128]{2,1,0:T(4,128)S(1)}, f32[32,128]{1,0:T(8,128)S(1)}, f32[32,128]{1,0:T(8,128)S(1)}, f32[32,128]{1,0:T(8,128)S(1)}, bf16[128,2048]{1,0:T(8,128)(2,1)S(1)}, /*index=5*/f32[24,2048]{1,0:T(8,128)S(1)}) custom-call(f32[96,4,128]{2,1,0:T(4,128)S(1)} %all_to_all.28.in_ref, f32[3,128]{1,0:T(4,128)S(1)} %get-tuple-element.118.sc_ref), custom_call_target="tpu_custom_call" | custom-call | tf_op jit(solution)/shard_map/owner/pallas_call | solution.py:992
  19.6 9.9 %all_to_all.29.back_ref = f32[32,4,128]{2,1,0:T(4,128)S(1)} all-to-all(f32[32,4,128]{2,1,0:T(4,128)S(1)} %get-tuple-element.119), channel_id=1, replica_groups=mesh['grp'=4,'tile'=8] {'grp','tile'}, dimensions={0} | all-to-all | bytes 131072 | tf_op jit(solution)/shard_map/all_to_all | solution.py:999
  29.5 1.0 %points.3 = (f32[32,2,128]{2,1,0:T(2,128)S(1)}, f32[48,256]{1,0:T(8,128)S(1)}, f32[2,1024]{1,0:T(2,128)S(1)}, f32[2,128]{1,0:T(2,128)S(1)}, f32[1,128]{1,0:T(1,128)S(1)}) custom-call(f32[32,4,128]{2,1,0:T(4,128)S(1)} %all_to_all.29.back_ref, f32[6,1024]{1,0:T(8,128)S(1)} %get-tuple-element.139.jp_ref, s32[1,1024]{1,0:T(1,128)S(1)} %get-tuple-element.140.pidx_ref, ...), custom_call_target="tpu_custom_call" | custom-call | tf_op jit(solution)/shard_map/points/pallas_call | solution.py:1000
  30.6 10.2 %conditional.1 = ((f32[3,4096]{1,0:T(4,128)}, f32[9,384]{1,0:T(8,128)}, f32[3,4096]{1,0:T(4,128)}, f32[9,384]{1,0:T(8,128)})) conditional(s32[]{:T(128)} %bitcast.4, (f32[32,2,128]{2,1,0:T(2,128)S(1)}, f32[96,4,128]{2,1,0:T(4,128)S(1)}, f32[6,1024]{1,0:T(8,128)S(1)}, s32[1,1024]{1,0:T(1,128)S(1)}, f32[2,1024]{1,0:T(2,128)S(1)}, ...), branch_computations={%region_0.0_spmd, %region_1.0_spmd} | conditional | flops 2000000000 | bytes 3728048 | solution.py:1033
  30.6 8.9 %all_to_all.26.err_ref = f32[32,2,128]{2,1,0:T(2,128)S(1)} all-to-all(f32[32,2,128]{2,1,0:T(2,128)S(1)} %get-tuple-element.38), channel_id=1, replica_groups=mesh['grp'=4,'tile'=8] {'grp','tile'}, dimensions={0} | all-to-all | bytes 65536 | tf_op jit(solution)/shard_map/cond/branch_0_fun/all_to_all | solution.py:1009
  39.6 1.2 %finish.2 = (f32[3,4096]{1,0:T(4,128)}, f32[9,384]{1,0:T(8,128)}, f32[3,4096]{1,0:T(4,128)}, f32[9,384]{1,0:T(8,128)}) custom-call(f32[32,2,128]{2,1,0:T(2,128)S(1)} %all_to_all.26.err_ref, f32[96,4,128]{2,1,0:T(4,128)S(1)} %get-tuple-element.39.in_ref, f32[6,1024]{1,0:T(8,128)S(1)} %get-tuple-element.40.jp_ref, s32[1,1024]{1,0:T(1,128)S(1)} %get-tuple-element.41.pidx_ref, ...), custom_call_target="tpu_custom_call" | custom-call | tf_op jit(solution)/shard_map/cond/branch_0_fun/finish/pallas_call | solution.py:1010

commit v8 on v7

--- a/solution.py
+++ b/solution.py
@@ -109,9 +109,8 @@
 
 
 def scatter_points(mask, hot, rows):
-    parts = [halves(v) for v in rows]
-    lhs = jnp.concatenate([spread_row(mask, v[k]) for k in range(2) for v in parts], axis=0)
-    return both(dot_nt(lhs.astype(BF16), hot))
+    pieces = [spread_row(mask, v[k : k + 1]) for v in halves(rows) for k in range(rows.shape[0])]
+    return both(dot_nt(jnp.concatenate(pieces, axis=0).astype(BF16), hot))
 
 
 def gather_points(mask, hot, table):
@@ -159,7 +158,7 @@
     res = [res_ref[a : a + 1, :] for a in range(2)]
     grad = [-(jp[i] * res[0] + jp[3 + i] * res[1]) for i in range(3)]
     square = [jp[i] * jp[i] + jp[3 + i] * jp[3 + i] for i in range(3)]
-    table = scatter_points(mask, hot, grad + square)
+    table = scatter_points(mask, hot, jnp.concatenate(grad + square, axis=0))
     rhs = table[: 3 * PH]
     diag = table[3 * PH :] + DAMPING
     pb_ref[...] = rhs
@@ -351,7 +350,7 @@
     rhs, diag = pb_ref[...], pd_ref[...]
     z = rhs / diag
     error = [pu_ref[a : a + 1, :] + w[a] for a in range(2)]
-    s = z + scatter_points(mask, hot, [jp[i] * error[0] + jp[3 + i] * error[1] for i in range(3)])
+    s = z + scatter_points(mask, hot, jp_ref[0:3, :] * error[0] + jp_ref[3:6, :] * error[1])
     r1 = rhs - alpha * s
     z1 = r1 / diag
     at = gather_points(mask, hot, z1)
@@ -383,11 +382,8 @@
     index = pidx_ref[...]
     mask = is_row(index >> LO_BITS, PH)
     hot = one_hot_rows(index & (LO - 1), LO)
-    jp = [jp_ref[k : k + 1, :] for k in range(6)]
-    error = [pe_ref[a : a + 1, :] for a in range(2)]
-    pt_ref[...] = scatter_points(
-        mask, hot, [jp[i] * error[0] + jp[3 + i] * error[1] for i in range(3)]
-    )
+    terms = jp_ref[0:3, :] * pe_ref[0:1, :] + jp_ref[3:6, :] * pe_ref[1:2, :]
+    pt_ref[...] = scatter_points(mask, hot, terms)
 
 
 def final_kernel(
@@ -575,11 +571,10 @@
     index = pidx_ref[...]
     mask = is_row(index >> LO_BITS, PH)
     hot = one_hot_rows(index & (LO - 1), LO)
-    jp = [jp_ref[k : k + 1, :] for k in range(6)]
-    res = [res_ref[a : a + 1, :] for a in range(2)]
-    grad = [-(jp[i] * res[0] + jp[3 + i] * res[1]) for i in range(3)]
-    square = [jp[i] * jp[i] + jp[3 + i] * jp[3 + i] for i in range(3)]
-    return scatter_points(mask, hot, grad + square), mask, hot, jp
+    jp = jp_ref[0:3, :], jp_ref[3:6, :]
+    grad = -(jp[0] * res_ref[0:1, :] + jp[1] * res_ref[1:2, :])
+    square = jp[0] * jp[0] + jp[1] * jp[1]
+    return scatter_points(mask, hot, jnp.concatenate([grad, square], axis=0)), mask, hot, jp
 
 
 def start_copies(pairs, sems):
@@ -621,50 +616,52 @@
     place_ref[1:2, :] = rank.astype(jnp.int32)
     over = jnp.max(jnp.where(rank >= SLOTS, 1.0, 0.0), axis=1, keepdims=True)
     rank = rank.astype(jnp.int32)
-    hots = [one_hot_rows(rank + a * SLOTS, HALF) for a in range(2)]
-    rights = [
-        jnp.concatenate([hot[:, h * slot : (h + 1) * slot] for hot in hots], axis=1) for h in range(n_grp)
-    ]
-    def route_block(h):
+    hot_rank = one_hot_rows(rank, HALF)
+    wide = sixteen(owner)
+    numbers = row_numbers(owner.shape[1])
+    core = lax.axis_index("tile") % 2
+    upper, lower, others = core, 1 + core, 2 - 2 * core
+    low = low_lanes(8)
+
+    def route_main(h):
         cols = slice(h * slot, (h + 1) * slot)
-        here = [sixteen(owner[:, cols]) == BF16(t) for t in range(n_tile)]
-        left = []
-        for a in range(2):
-            rows = [
-                jc_ref[9 * a : 9 * a + 8, cols],
-                jc_ref[9 * a + 8 : 9 * a + 9, cols],
-                res_ref[a : a + 1, cols],
-                local[:, cols],
-                jnp.zeros((5, slot), F32),
-            ]
-            left.append(masked_rows(two_parts(jnp.concatenate(rows, axis=0)), here))
-        moved = both(dot_nt(jnp.concatenate(left, axis=1), rights[h]))
+        here = [wide[:, cols] == BF16(t) for t in range(n_tile)]
+        parts = two_parts(jnp.concatenate([jc_ref[0:8, cols], jc_ref[9:17, cols]], axis=0))
+        moved = both(dot_nt(masked_rows(parts, here), hot_rank[:, cols]))
         for t in range(n_tile):
-            for part in range(3):
-                row = 16 * t + 4 * part
-                out_ref[3 * (h * n_tile + t) + part] = moved[row : row + 4]
+            first, second = moved[16 * t : 16 * t + 8], moved[16 * t + 8 : 16 * t + 16]
+            tile = jnp.where(low, first, swap_lanes(second))
+            out_ref[3 * (h * n_tile + t) + upper] = tile[0:4]
+            out_ref[3 * (h * n_tile + t) + lower] = tile[4:8]
+
+    def route_rest(parts, here, h):
+        cols = slice(h * slot, (h + 1) * slot)
+        left = masked_rows([p[:, cols] for p in parts], [m[:, cols] for m in here])
+        moved = both(dot_nt(left, hot_rank[:, cols]))
+        for t in range(n_tile):
+            rows = moved[8 * t : 8 * t + 8]
+            tile = jnp.where(low[0:4], rows[0:4], swap_lanes(rows)[4:8])
+            out_ref[3 * (h * n_tile + t) + others] = tile
 
     table, mask, hot, jp = point_sums(pidx_ref, jp_ref, res_ref)
     for h in range(n_grp // 2):
-        route_block(h)
+        route_main(h)
     rhs, diag = table[: 3 * PH], table[3 * PH :] + DAMPING
     z = rhs / diag
     at = gather_points(mask, hot, z)
     for h in range(n_grp // 2, n_grp):
-        route_block(h)
+        route_main(h)
     pb_ref[...] = rhs
     pd_ref[...] = diag
-    u = [sum(jp[3 * a + i] * at[i] for i in range(3)) for a in range(2)]
+    u = [sum(jp[a][i : i + 1] * at[i] for i in range(3)) for a in range(2)]
     pu_ref[0:1, :] = u[0]
     pu_ref[1:2, :] = u[1]
     sc_ref[...] = lanes(jnp.concatenate([total_of(rhs * z), total_of(z * z), over], axis=0), HALF)
-    masks = [sixteen(owner) == as_16_bit(row_numbers(owner.shape[1]) + t) for t in range(0, n_tile, 16)]
-    left = [masked_rows(two_parts(jnp.broadcast_to(u[a], (16, u[a].shape[1]))), masks) for a in range(2)]
+    rows = [jc_ref[8:9, :], res_ref[0:1, :], local, u[0], jc_ref[17:18, :], res_ref[1:2, :], local, u[1]]
+    parts = two_parts(jnp.concatenate(rows * 2, axis=0))
+    here = [wide == as_16_bit((numbers >> 3) + t) for t in range(0, n_tile, 2)]
     for h in range(n_grp):
-        cols = slice(h * slot, (h + 1) * slot)
-        moved = both(dot_nt(jnp.concatenate([v[:, cols] for v in left], axis=1), rights[h]))
-        for t in range(n_tile):
-            out_ref[3 * (h * n_tile + t) + 2, 3:4, :] = moved[t : t + 1]
+        route_rest(parts, here, h)
 
 
 def unfold(even, odd):
@@ -672,15 +669,24 @@
     return jnp.where(low, even, swap_lanes(odd)), jnp.where(low, swap_lanes(even), odd)
 
 
+def unfold_rest(both_rows):
+    low, swapped = low_lanes(4), swap_lanes(both_rows)
+    return (
+        jnp.where(low, both_rows[0:4], swapped[4:8]),
+        jnp.where(low, swapped[0:4], both_rows[4:8]),
+    )
+
+
 def side_by_side(even, odd):
     return jnp.where(low_lanes(even.shape[0]), even, swap_lanes(odd))
 
 
 def read_routed(ref, sources):
     main, rest = ([], []), ([], [])
-    for s, t in zip(sources[::2], sources[1::2]):
-        pair = unfold(*(jnp.concatenate([ref[3 * k], ref[3 * k + 1]], axis=0) for k in (s, t)))
-        pair_rest = unfold(ref[3 * s + 2], ref[3 * t + 2])
+    for s in sources[::2]:
+        tile = 3 * (s // 2)
+        pair = unfold(ref[tile], ref[tile + 2])
+        pair_rest = unfold_rest(ref[tile + 1])
         for a in range(2):
             main[a].append(pair[a])
             rest[a].append(pair_rest[a])
@@ -825,6 +831,7 @@
     hot = one_hot_rows(index & (LO - 1), LO)
     jp = [jp_ref[k : k + 1, :] for k in range(6)]
     scalars = jnp.sum(back_ref[...], axis=0)[:, SLOTS : SLOTS + 1]
+    scalars = scalars[0:4] + scalars[4:8]
     gamma, delta = scalars[0:1], scalars[1:2]
     over_ref[...] = lanes(scalars[2:3], HALF)
     alpha = gamma / delta
@@ -834,7 +841,7 @@
     terms = []
     for h in range(n_grp):
         cols = slice(h * slot, (h + 1) * slot)
-        rows = jnp.concatenate([back_ref[h * n_tile + t] for t in range(n_tile)], axis=0)
+        rows = jnp.concatenate([back_ref[h * n_tile // 2 + k] for k in range(n_tile // 2)], axis=0)
         found = both(dot_nn(stacked(rows), slots[:, cols]))
         found = jnp.where(numbers == owner[:, cols], found, 0.0)
         found = sum(found[8 * k : 8 * k + 8] for k in range(n_tile // 2))
@@ -845,7 +852,7 @@
     rhs, diag = pb_ref[...], pd_ref[...]
     z = rhs / diag
     error = [pu_ref[a : a + 1, :] + w0[a] for a in range(2)]
-    s = z + scatter_points(mask, hot, [jp[i] * error[0] + jp[3 + i] * error[1] for i in range(3)])
+    s = z + scatter_points(mask, hot, jp_ref[0:3, :] * error[0] + jp_ref[3:6, :] * error[1])
     r1 = rhs - alpha * s
     z1 = r1 / diag
     at = gather_points(mask, hot, z1)
@@ -874,18 +881,19 @@
             out_ref[h * n_tile + t] = jnp.where(low, moved[2 * t : 2 * t + 2], tail)
 
 
-def point_results(alpha, alpha1, ratio, pb_ref, pd_ref, ps_ref, pt_ref, px_ref, pr_ref):
+def point_results(alpha, alpha1, ratio, pb_ref, pd_ref, ps_ref, pt_ref, px_ref, pr_ref, copies):
     rhs, diag, s = pb_ref[...], pd_ref[...], ps_ref[...]
     z = rhs / diag
     r1 = rhs - alpha * s
     z1 = r1 / diag
     x = alpha * z + alpha1 * (z1 + ratio * z)
     r2 = r1 - alpha1 * (z1 + pt_ref[...] + ratio * s)
-    for i in range(3):
-        for hi in range(PH):
-            row = i * PH + hi
-            px_ref[i : i + 1, hi * LO : (hi + 1) * LO] = x[row : row + 1]
-            pr_ref[i : i + 1, hi * LO : (hi + 1) * LO] = r2[row : row + 1]
+    for table, target, copy in ((x, px_ref, copies[0]), (r2, pr_ref, copies[1])):
+        for i in range(3):
+            for hi in range(PH):
+                row = i * PH + hi
+                target[i : i + 1, hi * LO : (hi + 1) * LO] = table[row : row + 1]
+        copy.start()
 
 
 def routed_final_kernel(
@@ -926,13 +934,13 @@
     gamma, alpha = sc_ref[0:1, 0:1], sc_ref[1:2, 0:1]
     ratio = gamma1 / gamma
     alpha1 = gamma1 / (delta1 - ratio * gamma1 / alpha)
-    point_results(alpha, alpha1, ratio, pb_ref, pd_ref, ps_ref, pt_ref, px_ref, pr_ref)
     copies = [
         pltpu.make_async_copy(here, there, sems.at[k])
         for k, (here, there) in enumerate(zip((px_ref, cx_ref, pr_ref, cr_ref), outs))
     ]
-    copies[0].start()
-    copies[2].start()
+    point_results(
+        alpha, alpha1, ratio, pb_ref, pd_ref, ps_ref, pt_ref, px_ref, pr_ref, (copies[0], copies[2])
+    )
     rhs, s = cb_ref[...], cs_ref[...]
     z = rhs / cd_ref[...]
     r1 = rhs - alpha * s
@@ -973,7 +981,7 @@
         compiler_params=PARAMS,
         name="route",
     )(*(pltpu.with_memory_space_constraint(x, pltpu.HBM) for x in (jac_point, jac_cam, resid, pidx, cidx)))
-    routed = lax.all_to_all(routed, ("grp", "tile"), 0, 0, tiled=True)
+    routed = lax.all_to_all(routed, ("grp", "tile"), 0, 0, tiled=True).reshape(3 * devices // 2, 8, HALF)
     slots = devices * SLOTS
     per = min(STEP, devices)
     scratch = [
@@ -996,7 +1004,7 @@
         compiler_params=PARAMS,
         name="owner",
     )(routed, sc)
-    back = lax.all_to_all(back, ("grp", "tile"), 0, 0, tiled=True)
+    back = lax.all_to_all(back, ("grp", "tile"), 0, 0, tiled=True).reshape(devices // 2, 8, HALF)
     errors, ps, pe, sc, over = pl.pallas_call(
         functools.partial(routed_point_kernel, n_grp, n_tile),
         out_shape=(shape(devices, 2, HALF), points, shape(2, obs), shape(2, HALF), shape(1, HALF)),

time: 41 us -> 41 us (level)
  no operation moved by 1% of the time
where the time goes in v8:
time: 41 us; the launch traced here: 40.8 us
  blocking collectives  34.7 us (85%)
  Pallas kernels  5.33 us (13%)
  between operations  0.71 us (2%)
    all_to_all x1, blocking collectives, shards(): lax.all_to_all(routed, ('grp', 'tile'), 0, 0, tiled=True)  15.9 us
    all_to_all x1, blocking collectives, shards(): lax.all_to_all(back, ('grp', 'tile'), 0, 0, tiled=True)  9.91 us
    all_to_all x1, blocking collectives, fits(): errors = lax.all_to_all(operands[5], ('grp', 'tile'), 0, 0, tiled=True)  8.93 us
    pallas_call x1, Pallas kernels, shards(): pl.pallas_call(functools.partial(route_kernel, n_grp, n_tile), in_specs=[...  1.93 us
    pallas_call x1, Pallas kernels, fits(): pl.pallas_call(routed_final_kernel, out_shape=outputs, out_specs=[hbm] *...  1.21 us
    pallas_call x1, Pallas kernels, shards(): pl.pallas_call(owner, out_shape=(shape(devices, 4, HALF), cameras, camera...  1.19 us
    pallas_call x1, Pallas kernels, shards(): pl.pallas_call(functools.partial(routed_point_kernel, n_grp, n_tile), out...  1 us

profile of v8, /device:TPU:0, one launch (start us, length us, event | category | flops | bytes accessed | tf_op | source)
XLA Modules:
  0.0 40.8 jit_solution(10000915893229551453)
XLA Ops:
  0.6 1.9 %route.1 = (f32[96,4,128]{2,1,0:T(4,128)S(1)}, f32[48,256]{1,0:T(8,128)S(1)}, f32[48,256]{1,0:T(8,128)S(1)}, f32[2,1024]{1,0:T(2,128)S(1)}, f32[6,1024]{1,0:T(8,...) custom-call(f32[6,1024]{1,0:T(8,128)} %jp_hbm.1, f32[18,1024]{1,0:T(8,128)} %jc_hbm.1, ...), custom_call_target="tpu_custom_call" | custom-call | tf_op jit(solution)/shard_map/route/pallas_call | solution.py:971
  2.6 15.9 %all_to_all.28 = f32[96,4,128]{2,1,0:T(4,128)S(1)} all-to-all(f32[96,4,128]{2,1,0:T(4,128)S(1)} %get-tuple-element.117), channel_id=1, replica_groups=mesh['grp'=4,'tile'=8] {'grp','tile'}, dimensions={0} | all-to-all | bytes 393216 | tf_op jit(solution)/shard_map/all_to_all | solution.py:984
  18.4 1.2 %owner.1 = (f32[32,4,128]{2,1,0:T(4,128)S(1)}, f32[32,128]{1,0:T(8,128)S(1)}, f32[32,128]{1,0:T(8,128)S(1)}, f32[32,128]{1,0:T(8,128)S(1)}, bf16[128,2048]{1,0:T(8,128)(2,1)S(1)}, /*index=5*/f32[24,2048]{1,0:T(8,128)S(1)}) custom-call(f32[48,8,128]{2,1,0:T(8,128)S(1)} %bitcast.10, f32[3,128]{1,0:T(4,128)S(1)} %get-tuple-element.118.sc_ref), custom_call_target="tpu_custom_call" | custom-call | tf_op jit(solution)/shard_map/owner/pallas_call | solution.py:1000
  19.6 9.9 %all_to_all.29 = f32[32,4,128]{2,1,0:T(4,128)S(1)} all-to-all(f32[32,4,128]{2,1,0:T(4,128)S(1)} %get-tuple-element.119), channel_id=1, replica_groups=mesh['grp'=4,'tile'=8] {'grp','tile'}, dimensions={0} | all-to-all | bytes 131072 | tf_op jit(solution)/shard_map/all_to_all | solution.py:1007
  29.5 1.0 %points.3 = (f32[32,2,128]{2,1,0:T(2,128)S(1)}, f32[48,256]{1,0:T(8,128)S(1)}, f32[2,1024]{1,0:T(2,128)S(1)}, f32[2,128]{1,0:T(2,128)S(1)}, f32[1,128]{1,0:T(1,128)S(1)}) custom-call(f32[16,8,128]{2,1,0:T(8,128)S(1)} %bitcast.8, f32[6,1024]{1,0:T(8,128)S(1)} %get-tuple-element.139.jp_ref, s32[1,1024]{1,0:T(1,128)S(1)} %get-tuple-element.140.pidx_ref, ...), custom_call_target="tpu_custom_call" | custom-call | tf_op jit(solution)/shard_map/points/pallas_call | solution.py:1008
  30.6 10.2 %conditional.1 = ((f32[3,4096]{1,0:T(4,128)}, f32[9,384]{1,0:T(8,128)}, f32[3,4096]{1,0:T(4,128)}, f32[9,384]{1,0:T(8,128)})) conditional(s32[]{:T(128)} %bitcast.6, (f32[32,2,128]{2,1,0:T(2,128)S(1)}, f32[48,8,128]{2,1,0:T(8,128)S(1)}, f32[6,1024]{1,0:T(8,128)S(1)}, s32[1,1024]{1,0:T(1,128)S(1)}, f32[2,1024]{1,0:T(2,128)S(1)}, ...), branch_computations={%region_0.0_spmd, %region_1.0_spmd} | conditional | flops 2000000000 | bytes 3728048 | solution.py:1041
  30.6 8.9 %all_to_all.26.err_ref = f32[32,2,128]{2,1,0:T(2,128)S(1)} all-to-all(f32[32,2,128]{2,1,0:T(2,128)S(1)} %get-tuple-element.38), channel_id=1, replica_groups=mesh['grp'=4,'tile'=8] {'grp','tile'}, dimensions={0} | all-to-all | bytes 65536 | tf_op jit(solution)/shard_map/cond/branch_0_fun/all_to_all | solution.py:1017
  39.5 1.2 %finish.2 = (f32[3,4096]{1,0:T(4,128)}, f32[9,384]{1,0:T(8,128)}, f32[3,4096]{1,0:T(4,128)}, f32[9,384]{1,0:T(8,128)}) custom-call(f32[32,2,128]{2,1,0:T(2,128)S(1)} %all_to_all.26.err_ref, f32[48,8,128]{2,1,0:T(8,128)S(1)} %get-tuple-element.39.in_ref, f32[6,1024]{1,0:T(8,128)S(1)} %get-tuple-element.40.jp_ref, s32[1,1024]{1,0:T(1,128)S(1)} %get-tuple-element.41.pidx_ref, ...), custom_call_target="tpu_custom_call" | custom-call | tf_op jit(solution)/shard_map/cond/branch_0_fun/finish/pallas_call | solution.py:1018

commit v9 on v8

--- a/solution.py
+++ b/solution.py
@@ -16,6 +16,7 @@
 F32 = jnp.float32
 BF16 = jnp.bfloat16
 SLOTS = 64
+FULL = SLOTS - 1
 HALF = 128
 PARAMS = pltpu.CompilerParams(vmem_limit_bytes=48 * 1024 * 1024)
 
@@ -614,7 +615,7 @@
     rank = jnp.sum(jnp.where(mine, counts, 0.0), axis=0, keepdims=True)
     place_ref[0:1, :] = owner
     place_ref[1:2, :] = rank.astype(jnp.int32)
-    over = jnp.max(jnp.where(rank >= SLOTS, 1.0, 0.0), axis=1, keepdims=True)
+    over = jnp.max(jnp.where(rank >= FULL, 1.0, 0.0), axis=1, keepdims=True)
     rank = rank.astype(jnp.int32)
     hot_rank = one_hot_rows(rank, HALF)
     wide = sixteen(owner)
@@ -677,8 +678,8 @@
     )
 
 
-def side_by_side(even, odd):
-    return jnp.where(low_lanes(even.shape[0]), even, swap_lanes(odd))
+def last_slot(v):
+    return (lax.broadcasted_iota(jnp.int32, v.shape, 1) & (SLOTS - 1)) == FULL
 
 
 def read_routed(ref, sources):
@@ -793,7 +794,7 @@
         w = gather_own(hi, hot, zz_ref[...], main, rest)
         e = [rest[a][3:4] + w[a] for a in range(2)]
         for a in range(2):
-            w_ref[number, a : a + 1, :] = w[a]
+            w_ref[number, 2 * a : 2 * a + 1, :] = w[a]
         acc_ref[0:OWN_ROWS, :] += scatter_j(hi, hot, main, rest, e)
         return energy + e[0] * e[0] + e[1] * e[1]
 
@@ -803,19 +804,25 @@
     zz_ref[...] = stacked(s / diag)
     gamma = sc_ref[0:1, :] + total_of(rhs * z)
     delta = sc_ref[1:2, :] + total_of(z * z) + total_of(energy)
-    tail = jnp.concatenate([gamma, delta, sc_ref[2:3, :], sc_ref[2:3, :]], axis=0)
+    over = sc_ref[2:3, :]
+    low = low_lanes(2)
+    tail = jnp.where(
+        low, jnp.concatenate([gamma, over], axis=0), jnp.concatenate([delta, over], axis=0)
+    )
 
     def send(slots, number, carry):
         main, rest, hi, hot = slots
         v = gather_own(hi, hot, zz_ref[...], main, rest)
         for a in range(2):
-            w_ref[number, 2 + a : 3 + a, :] = v[a]
+            w_ref[number, 2 * a + 1 : 2 * a + 2, :] = v[a]
         w = w_ref[number]
-        low = low_lanes(4)
         for k in range(per // 2):
-            pair = w[:, k * HALF : (k + 1) * HALF]
-            back_ref[number * per + 2 * k] = jnp.where(low, pair, tail)
-            back_ref[number * per + 2 * k + 1] = jnp.where(low, swap_lanes(pair), tail)
+            cols = slice(k * HALF, (k + 1) * HALF)
+            first, second = w[0:2, cols], w[2:4, cols]
+            even = jnp.where(low, first, swap_lanes(second))
+            odd = jnp.where(low, swap_lanes(first), second)
+            for t, tile in ((2 * k, even), (2 * k + 1, odd)):
+                back_ref[number * per + t] = jnp.where(last_slot(tile), tail, tile)
         return carry
 
     loop(send, 0)
@@ -830,25 +837,32 @@
     mask = is_row(index >> LO_BITS, PH)
     hot = one_hot_rows(index & (LO - 1), LO)
     jp = [jp_ref[k : k + 1, :] for k in range(6)]
-    scalars = jnp.sum(back_ref[...], axis=0)[:, SLOTS : SLOTS + 1]
+    scalars = jnp.sum(back_ref[...], axis=0)
     scalars = scalars[0:4] + scalars[4:8]
-    gamma, delta = scalars[0:1], scalars[1:2]
-    over_ref[...] = lanes(scalars[2:3], HALF)
+    scalars = scalars[0:2] + scalars[2:4]
+    gamma, delta = scalars[0:1, FULL : FULL + 1], scalars[0:1, HALF - 1 : HALF]
+    over_ref[...] = lanes(scalars[1:2, FULL : FULL + 1], HALF)
     alpha = gamma / delta
     owner = place_ref[0:1, :]
-    slots = one_hot_rows(place_ref[1:2, :], HALF)
-    numbers = lax.broadcasted_iota(jnp.int32, (4 * n_tile, slot), 0) >> 2
+    hot_rank = one_hot_rows(place_ref[1:2, :], HALF)
+    numbers = lax.broadcasted_iota(jnp.int32, (2 * n_tile, slot), 0) >> 1
     terms = []
     for h in range(n_grp):
         cols = slice(h * slot, (h + 1) * slot)
-        rows = jnp.concatenate([back_ref[h * n_tile // 2 + k] for k in range(n_tile // 2)], axis=0)
-        found = both(dot_nn(stacked(rows), slots[:, cols]))
-        found = jnp.where(numbers == owner[:, cols], found, 0.0)
-        found = sum(found[8 * k : 8 * k + 8] for k in range(n_tile // 2))
-        terms.append(found[0:4] + found[4:8])
+        rows = jnp.concatenate([back_ref[h * n_tile // 4 + k] for k in range(n_tile // 4)], axis=0)
+        rows = jnp.concatenate([rows, swap_lanes(rows)], axis=0)
+        found = both(dot_nn(stacked(rows), hot_rank[:, cols]))
+        here = numbers == owner[:, cols]
+        of_a = []
+        for a in range(2):
+            mine = jnp.where(here, found[2 * n_tile * a : 2 * n_tile * (a + 1)], 0.0)
+            mine = sum(mine[8 * k : 8 * k + 8] for k in range(n_tile // 4))
+            mine = mine[0:4] + mine[4:8]
+            of_a.append(mine[0:2] + mine[2:4])
+        terms.append(jnp.concatenate(of_a, axis=0))
     terms = jnp.concatenate(terms, axis=1)
-    w0 = [terms[a : a + 1] for a in range(2)]
-    w1 = [terms[2 + a : 3 + a] for a in range(2)]
+    w0 = [terms[2 * a : 2 * a + 1] for a in range(2)]
+    w1 = [terms[2 * a + 1 : 2 * a + 2] for a in range(2)]
     rhs, diag = pb_ref[...], pd_ref[...]
     z = rhs / diag
     error = [pu_ref[a : a + 1, :] + w0[a] for a in range(2)]
@@ -867,18 +881,19 @@
         total_of(error[0] * error[0] + error[1] * error[1]) + total_of(z1 * z1) + total_of(cz1 * cz1)
     )
     sc_ref[...] = lanes(jnp.concatenate([gamma, alpha], axis=0), HALF)
-    tail = lanes(jnp.concatenate([gamma1, delta1], axis=0), HALF)
-    low = low_lanes(2)
-    numbers = row_numbers(slot)
+    tail = jnp.where(low_lanes(1), gamma1, delta1)
+    wide, numbers = sixteen(owner), row_numbers(owner.shape[1])
+    parts = two_parts(jnp.concatenate([eights(e) for e in error], axis=0))
+    here = [wide == as_16_bit((numbers & 7) + t) for t in range(0, n_tile, 8)]
+    left = masked_rows(parts, here)
+    low = low_lanes(8)
     for h in range(n_grp):
-        cols = slice(h * slot, (h + 1) * slot)
-        first, second = (jnp.broadcast_to(e[:, cols], (16, slot)) for e in error)
-        parts = two_parts(jnp.where((numbers & 1) == 0, first, second))
-        wide = sixteen(owner[:, cols])
-        here = [wide == as_16_bit((numbers >> 1) + t) for t in range(0, n_tile, 8)]
-        moved = both(dot_nt(masked_rows(parts, here), slots[:, cols]))
-        for t in range(n_tile):
-            out_ref[h * n_tile + t] = jnp.where(low, moved[2 * t : 2 * t + 2], tail)
+        moved = both(dot_nt(left[:, h * slot : (h + 1) * slot], hot_rank[:, h * slot : (h + 1) * slot]))
+        for t in range(0, n_tile, 8):
+            tile = jnp.where(low, moved[2 * t : 2 * t + 8], swap_lanes(moved[2 * t + 8 : 2 * t + 16]))
+            tile = jnp.where(last_slot(tile), tail, tile)
+            for k in range(8):
+                out_ref[h * n_tile + t + k] = tile[k : k + 1]
 
 
 def point_results(alpha, alpha1, ratio, pb_ref, pd_ref, ps_ref, pt_ref, px_ref, pr_ref, copies):
@@ -917,10 +932,9 @@
             hi = rows[18:19, :]
         else:
             main, rest, hi, hot = read_routed(in_ref, sources)
-        e = jnp.concatenate(
-            [side_by_side(err_ref[s], err_ref[t]) for s, t in zip(sources[::2], sources[1::2])], axis=1
-        )
-        acc_ref[...] += scatter_j(hi, hot, main, rest, [e[0:1], e[1:2]])
+        pairs = [unfold(err_ref[s], err_ref[t]) for s, t in zip(sources[::2], sources[1::2])]
+        e = [jnp.concatenate([pair[a] for pair in pairs], axis=1) for a in range(2)]
+        acc_ref[...] += scatter_j(hi, hot, main, rest, e)
         return carry
 
     acc_ref[...] = jnp.zeros(acc_ref.shape, F32)
@@ -930,7 +944,7 @@
         lax.fori_loop(0, steps, body, 0)
     last_point_sums_kernel(jp_ref, pidx_ref, pe_ref, pt_ref)
     scalars = jnp.sum(err_ref[...], axis=0)
-    gamma1, delta1 = scalars[0:1, SLOTS : SLOTS + 1], scalars[1:2, SLOTS : SLOTS + 1]
+    gamma1, delta1 = scalars[:, FULL : FULL + 1], scalars[:, HALF - 1 : HALF]
     gamma, alpha = sc_ref[0:1, 0:1], sc_ref[1:2, 0:1]
     ratio = gamma1 / gamma
     alpha1 = gamma1 / (delta1 - ratio * gamma1 / alpha)
@@ -999,15 +1013,15 @@
 
     back, tb, td, ts, *kept = pl.pallas_call(
         owner,
-        out_shape=(shape(devices, 4, HALF), cameras, cameras, cameras) + kept_shapes,
+        out_shape=(shape(devices, 2, HALF), cameras, cameras, cameras) + kept_shapes,
         scratch_shapes=scratch,
         compiler_params=PARAMS,
         name="owner",
     )(routed, sc)
-    back = lax.all_to_all(back, ("grp", "tile"), 0, 0, tiled=True).reshape(devices // 2, 8, HALF)
+    back = lax.all_to_all(back, ("grp", "tile"), 0, 0, tiled=True).reshape(devices // 4, 8, HALF)
     errors, ps, pe, sc, over = pl.pallas_call(
         functools.partial(routed_point_kernel, n_grp, n_tile),
-        out_shape=(shape(devices, 2, HALF), points, shape(2, obs), shape(2, HALF), shape(1, HALF)),
+        out_shape=(shape(devices, 1, HALF), points, shape(2, obs), shape(2, HALF), shape(1, HALF)),
         compiler_params=PARAMS,
         name="points",
     )(back, jp, pidx_here, place, pb, pd, pu, tb, td, ts)

time: 41 us -> 40.9 us (level)
  no operation moved by 1% of the time
where the time goes in v9:
time: 40.9 us; the launch traced here: 40.7 us
  blocking collectives  34.5 us (84%)
  Pallas kernels  5.42 us (13%)
  between operations  0.76 us (2%)
    all_to_all x1, blocking collectives, shards(): lax.all_to_all(routed, ('grp', 'tile'), 0, 0, tiled=True)  15.9 us
    all_to_all x1, blocking collectives, shards(): lax.all_to_all(back, ('grp', 'tile'), 0, 0, tiled=True)  9.77 us
    all_to_all x1, blocking collectives, fits(): errors = lax.all_to_all(operands[5], ('grp', 'tile'), 0, 0, tiled=True)  8.84 us
    pallas_call x1, Pallas kernels, shards(): pl.pallas_call(functools.partial(route_kernel, n_grp, n_tile), in_specs=[...  1.93 us
    pallas_call x1, Pallas kernels, fits(): pl.pallas_call(routed_final_kernel, out_shape=outputs, out_specs=[hbm] *...  1.22 us
    pallas_call x1, Pallas kernels, shards(): pl.pallas_call(owner, out_shape=(shape(devices, 2, HALF), cameras, camera...  1.2 us
    pallas_call x1, Pallas kernels, shards(): pl.pallas_call(functools.partial(routed_point_kernel, n_grp, n_tile), out...  1.07 us

profile of v9, /device:TPU:0, one launch (start us, length us, event | category | flops | bytes accessed | tf_op | source)
XLA Modules:
  0.0 40.7 jit_solution(1365649654755329752)
XLA Ops:
  0.6 1.9 %route.1 = (f32[96,4,128]{2,1,0:T(4,128)S(1)}, f32[48,256]{1,0:T(8,128)S(1)}, f32[48,256]{1,0:T(8,128)S(1)}, f32[2,1024]{1,0:T(2,128)S(1)}, f32[6,1024]{1,0:T(8,...) custom-call(f32[6,1024]{1,0:T(8,128)} %jp_hbm.1, f32[18,1024]{1,0:T(8,128)} %jc_hbm.1, ...), custom_call_target="tpu_custom_call" | custom-call | tf_op jit(solution)/shard_map/route/pallas_call | solution.py:985
  2.6 15.9 %all_to_all.28 = f32[96,4,128]{2,1,0:T(4,128)S(1)} all-to-all(f32[96,4,128]{2,1,0:T(4,128)S(1)} %get-tuple-element.117), channel_id=1, replica_groups=mesh['grp'=4,'tile'=8] {'grp','tile'}, dimensions={0} | all-to-all | bytes 393216 | tf_op jit(solution)/shard_map/all_to_all | solution.py:998
  18.4 1.2 %owner.1 = (f32[32,2,128]{2,1,0:T(2,128)S(1)}, f32[32,128]{1,0:T(8,128)S(1)}, f32[32,128]{1,0:T(8,128)S(1)}, f32[32,128]{1,0:T(8,128)S(1)}, bf16[128,2048]{1,0:T(8,128)(2,1)S(1)}, /*index=5*/f32[24,2048]{1,0:T(8,128)S(1)}) custom-call(f32[48,8,128]{2,1,0:T(8,128)S(1)} %bitcast.10, f32[3,128]{1,0:T(4,128)S(1)} %get-tuple-element.118.sc_ref), custom_call_target="tpu_custom_call" | custom-call | tf_op jit(solution)/shard_map/owner/pallas_call | solution.py:1014
  19.6 9.8 %all_to_all.29 = f32[32,2,128]{2,1,0:T(2,128)S(1)} all-to-all(f32[32,2,128]{2,1,0:T(2,128)S(1)} %get-tuple-element.119), channel_id=1, replica_groups=mesh['grp'=4,'tile'=8] {'grp','tile'}, dimensions={0} | all-to-all | bytes 65536 | tf_op jit(solution)/shard_map/all_to_all | solution.py:1021
  29.4 1.1 %points.3 = (f32[32,1,128]{2,1,0:T(1,128)S(1)}, f32[48,256]{1,0:T(8,128)S(1)}, f32[2,1024]{1,0:T(2,128)S(1)}, f32[2,128]{1,0:T(2,128)S(1)}, f32[1,128]{1,0:T(1,128)S(1)}) custom-call(f32[8,8,128]{2,1,0:T(8,128)S(1)} %bitcast.8, f32[6,1024]{1,0:T(8,128)S(1)} %get-tuple-element.139.jp_ref, s32[1,1024]{1,0:T(1,128)S(1)} %get-tuple-element.140.pidx_ref, ...), custom_call_target="tpu_custom_call" | custom-call | tf_op jit(solution)/shard_map/points/pallas_call | solution.py:1022
  30.6 10.1 %conditional.1 = ((f32[3,4096]{1,0:T(4,128)}, f32[9,384]{1,0:T(8,128)}, f32[3,4096]{1,0:T(4,128)}, f32[9,384]{1,0:T(8,128)})) conditional(s32[]{:T(128)} %bitcast.6, (f32[32,1,128]{2,1,0:T(1,128)S(1)}, f32[48,8,128]{2,1,0:T(8,128)S(1)}, f32[6,1024]{1,0:T(8,128)S(1)}, s32[1,1024]{1,0:T(1,128)S(1)}, f32[2,1024]{1,0:T(2,128)S(1)}, ...), branch_computations={%region_0.0_spmd, %region_1.0_spmd} | conditional | flops 2000000000 | bytes 3728048 | solution.py:1055
  30.6 8.8 %all_to_all.26.err_ref = f32[32,1,128]{2,1,0:T(1,128)S(1)} all-to-all(f32[32,1,128]{2,1,0:T(1,128)S(1)} %get-tuple-element.38), channel_id=1, replica_groups=mesh['grp'=4,'tile'=8] {'grp','tile'}, dimensions={0} | all-to-all | bytes 32768 | tf_op jit(solution)/shard_map/cond/branch_0_fun/all_to_all | solution.py:1031
  39.4 1.2 %finish.2 = (f32[3,4096]{1,0:T(4,128)}, f32[9,384]{1,0:T(8,128)}, f32[3,4096]{1,0:T(4,128)}, f32[9,384]{1,0:T(8,128)}) custom-call(f32[32,1,128]{2,1,0:T(1,128)S(1)} %all_to_all.26.err_ref, f32[48,8,128]{2,1,0:T(8,128)S(1)} %get-tuple-element.39.in_ref, f32[6,1024]{1,0:T(8,128)S(1)} %get-tuple-element.40.jp_ref, s32[1,1024]{1,0:T(1,128)S(1)} %get-tuple-element.41.pidx_ref, ...), custom_call_target="tpu_custom_call" | custom-call | tf_op jit(solution)/shard_map/cond/branch_0_fun/finish/pallas_call | solution.py:1032

commit v10 on v9

--- a/solution.py
+++ b/solution.py
@@ -591,16 +591,12 @@
     out_ref, pb_ref, pd_ref, pu_ref, jp_ref, pidx_ref, place_ref, sc_ref,
     jc_ref, res_ref, cidx_ref, sems,
 ):
-    start_copies(
-        (
-            (pidx_hbm, pidx_ref),
-            (jp_hbm, jp_ref),
-            (res_hbm, res_ref),
-            (jc_hbm, jc_ref),
-            (cidx_hbm, cidx_ref),
-        ),
-        sems,
-    )
+    width = cidx_ref.shape[1] // 4
+    pairs = [(pidx_hbm, pidx_ref), (jp_hbm, jp_ref), (res_hbm, res_ref), (cidx_hbm, cidx_ref)]
+    for k in range(4):
+        part = pl.ds(k * width, width)
+        pairs.append((jc_hbm.at[:, part], jc_ref.at[:, part]))
+    start_copies(pairs, sems)
     slot = cidx_ref.shape[1] // n_grp
     cams = cidx_ref[...]
     owner = ((cams >> 7) * 171) >> 9
@@ -645,13 +641,11 @@
             out_ref[3 * (h * n_tile + t) + others] = tile
 
     table, mask, hot, jp = point_sums(pidx_ref, jp_ref, res_ref)
-    for h in range(n_grp // 2):
+    for h in range(n_grp):
         route_main(h)
     rhs, diag = table[: 3 * PH], table[3 * PH :] + DAMPING
     z = rhs / diag
     at = gather_points(mask, hot, z)
-    for h in range(n_grp // 2, n_grp):
-        route_main(h)
     pb_ref[...] = rhs
     pd_ref[...] = diag
     u = [sum(jp[a][i : i + 1] * at[i] for i in range(3)) for a in range(2)]
@@ -990,7 +984,7 @@
             pltpu.VMEM((18, obs), F32),
             pltpu.VMEM((2, obs), F32),
             pltpu.VMEM((1, obs), jnp.int32),
-            pltpu.SemaphoreType.DMA((5,)),
+            pltpu.SemaphoreType.DMA((8,)),
         ],
         compiler_params=PARAMS,
         name="route",

time: 40.9 us -> 40.8 us (level)
  no operation moved by 1% of the time
where the time goes in v10:
time: 40.8 us; the launch traced here: 40.5 us
  blocking collectives  34.5 us (85%)
  Pallas kernels  5.32 us (13%)
  between operations  0.76 us (2%)
    all_to_all x1, blocking collectives, shards(): lax.all_to_all(routed, ('grp', 'tile'), 0, 0, tiled=True)  15.8 us
    all_to_all x1, blocking collectives, shards(): lax.all_to_all(back, ('grp', 'tile'), 0, 0, tiled=True)  9.76 us
    all_to_all x1, blocking collectives, fits(): errors = lax.all_to_all(operands[5], ('grp', 'tile'), 0, 0, tiled=True)  8.84 us
    pallas_call x1, Pallas kernels, shards(): pl.pallas_call(functools.partial(route_kernel, n_grp, n_tile), in_specs=[...  1.83 us
    pallas_call x1, Pallas kernels, fits(): pl.pallas_call(routed_final_kernel, out_shape=outputs, out_specs=[hbm] *...  1.22 us
    pallas_call x1, Pallas kernels, shards(): pl.pallas_call(owner, out_shape=(shape(devices, 2, HALF), cameras, camera...  1.2 us
    pallas_call x1, Pallas kernels, shards(): pl.pallas_call(functools.partial(routed_point_kernel, n_grp, n_tile), out...  1.07 us

profile of v10, /device:TPU:0, one launch (start us, length us, event | category | flops | bytes accessed | tf_op | source)
XLA Modules:
  0.0 40.5 jit_solution(9195448570607606384)
XLA Ops:
  0.6 1.8 %route.1 = (f32[96,4,128]{2,1,0:T(4,128)S(1)}, f32[48,256]{1,0:T(8,128)S(1)}, f32[48,256]{1,0:T(8,128)S(1)}, f32[2,1024]{1,0:T(2,128)S(1)}, f32[6,1024]{1,0:T(8,...) custom-call(f32[6,1024]{1,0:T(8,128)} %jp_hbm.1, f32[18,1024]{1,0:T(8,128)} %jc_hbm.1, ...), custom_call_target="tpu_custom_call" | custom-call | tf_op jit(solution)/shard_map/route/pallas_call | solution.py:979
  2.5 15.8 %all_to_all.28 = f32[96,4,128]{2,1,0:T(4,128)S(1)} all-to-all(f32[96,4,128]{2,1,0:T(4,128)S(1)} %get-tuple-element.117), channel_id=1, replica_groups=mesh['grp'=4,'tile'=8] {'grp','tile'}, dimensions={0} | all-to-all | bytes 393216 | tf_op jit(solution)/shard_map/all_to_all | solution.py:992
  18.3 1.2 %owner.1 = (f32[32,2,128]{2,1,0:T(2,128)S(1)}, f32[32,128]{1,0:T(8,128)S(1)}, f32[32,128]{1,0:T(8,128)S(1)}, f32[32,128]{1,0:T(8,128)S(1)}, bf16[128,2048]{1,0:T(8,128)(2,1)S(1)}, /*index=5*/f32[24,2048]{1,0:T(8,128)S(1)}) custom-call(f32[48,8,128]{2,1,0:T(8,128)S(1)} %bitcast.10, f32[3,128]{1,0:T(4,128)S(1)} %get-tuple-element.118.sc_ref), custom_call_target="tpu_custom_call" | custom-call | tf_op jit(solution)/shard_map/owner/pallas_call | solution.py:1008
  19.5 9.8 %all_to_all.29 = f32[32,2,128]{2,1,0:T(2,128)S(1)} all-to-all(f32[32,2,128]{2,1,0:T(2,128)S(1)} %get-tuple-element.119), channel_id=1, replica_groups=mesh['grp'=4,'tile'=8] {'grp','tile'}, dimensions={0} | all-to-all | bytes 65536 | tf_op jit(solution)/shard_map/all_to_all | solution.py:1015
  29.3 1.1 %points.3 = (f32[32,1,128]{2,1,0:T(1,128)S(1)}, f32[48,256]{1,0:T(8,128)S(1)}, f32[2,1024]{1,0:T(2,128)S(1)}, f32[2,128]{1,0:T(2,128)S(1)}, f32[1,128]{1,0:T(1,128)S(1)}) custom-call(f32[8,8,128]{2,1,0:T(8,128)S(1)} %bitcast.8, f32[6,1024]{1,0:T(8,128)S(1)} %get-tuple-element.139.jp_ref, s32[1,1024]{1,0:T(1,128)S(1)} %get-tuple-element.140.pidx_ref, ...), custom_call_target="tpu_custom_call" | custom-call | tf_op jit(solution)/shard_map/points/pallas_call | solution.py:1016
  30.5 10.1 %conditional.1 = ((f32[3,4096]{1,0:T(4,128)}, f32[9,384]{1,0:T(8,128)}, f32[3,4096]{1,0:T(4,128)}, f32[9,384]{1,0:T(8,128)})) conditional(s32[]{:T(128)} %bitcast.6, (f32[32,1,128]{2,1,0:T(1,128)S(1)}, f32[48,8,128]{2,1,0:T(8,128)S(1)}, f32[6,1024]{1,0:T(8,128)S(1)}, s32[1,1024]{1,0:T(1,128)S(1)}, f32[2,1024]{1,0:T(2,128)S(1)}, ...), branch_computations={%region_0.0_spmd, %region_1.0_spmd} | conditional | flops 2000000000 | bytes 3728048 | solution.py:1049
  30.5 8.8 %all_to_all.26.err_ref = f32[32,1,128]{2,1,0:T(1,128)S(1)} all-to-all(f32[32,1,128]{2,1,0:T(1,128)S(1)} %get-tuple-element.38), channel_id=1, replica_groups=mesh['grp'=4,'tile'=8] {'grp','tile'}, dimensions={0} | all-to-all | bytes 32768 | tf_op jit(solution)/shard_map/cond/branch_0_fun/all_to_all | solution.py:1025
  39.3 1.2 %finish.2 = (f32[3,4096]{1,0:T(4,128)}, f32[9,384]{1,0:T(8,128)}, f32[3,4096]{1,0:T(4,128)}, f32[9,384]{1,0:T(8,128)}) custom-call(f32[32,1,128]{2,1,0:T(1,128)S(1)} %all_to_all.26.err_ref, f32[48,8,128]{2,1,0:T(8,128)S(1)} %get-tuple-element.39.in_ref, f32[6,1024]{1,0:T(8,128)S(1)} %get-tuple-element.40.jp_ref, s32[1,1024]{1,0:T(1,128)S(1)} %get-tuple-element.41.pidx_ref, ...), custom_call_target="tpu_custom_call" | custom-call | tf_op jit(solution)/shard_map/cond/branch_0_fun/finish/pallas_call | solution.py:1026

commit v11 on v10

--- a/solution.py
+++ b/solution.py
@@ -116,9 +116,10 @@
 
 def gather_points(mask, hot, table):
     found = both(dot_nn(stacked(table), hot))
+    rows = mask.shape[0]
     return [
-        jnp.sum(jnp.where(mask, found[i * PH : (i + 1) * PH], 0.0), axis=0, keepdims=True)
-        for i in range(found.shape[0] // PH)
+        jnp.sum(jnp.where(mask, found[i * rows : (i + 1) * rows], 0.0), axis=0, keepdims=True)
+        for i in range(found.shape[0] // rows)
     ]
 
 
@@ -822,14 +823,25 @@
     loop(send, 0)
 
 
+def halved(ref):
+    return jnp.concatenate(
+        [
+            ref[i * PH : (i + 1) * PH, half * HALF : (half + 1) * HALF]
+            for i in range(3)
+            for half in range(2)
+        ],
+        axis=0,
+    )
+
+
 def routed_point_kernel(
     n_grp, n_tile, back_ref, jp_ref, pidx_ref, place_ref, pb_ref, pd_ref, pu_ref, cb_ref, cd_ref, cs_ref,
     out_ref, ps_ref, pe_ref, sc_ref, over_ref,
 ):
     slot = place_ref.shape[1] // n_grp
     index = pidx_ref[...]
-    mask = is_row(index >> LO_BITS, PH)
-    hot = one_hot_rows(index & (LO - 1), LO)
+    mask = is_row(((index >> 7) & 1) * PH + (index >> LO_BITS), 2 * PH)
+    hot = one_hot_rows(index & (HALF - 1), HALF)
     jp = [jp_ref[k : k + 1, :] for k in range(6)]
     scalars = jnp.sum(back_ref[...], axis=0)
     scalars = scalars[0:4] + scalars[4:8]
@@ -857,7 +869,7 @@
     terms = jnp.concatenate(terms, axis=1)
     w0 = [terms[2 * a : 2 * a + 1] for a in range(2)]
     w1 = [terms[2 * a + 1 : 2 * a + 2] for a in range(2)]
-    rhs, diag = pb_ref[...], pd_ref[...]
+    rhs, diag = halved(pb_ref), halved(pd_ref)
     z = rhs / diag
     error = [pu_ref[a : a + 1, :] + w0[a] for a in range(2)]
     s = z + scatter_points(mask, hot, jp_ref[0:3, :] * error[0] + jp_ref[3:6, :] * error[1])
@@ -865,7 +877,10 @@
     z1 = r1 / diag
     at = gather_points(mask, hot, z1)
     error = [sum(jp[3 * a + i] * at[i] for i in range(3)) + (w0[a] - alpha * w1[a]) for a in range(2)]
-    ps_ref[...] = s
+    for i in range(3):
+        for half in range(2):
+            row = (2 * i + half) * PH
+            ps_ref[i * PH : (i + 1) * PH, half * HALF : (half + 1) * HALF] = s[row : row + PH]
     pe_ref[0:1, :] = error[0]
     pe_ref[1:2, :] = error[1]
     cr1 = cb_ref[...] - alpha * cs_ref[...]

time: 40.8 us -> 40.6 us (level)
  no operation moved by 1% of the time
where the time goes in v11:
time: 40.6 us; the launch traced here: 40.4 us
  blocking collectives  34.5 us (85%)
  Pallas kernels  5.14 us (13%)
  between operations  0.76 us (2%)
    all_to_all x1, blocking collectives, shards(): lax.all_to_all(routed, ('grp', 'tile'), 0, 0, tiled=True)  15.8 us
    all_to_all x1, blocking collectives, shards(): lax.all_to_all(back, ('grp', 'tile'), 0, 0, tiled=True)  9.76 us
    all_to_all x1, blocking collectives, fits(): errors = lax.all_to_all(operands[5], ('grp', 'tile'), 0, 0, tiled=True)  8.84 us
    pallas_call x1, Pallas kernels, shards(): pl.pallas_call(functools.partial(route_kernel, n_grp, n_tile), in_specs=[...  1.83 us
    pallas_call x1, Pallas kernels, fits(): pl.pallas_call(routed_final_kernel, out_shape=outputs, out_specs=[hbm] *...  1.22 us
    pallas_call x1, Pallas kernels, shards(): pl.pallas_call(owner, out_shape=(shape(devices, 2, HALF), cameras, camera...  1.2 us
    pallas_call x1, Pallas kernels, shards(): pl.pallas_call(functools.partial(routed_point_kernel, n_grp, n_tile), out...  0.89 us

profile of v11, /device:TPU:0, one launch (start us, length us, event | category | flops | bytes accessed | tf_op | source)
XLA Modules:
  0.0 40.4 jit_solution(1622196928620370445)
XLA Ops:
  0.6 1.8 %route.1 = (f32[96,4,128]{2,1,0:T(4,128)S(1)}, f32[48,256]{1,0:T(8,128)S(1)}, f32[48,256]{1,0:T(8,128)S(1)}, f32[2,1024]{1,0:T(2,128)S(1)}, f32[6,1024]{1,0:T(8,...) custom-call(f32[6,1024]{1,0:T(8,128)} %jp_hbm.1, f32[18,1024]{1,0:T(8,128)} %jc_hbm.1, ...), custom_call_target="tpu_custom_call" | custom-call | tf_op jit(solution)/shard_map/route/pallas_call | solution.py:994
  2.5 15.8 %all_to_all.28 = f32[96,4,128]{2,1,0:T(4,128)S(1)} all-to-all(f32[96,4,128]{2,1,0:T(4,128)S(1)} %get-tuple-element.117), channel_id=1, replica_groups=mesh['grp'=4,'tile'=8] {'grp','tile'}, dimensions={0} | all-to-all | bytes 393216 | tf_op jit(solution)/shard_map/all_to_all | solution.py:1007
  18.3 1.2 %owner.1 = (f32[32,2,128]{2,1,0:T(2,128)S(1)}, f32[32,128]{1,0:T(8,128)S(1)}, f32[32,128]{1,0:T(8,128)S(1)}, f32[32,128]{1,0:T(8,128)S(1)}, bf16[128,2048]{1,0:T(8,128)(2,1)S(1)}, /*index=5*/f32[24,2048]{1,0:T(8,128)S(1)}) custom-call(f32[48,8,128]{2,1,0:T(8,128)S(1)} %bitcast.10, f32[3,128]{1,0:T(4,128)S(1)} %get-tuple-element.118.sc_ref), custom_call_target="tpu_custom_call" | custom-call | tf_op jit(solution)/shard_map/owner/pallas_call | solution.py:1023
  19.5 9.8 %all_to_all.29 = f32[32,2,128]{2,1,0:T(2,128)S(1)} all-to-all(f32[32,2,128]{2,1,0:T(2,128)S(1)} %get-tuple-element.119), channel_id=1, replica_groups=mesh['grp'=4,'tile'=8] {'grp','tile'}, dimensions={0} | all-to-all | bytes 65536 | tf_op jit(solution)/shard_map/all_to_all | solution.py:1030
  29.3 0.9 %points.3 = (f32[32,1,128]{2,1,0:T(1,128)S(1)}, f32[48,256]{1,0:T(8,128)S(1)}, f32[2,1024]{1,0:T(2,128)S(1)}, f32[2,128]{1,0:T(2,128)S(1)}, f32[1,128]{1,0:T(1,128)S(1)}) custom-call(f32[8,8,128]{2,1,0:T(8,128)S(1)} %bitcast.8, f32[6,1024]{1,0:T(8,128)S(1)} %get-tuple-element.139.jp_ref, s32[1,1024]{1,0:T(1,128)S(1)} %get-tuple-element.140.pidx_ref, ...), custom_call_target="tpu_custom_call" | custom-call | tf_op jit(solution)/shard_map/points/pallas_call | solution.py:1031
  30.3 10.1 %conditional.1 = ((f32[3,4096]{1,0:T(4,128)}, f32[9,384]{1,0:T(8,128)}, f32[3,4096]{1,0:T(4,128)}, f32[9,384]{1,0:T(8,128)})) conditional(s32[]{:T(128)} %bitcast.6, (f32[32,1,128]{2,1,0:T(1,128)S(1)}, f32[48,8,128]{2,1,0:T(8,128)S(1)}, f32[6,1024]{1,0:T(8,128)S(1)}, s32[1,1024]{1,0:T(1,128)S(1)}, f32[2,1024]{1,0:T(2,128)S(1)}, ...), branch_computations={%region_0.0_spmd, %region_1.0_spmd} | conditional | flops 2000000000 | bytes 3728048 | solution.py:1064
  30.3 8.8 %all_to_all.26.err_ref = f32[32,1,128]{2,1,0:T(1,128)S(1)} all-to-all(f32[32,1,128]{2,1,0:T(1,128)S(1)} %get-tuple-element.38), channel_id=1, replica_groups=mesh['grp'=4,'tile'=8] {'grp','tile'}, dimensions={0} | all-to-all | bytes 32768 | tf_op jit(solution)/shard_map/cond/branch_0_fun/all_to_all | solution.py:1040
  39.1 1.2 %finish.2 = (f32[3,4096]{1,0:T(4,128)}, f32[9,384]{1,0:T(8,128)}, f32[3,4096]{1,0:T(4,128)}, f32[9,384]{1,0:T(8,128)}) custom-call(f32[32,1,128]{2,1,0:T(1,128)S(1)} %all_to_all.26.err_ref, f32[48,8,128]{2,1,0:T(8,128)S(1)} %get-tuple-element.39.in_ref, f32[6,1024]{1,0:T(8,128)S(1)} %get-tuple-element.40.jp_ref, s32[1,1024]{1,0:T(1,128)S(1)} %get-tuple-element.41.pidx_ref, ...), custom_call_target="tpu_custom_call" | custom-call | tf_op jit(solution)/shard_map/cond/branch_0_fun/finish/pallas_call | solution.py:1041

commit v12 on v11

--- a/solution.py
+++ b/solution.py
@@ -951,7 +951,14 @@
         body(0, 0)
     else:
         lax.fori_loop(0, steps, body, 0)
-    last_point_sums_kernel(jp_ref, pidx_ref, pe_ref, pt_ref)
+    index = pidx_ref[...]
+    mask = is_row(((index >> 7) & 1) * PH + (index >> LO_BITS), 2 * PH)
+    terms = jp_ref[0:3, :] * pe_ref[0:1, :] + jp_ref[3:6, :] * pe_ref[1:2, :]
+    sums = scatter_points(mask, one_hot_rows(index & (HALF - 1), HALF), terms)
+    for i in range(3):
+        for half in range(2):
+            row = (2 * i + half) * PH
+            pt_ref[i * PH : (i + 1) * PH, half * HALF : (half + 1) * HALF] = sums[row : row + PH]
     scalars = jnp.sum(err_ref[...], axis=0)
     gamma1, delta1 = scalars[:, FULL : FULL + 1], scalars[:, HALF - 1 : HALF]
     gamma, alpha = sc_ref[0:1, 0:1], sc_ref[1:2, 0:1]

time: 40.6 us -> 40.6 us (level)
  no operation moved by 1% of the time
where the time goes in v12:
time: 40.6 us; the launch traced here: 40.3 us
  blocking collectives  34.5 us (85%)
  Pallas kernels  5.11 us (13%)
  between operations  0.76 us (2%)
    all_to_all x1, blocking collectives, shards(): lax.all_to_all(routed, ('grp', 'tile'), 0, 0, tiled=True)  15.8 us
    all_to_all x1, blocking collectives, shards(): lax.all_to_all(back, ('grp', 'tile'), 0, 0, tiled=True)  9.76 us
    all_to_all x1, blocking collectives, fits(): errors = lax.all_to_all(operands[5], ('grp', 'tile'), 0, 0, tiled=True)  8.84 us
    pallas_call x1, Pallas kernels, shards(): pl.pallas_call(functools.partial(route_kernel, n_grp, n_tile), in_specs=[...  1.83 us
    pallas_call x1, Pallas kernels, shards(): pl.pallas_call(owner, out_shape=(shape(devices, 2, HALF), cameras, camera...  1.2 us
    pallas_call x1, Pallas kernels, fits(): pl.pallas_call(routed_final_kernel, out_shape=outputs, out_specs=[hbm] *...  1.19 us
    pallas_call x1, Pallas kernels, shards(): pl.pallas_call(functools.partial(routed_point_kernel, n_grp, n_tile), out...  0.89 us

profile of v12, /device:TPU:0, one launch (start us, length us, event | category | flops | bytes accessed | tf_op | source)
XLA Modules:
  0.0 40.3 jit_solution(17160209869756888094)
XLA Ops:
  0.6 1.8 %route.1 = (f32[96,4,128]{2,1,0:T(4,128)S(1)}, f32[48,256]{1,0:T(8,128)S(1)}, f32[48,256]{1,0:T(8,128)S(1)}, f32[2,1024]{1,0:T(2,128)S(1)}, f32[6,1024]{1,0:T(8,...) custom-call(f32[6,1024]{1,0:T(8,128)} %jp_hbm.1, f32[18,1024]{1,0:T(8,128)} %jc_hbm.1, ...), custom_call_target="tpu_custom_call" | custom-call | tf_op jit(solution)/shard_map/route/pallas_call | solution.py:1001
  2.5 15.8 %all_to_all.28 = f32[96,4,128]{2,1,0:T(4,128)S(1)} all-to-all(f32[96,4,128]{2,1,0:T(4,128)S(1)} %get-tuple-element.117), channel_id=1, replica_groups=mesh['grp'=4,'tile'=8] {'grp','tile'}, dimensions={0} | all-to-all | bytes 393216 | tf_op jit(solution)/shard_map/all_to_all | solution.py:1014
  18.3 1.2 %owner.1 = (f32[32,2,128]{2,1,0:T(2,128)S(1)}, f32[32,128]{1,0:T(8,128)S(1)}, f32[32,128]{1,0:T(8,128)S(1)}, f32[32,128]{1,0:T(8,128)S(1)}, bf16[128,2048]{1,0:T(8,128)(2,1)S(1)}, /*index=5*/f32[24,2048]{1,0:T(8,128)S(1)}) custom-call(f32[48,8,128]{2,1,0:T(8,128)S(1)} %bitcast.10, f32[3,128]{1,0:T(4,128)S(1)} %get-tuple-element.118.sc_ref), custom_call_target="tpu_custom_call" | custom-call | tf_op jit(solution)/shard_map/owner/pallas_call | solution.py:1030
  19.5 9.8 %all_to_all.29 = f32[32,2,128]{2,1,0:T(2,128)S(1)} all-to-all(f32[32,2,128]{2,1,0:T(2,128)S(1)} %get-tuple-element.119), channel_id=1, replica_groups=mesh['grp'=4,'tile'=8] {'grp','tile'}, dimensions={0} | all-to-all | bytes 65536 | tf_op jit(solution)/shard_map/all_to_all | solution.py:1037
  29.3 0.9 %points.3 = (f32[32,1,128]{2,1,0:T(1,128)S(1)}, f32[48,256]{1,0:T(8,128)S(1)}, f32[2,1024]{1,0:T(2,128)S(1)}, f32[2,128]{1,0:T(2,128)S(1)}, f32[1,128]{1,0:T(1,128)S(1)}) custom-call(f32[8,8,128]{2,1,0:T(8,128)S(1)} %bitcast.8, f32[6,1024]{1,0:T(8,128)S(1)} %get-tuple-element.139.jp_ref, s32[1,1024]{1,0:T(1,128)S(1)} %get-tuple-element.140.pidx_ref, ...), custom_call_target="tpu_custom_call" | custom-call | tf_op jit(solution)/shard_map/points/pallas_call | solution.py:1038
  30.3 10.0 %conditional.1 = ((f32[3,4096]{1,0:T(4,128)}, f32[9,384]{1,0:T(8,128)}, f32[3,4096]{1,0:T(4,128)}, f32[9,384]{1,0:T(8,128)})) conditional(s32[]{:T(128)} %bitcast.6, (f32[32,1,128]{2,1,0:T(1,128)S(1)}, f32[48,8,128]{2,1,0:T(8,128)S(1)}, f32[6,1024]{1,0:T(8,128)S(1)}, s32[1,1024]{1,0:T(1,128)S(1)}, f32[2,1024]{1,0:T(2,128)S(1)}, ...), branch_computations={%region_0.0_spmd, %region_1.0_spmd} | conditional | flops 2000000000 | bytes 3728048 | solution.py:1071
  30.3 8.8 %all_to_all.26.err_ref = f32[32,1,128]{2,1,0:T(1,128)S(1)} all-to-all(f32[32,1,128]{2,1,0:T(1,128)S(1)} %get-tuple-element.38), channel_id=1, replica_groups=mesh['grp'=4,'tile'=8] {'grp','tile'}, dimensions={0} | all-to-all | bytes 32768 | tf_op jit(solution)/shard_map/cond/branch_0_fun/all_to_all | solution.py:1047
  39.1 1.2 %finish.2 = (f32[3,4096]{1,0:T(4,128)}, f32[9,384]{1,0:T(8,128)}, f32[3,4096]{1,0:T(4,128)}, f32[9,384]{1,0:T(8,128)}) custom-call(f32[32,1,128]{2,1,0:T(1,128)S(1)} %all_to_all.26.err_ref, f32[48,8,128]{2,1,0:T(8,128)S(1)} %get-tuple-element.39.in_ref, f32[6,1024]{1,0:T(8,128)S(1)} %get-tuple-element.40.jp_ref, s32[1,1024]{1,0:T(1,128)S(1)} %get-tuple-element.41.pidx_ref, ...), custom_call_target="tpu_custom_call" | custom-call | tf_op jit(solution)/shard_map/cond/branch_0_fun/finish/pallas_call | solution.py:1048
